TPU v7x, 512 devices: a whole 4x4x16 slice. The times are simulated.
512 devices in a mesh: bx: 32 (over y_hi, z), by: 16 (over y_lo, x, core).
Axes of the slice: x: 4, y: 4 (y_hi: 2, y_lo: 2; y = y_hi * 2 + y_lo), z: 16, core: 2. Of those that a mesh axis runs over, the one named last changes fastest.
Arguments:
- polarization: float32 [3, 8, 1024, 2048], P(None, None, 'bx', 'by'), may hold values from -1.6 to 1.6
- alpha_field: float32 [8, 1024, 2048], P(None, 'bx', 'by'), may hold values from -1 to 1
- landau: float32 [3, 8], replicated, may hold values from 0.05 to 0.25
- stiffness: float32 [8], replicated, may hold values from 0.5 to 1.5
- permittivity: float32 [8], replicated, may hold values from 0.5 to 2
- interfaces: float32 [9], replicated, may hold values from 0.0002 to 0.0008
Outputs:
- polar_next: float32 [3, 8, 1024, 2048], P(None, None, 'bx', 'by')
- depol_field: float32 [3, 8, 1024, 2048], P(None, None, 'bx', 'by')
All inputs are finite; a program needn't handle non-finite values.
Results may differ from a plain program's by a relative error of at most 0.0003.
Values sent between devices are 32-bit elements; how exact they have to be, the bound alone decides.
No kernel may reach another device: no remote copies, remote signals or barrier semaphores. Data moves between devices by JAX's collectives and lax.ppermute only.
A program may use at most 64 MiB of HBM per device.

v0:
```python
import jax
import jax.numpy as jnp
from jax import lax
from jax.sharding import PartitionSpec as P

STEPS = 2


step_size = 0.05
highest = lax.Precision.HIGHEST


def extended(block, sides, width):
    for axis, dim in sides:
        count = lax.axis_size(axis)
        forward = [(i, i + 1) for i in range(count - 1)]
        forward.append((count - 1, 0))
        backward = [(target, source) for source, target in forward]
        low = lax.ppermute(
            lax.slice_in_dim(block, block.shape[dim] - width, None, axis=dim), axis, forward
        )
        high = lax.ppermute(lax.slice_in_dim(block, 0, width, axis=dim), axis, backward)
        block = jnp.concatenate([low, block, high], axis=dim)
    return block


def phase_table(left_index, right_index, length, sign):
    turns = left_index * right_index % length
    angle = 2.0 * jnp.pi / length * turns.astype(jnp.float32)
    return (jnp.cos(angle), sign * jnp.sin(angle))


def mix(form, real_part, imag_part, cos_table, sin_table):
    real_out = jnp.einsum(form, real_part, cos_table, precision=highest) - jnp.einsum(
        form, imag_part, sin_table, precision=highest
    )
    imag_out = jnp.einsum(form, real_part, sin_table, precision=highest) + jnp.einsum(
        form, imag_part, cos_table, precision=highest
    )
    return (real_out, imag_out)


def rotate(real_part, imag_part, cos_table, sin_table):
    return (
        real_part * cos_table - imag_part * sin_table,
        real_part * sin_table + imag_part * cos_table,
    )


def shift_up(source, axis_no):
    upper_part = lax.slice_in_dim(source, 1, source.shape[axis_no], axis=axis_no)
    return jnp.concatenate(
        [upper_part, jnp.zeros_like(lax.slice_in_dim(source, 0, 1, axis=axis_no))], axis=axis_no
    )


def shift_down(source, axis_no):
    lower_part = lax.slice_in_dim(source, 0, source.shape[axis_no] - 1, axis=axis_no)
    return jnp.concatenate(
        [jnp.zeros_like(lax.slice_in_dim(source, 0, 1, axis=axis_no)), lower_part], axis=axis_no
    )


def forward(charge):
    layers, rows, cols = charge.shape
    row_parts = lax.axis_size("bx")
    col_parts = lax.axis_size("by")
    row_me = lax.axis_index("bx")
    col_me = lax.axis_index("by")
    row_sub = rows // row_parts
    col_sub = cols // col_parts
    grid_x = rows * row_parts
    grid_y = cols * col_parts
    block = layers * rows
    lined = lax.all_to_all(
        charge.reshape(1, layers, row_parts, row_sub, cols),
        "bx",
        split_axis=2,
        concat_axis=0,
        tiled=True,
    )
    lined = lined.reshape(row_parts, layers * row_sub * cols)
    part_rows = jnp.arange(row_parts, dtype=jnp.int32)
    cos_table, sin_table = phase_table(part_rows[:, None], part_rows[None, :], row_parts, -1.0)
    real_part = jnp.einsum("ib,ik->kb", lined, cos_table, precision=highest)
    imag_part = jnp.einsum("ib,ik->kb", lined, sin_table, precision=highest)
    local_rows = row_me * row_sub + jnp.arange(row_sub, dtype=jnp.int32)
    cos_table, sin_table = phase_table(
        part_rows[:, None, None, None], local_rows[None, None, :, None], grid_x, -1.0
    )
    real_part, imag_part = rotate(
        real_part.reshape(row_parts, layers, row_sub, cols),
        imag_part.reshape(row_parts, layers, row_sub, cols),
        cos_table,
        sin_table,
    )
    stacked = jnp.stack([real_part, imag_part]).reshape(2, row_parts, layers, 1, row_sub, cols)
    stacked = lax.all_to_all(stacked, "bx", split_axis=1, concat_axis=3, tiled=True)
    stacked = stacked.reshape(2, layers, rows, cols)
    all_rows = jnp.arange(rows, dtype=jnp.int32)
    cos_table, sin_table = phase_table(all_rows[:, None], all_rows[None, :], rows, -1.0)
    real_part, imag_part = mix("lrs,rk->slk", stacked[0], stacked[1], cos_table, sin_table)
    stacked = jnp.stack([real_part, imag_part]).reshape(2, 1, col_parts, col_sub, block)
    stacked = lax.all_to_all(stacked, "by", split_axis=2, concat_axis=1, tiled=True)
    stacked = stacked.reshape(2, col_parts, col_sub, block)
    part_cols = jnp.arange(col_parts, dtype=jnp.int32)
    cos_table, sin_table = phase_table(part_cols[:, None], part_cols[None, :], col_parts, -1.0)
    real_part, imag_part = mix("jtb,jk->ktb", stacked[0], stacked[1], cos_table, sin_table)
    local_cols = col_me * col_sub + jnp.arange(col_sub, dtype=jnp.int32)
    cos_table, sin_table = phase_table(
        part_cols[:, None, None], local_cols[None, :, None], grid_y, -1.0
    )
    real_part, imag_part = rotate(real_part, imag_part, cos_table, sin_table)
    stacked = lax.all_to_all(
        jnp.stack([real_part, imag_part]), "by", split_axis=1, concat_axis=2, tiled=True
    )
    stacked = stacked.reshape(2, cols, block)
    all_cols = jnp.arange(cols, dtype=jnp.int32)
    cos_table, sin_table = phase_table(all_cols[:, None], all_cols[None, :], cols, -1.0)
    real_part, imag_part = mix("sb,sk->kb", stacked[0], stacked[1], cos_table, sin_table)
    return jnp.stack([real_part, imag_part]).reshape(2, cols, layers, rows)


def inverse(spectra):
    fields = spectra.shape[0]
    cols = spectra.shape[2]
    layers = spectra.shape[3]
    rows = spectra.shape[4]
    row_parts = lax.axis_size("bx")
    col_parts = lax.axis_size("by")
    row_me = lax.axis_index("bx")
    col_me = lax.axis_index("by")
    row_sub = rows // row_parts
    col_sub = cols // col_parts
    grid_x = rows * row_parts
    grid_y = cols * col_parts
    block = layers * rows
    all_cols = jnp.arange(cols, dtype=jnp.int32)
    cos_table, sin_table = phase_table(all_cols[:, None], all_cols[None, :], cols, 1.0)
    real_part, imag_part = mix(
        "fkb,ks->fsb",
        spectra[:, 0].reshape(fields, cols, block),
        spectra[:, 1].reshape(fields, cols, block),
        cos_table,
        sin_table,
    )
    cos_table, sin_table = phase_table(col_me, all_cols, grid_y, 1.0)
    real_part, imag_part = rotate(
        real_part, imag_part, cos_table[None, :, None], sin_table[None, :, None]
    )
    stacked = jnp.stack([real_part, imag_part], axis=1).reshape(
        fields, 2, 1, col_parts, col_sub, block
    )
    stacked = lax.all_to_all(stacked, "by", split_axis=3, concat_axis=2, tiled=True)
    stacked = stacked.reshape(fields, 2, col_parts, col_sub, block)
    part_cols = jnp.arange(col_parts, dtype=jnp.int32)
    cos_table, sin_table = phase_table(part_cols[:, None], part_cols[None, :], col_parts, 1.0)
    real_part, imag_part = mix("fktb,kj->fjtb", stacked[:, 0], stacked[:, 1], cos_table, sin_table)
    stacked = lax.all_to_all(
        jnp.stack([real_part, imag_part], axis=1), "by", split_axis=2, concat_axis=3, tiled=True
    )
    stacked = stacked.reshape(fields, 2, cols, layers, rows)
    all_rows = jnp.arange(rows, dtype=jnp.int32)
    cos_table, sin_table = phase_table(all_rows[:, None], all_rows[None, :], rows, 1.0)
    real_part, imag_part = mix("fslk,kr->flrs", stacked[:, 0], stacked[:, 1], cos_table, sin_table)
    cos_table, sin_table = phase_table(row_me, all_rows, grid_x, 1.0)
    real_part, imag_part = rotate(
        real_part, imag_part, cos_table[None, None, :, None], sin_table[None, None, :, None]
    )
    stacked = jnp.stack([real_part, imag_part], axis=1).reshape(
        fields, 2, 1, layers, row_parts, row_sub, cols
    )
    stacked = lax.all_to_all(stacked, "bx", split_axis=4, concat_axis=2, tiled=True)
    stacked = stacked.reshape(fields, 2, row_parts, layers * row_sub * cols)
    part_rows = jnp.arange(row_parts, dtype=jnp.int32)
    cos_table, sin_table = phase_table(part_rows[:, None], part_rows[None, :], row_parts, 1.0)
    real_out = jnp.einsum("fkb,ki->fib", stacked[:, 0], cos_table, precision=highest) - jnp.einsum(
        "fkb,ki->fib", stacked[:, 1], sin_table, precision=highest
    )
    real_out = real_out.reshape(fields, row_parts, layers, 1, row_sub, cols)
    real_out = lax.all_to_all(real_out, "bx", split_axis=1, concat_axis=3, tiled=True)
    return real_out.reshape(fields, layers, rows, cols) * (1.0 / (grid_x * grid_y))


def frequencies(rows, cols):
    row_parts = lax.axis_size("bx")
    col_parts = lax.axis_size("by")
    freq_x = (lax.axis_index("bx") + row_parts * jnp.arange(rows, dtype=jnp.int32)).astype(
        jnp.float32
    )
    freq_y = (lax.axis_index("by") + col_parts * jnp.arange(cols, dtype=jnp.int32)).astype(
        jnp.float32
    )
    return (freq_x[None, :], freq_y[:, None], rows * row_parts, cols * col_parts)


def solve(spectrum, freq_x, freq_y, grid_x, grid_y, permittivity, interfaces):
    layers = spectrum.shape[2]
    wave_x = jnp.sin(jnp.pi * freq_x / grid_x)
    wave_y = jnp.sin(jnp.pi * freq_y / grid_y)
    lateral = 4.0 * wave_x**2 + 4.0 * wave_y**2
    ratios = []
    primes = []
    for layer_no in range(layers):
        diagonal = (
            permittivity[layer_no] * lateral + interfaces[layer_no] + interfaces[layer_no + 1]
        )
        source = spectrum[:, :, layer_no, :]
        if layer_no == 0:
            pivot_now = diagonal
            primed = source / pivot_now
        else:
            pivot_now = diagonal - interfaces[layer_no] * ratios[-1]
            primed = (source + interfaces[layer_no] * primes[-1]) / pivot_now
        primes.append(primed)
        ratios.append(interfaces[layer_no + 1] / pivot_now)
    values = [primes[-1]]
    for layer_no in range(layers - 2, -1, -1):
        values.insert(0, primes[layer_no] + ratios[layer_no] * values[0])
    return jnp.stack(values, axis=2)


def back_transform(spectra):
    return inverse(spectra)


def evolve(padded, alpha_field, landau, stiffness, field_now):
    centre = padded[:, :, 1:-1, 1:-1]
    squares = centre * centre
    total = squares[0] + squares[1] + squares[2]
    quartic = landau[0][None, :, None, None]
    mixed = landau[1][None, :, None, None]
    sextic = landau[2][None, :, None, None]
    kappa = stiffness[None, :, None, None]
    lateral = (
        padded[:, :, 2:, 1:-1]
        + padded[:, :, :-2, 1:-1]
        + padded[:, :, 1:-1, 2:]
        + padded[:, :, 1:-1, :-2]
        - 4.0 * centre
    )
    vertical = shift_up(centre, 1) + shift_down(centre, 1) - 2.0 * centre
    drive = (
        2.0 * alpha_field[None] * centre
        + 4.0 * quartic * centre * squares
        + 2.0 * mixed * centre * (total[None] - squares)
        + 6.0 * sextic * centre * squares * squares
    )
    smooth = kappa * (lateral + vertical)
    return centre - step_size * (drive - smooth - field_now)


def shards(polarization, alpha_field, landau, stiffness, permittivity, interfaces):
    polar_now = polarization
    field_now = jnp.zeros_like(polarization)
    for step_no in range(STEPS):
        padded = extended(polar_now, (("bx", 2), ("by", 3)), 1)
        along_px = padded[0]
        along_py = padded[1]
        charge = -(
            0.5 * (along_px[:, 2:, 1:-1] - along_px[:, :-2, 1:-1])
            + 0.5 * (along_py[:, 1:-1, 2:] - along_py[:, 1:-1, :-2])
            + 0.5 * (shift_up(polar_now[2], 0) - shift_down(polar_now[2], 0))
        )
        spectrum = forward(charge)
        freq_x, freq_y, grid_x, grid_y = frequencies(charge.shape[1], charge.shape[2])
        potential_hat = solve(spectrum, freq_x, freq_y, grid_x, grid_y, permittivity, interfaces)
        slope_x = jnp.sin(2.0 * jnp.pi * freq_x / grid_x)[:, None, :]
        slope_y = jnp.sin(2.0 * jnp.pi * freq_y / grid_y)[:, None, :]
        real_part = potential_hat[0]
        imag_part = potential_hat[1]
        spec_x = jnp.stack([slope_x * imag_part, -slope_x * real_part])
        spec_y = jnp.stack([slope_y * imag_part, -slope_y * real_part])
        spec_z = -0.5 * (shift_up(potential_hat, 2) - shift_down(potential_hat, 2))
        field_now = back_transform(jnp.stack([spec_x, spec_y, spec_z]))
        polar_now = evolve(padded, alpha_field, landau, stiffness, field_now)
    return (polar_now, field_now)


def solution(mesh):
    return jax.shard_map(
        shards,
        mesh=mesh,
        in_specs=(P(None, None, "bx", "by"), P(None, "bx", "by"), P(), P(), P(), P()),
        out_specs=(P(None, None, "bx", "by"), P(None, None, "bx", "by")),
        check_vma=False,
    )
```

profile of v0, /device:TPU:1, one launch (start us, length us, event | category | flops | bytes accessed | tf_op | source)
XLA Modules:
  0.0 508.7 jit_solution(16399818373037090773)
XLA Ops:
  1.9 4.4 collective-permute-start.1
  6.3 12.1 %collective-permute-start = (f32[3,8,1,128]{3,1,2,0:T(8,128)S(1)}, f32[3,8,1,128]{3,1,2,0:T(8,128)S(1)}, u32[]{:S(2)}, u32[]{:S(2)}) collective-permute-start(f32[3,8,1,128]{3,1,2,0:T(8,128)S(1)} %get-tuple-element.76), channel_id=1, source_target_pairs={{16,0},{32,16},{48,32},{64,48},{80,64},{96,80},{112,96},{128,112},... | collective-permute-start | bytes 36872 | tf_op jit(solution)/shard_map/ppermute | solution.py:22
  24.7 3.0 collective-permute-start.3
  27.7 3.8 collective-permute-done.2
  34.2 8.9 %all-to-all-start = ((f32[1,8,32,1,128]{4,1,3,0,2:T(8,128)}), f32[1,8,32,1,128]{4,1,3,0,2:T(8,128)S(1)}, u32[]{:S(2)}, u32[]{:S(2)}) async-start(f32[1,8,32,1,128]{4,1,3,0,2:T(8,128)} %fusion.65), calls=%async_computation | async-start | bytes 262144 | tf_op jit(solution)/shard_map/all_to_all | solution.py:75
  43.9 15.2 %all-to-all-done = f32[1,8,32,1,128]{4,1,3,0,2:T(8,128)S(1)} async-done(((f32[1,8,32,1,128]{4,1,3,0,2:T(8,128)}), f32[1,8,32,1,128]{4,1,3,0,2:T(8,128)S(1)}, u32[]{:S(2)}, u32[]{:S(2)}) %all-to-all-start) | async-done | bytes 131104 | tf_op jit(solution)/shard_map/all_to_all | solution.py:75
  60.8 3.9 all-to-all-start.1
  66.2 17.0 %all-to-all-done.1 = f32[2,32,8,1,1,128]{5,2,0,4,3,1:T(8,128)S(1)} async-done(((f32[2,32,8,1,1,128]{5,2,0,4,3,1:T(8,128)}), f32[2,32,8,1,1,128]{5,2,0,4,3,1:T(8,128)S(1)}, u32[]{:S(2)}, u32[]{:S(2)}) %all-to-all-start.1) | async-done | bytes 262176 | tf_op jit(solution)/shard_map/all_to_all | solution.py:98
  86.4 13.7 %all-to-all-start.2 = ((f32[2,1,16,8,256]{4,3,1,0,2:T(8,128)}), f32[2,1,16,8,256]{4,3,1,0,2:T(8,128)S(1)}, u32[]{:S(2)}, u32[]{:S(2)}) async-start(f32[2,1,16,8,256]{4,3,1,0,2:T(8,128)} %copy.96), calls=%async_computation.2 | async-start | bytes 524288 | tf_op jit(solution)/shard_map/all_to_all | solution.py:104
  100.2 7.0 %all-to-all-done.2 = f32[2,1,16,8,256]{4,3,1,0,2:T(8,128)S(1)} async-done(((f32[2,1,16,8,256]{4,3,1,0,2:T(8,128)}), f32[2,1,16,8,256]{4,3,1,0,2:T(8,128)S(1)}, u32[]{:S(2)}, u32[]{:S(2)}) %all-to-all-start.2) | async-done | bytes 262176 | tf_op jit(solution)/shard_map/all_to_all | solution.py:104
  109.4 4.5 all-to-all-start.3
  114.0 10.9 %fusion.196 = (f32[128,32]{0,1:T(8,128)S(1)}, f32[128,32]{0,1:T(8,128)S(1)}, f32[128,32]{0,1:T(8,128)S(1)}, f32[128,32]{0,1:T(8,128)S(1)}, f32[128,32]{0,1:T(8,1...) fusion(f32[]{:T(128)} %bitcast.52, f32[]{:T(128)} %bitcast.51, ...), kind=kLoop, calls=%fused_computation.421 | loop fusion | flops 188416 | bytes 246468 | tf_op jit(solution)/shard_map/sub | solution.py:213
  127.4 3.8 fusion.127
  135.9 18.4 %all_to_all.180 = f32[3,2,1,16,8,256]{5,4,0,1,2,3:T(8,128)S(1)} all-to-all(f32[3,2,1,16,8,256]{5,4,0,1,2,3:T(8,128)S(1)} %copy.166), channel_id=1, replica_groups=mesh['bx'=32,'by'=16] {'by'}, dimensions={3} | all-to-all | bytes 1572864 | tf_op jit(solution)/shard_map/all_to_all | solution.py:154
  157.4 16.6 %all_to_all.181 = f32[3,2,16,8,256]{4,3,0,1,2:T(8,128)S(1)} all-to-all(f32[3,2,16,8,256]{4,3,0,1,2:T(8,128)S(1)} %copy.111), channel_id=1, replica_groups=mesh['bx'=32,'by'=16] {'by'}, dimensions={2} | all-to-all | bytes 1572864 | tf_op jit(solution)/shard_map/all_to_all | solution.py:159
  184.6 44.9 %all_to_all.182 = f32[3,2,1,8,32,1,128]{6,3,0,1,5,2,4:T(8,128)S(1)} all-to-all(f32[3,2,1,8,32,1,128]{6,3,0,1,5,2,4:T(8,128)S(1)} %copy.115), channel_id=1, replica_groups=mesh['bx'=32,'by'=16] {'bx'}, dimensions={4} | all-to-all | bytes 1572864 | tf_op jit(solution)/shard_map/all_to_all | solution.py:173
  232.4 7.4 %all-to-all-start.7 = ((f32[3,32,8,1,1,128]{5,2,0,4,3,1:T(8,128)}), f32[3,32,8,1,1,128]{5,2,0,4,3,1:T(8,128)S(1)}, u32[]{:S(2)}, u32[]{:S(2)}) async-start(f32[3,32,8,1,1,128]{5,2,0,4,3,1:T(8,128)} %copy.119), calls=%async_computation.7 | async-start | bytes 786432 | tf_op jit(solution)/shard_map/all_to_all | solution.py:181
  240.1 26.2 %all-to-all-done.7 = f32[3,32,8,1,1,128]{5,2,0,4,3,1:T(8,128)S(1)} async-done(((f32[3,32,8,1,1,128]{5,2,0,4,3,1:T(8,128)}), f32[3,32,8,1,1,128]{5,2,0,4,3,1:T(8,128)S(1)}, u32[]{:S(2)}, u32[]{:S(2)}) %all-to-all-start.7) | async-done | bytes 393248 | tf_op jit(solution)/shard_map/all_to_all | solution.py:181
  269.6 3.4 collective-permute-start.5
  273.0 4.7 collective-permute-done.5
  277.9 6.1 %collective-permute-start.6 = (f32[3,8,34,1]{3,1,2,0:T(8,128)S(1)}, f32[3,8,34,1]{3,1,2,0:T(8,128)S(1)}, u32[]{:S(2)}, u32[]{:S(2)}) collective-permute-start(f32[3,8,34,1]{3,1,2,0:T(8,128)S(1)} %get-tuple-element.60), channel_id=1, source_target_pairs={{1,0},{2,1},{3,2},{4,3},{5,4},{6,5},{7,6},{8,7},{9,8},{10,9},{11,1... | collective-permute-start | bytes 9800 | tf_op jit(solution)/shard_map/ppermute | solution.py:22
  285.9 3.0 collective-permute-done.6
  291.4 19.8 %all_to_all.183 = f32[1,8,32,1,128]{4,1,3,0,2:T(8,128)S(1)} all-to-all(f32[1,8,32,1,128]{4,1,3,0,2:T(8,128)S(1)} %fusion.59), channel_id=1, replica_groups=mesh['bx'=32,'by'=16] {'bx'}, dimensions={2} | all-to-all | bytes 262144 | tf_op jit(solution)/shard_map/all_to_all | solution.py:75
  312.1 21.8 %all_to_all.184 = f32[2,32,8,1,1,128]{5,2,0,4,3,1:T(8,128)S(1)} all-to-all(f32[2,32,8,1,1,128]{5,2,0,4,3,1:T(8,128)S(1)} %copy.123), channel_id=1, replica_groups=mesh['bx'=32,'by'=16] {'bx'}, dimensions={1} | all-to-all | bytes 524288 | tf_op jit(solution)/shard_map/all_to_all | solution.py:98
  336.4 19.5 %all_to_all.185 = f32[2,1,16,8,256]{4,3,1,0,2:T(8,128)S(1)} all-to-all(f32[2,1,16,8,256]{4,3,1,0,2:T(8,128)S(1)} %copy.127), channel_id=1, replica_groups=mesh['bx'=32,'by'=16] {'by'}, dimensions={2} | all-to-all | bytes 524288 | tf_op jit(solution)/shard_map/all_to_all | solution.py:104
  357.6 10.6 %all_to_all.186 = f32[2,16,8,256]{3,2,0,1:T(8,128)S(1)} all-to-all(f32[2,16,8,256]{3,2,0,1:T(8,128)S(1)} %copy.130), channel_id=1, replica_groups=mesh['bx'=32,'by'=16] {'by'}, dimensions={1} | all-to-all | bytes 524288 | tf_op jit(solution)/shard_map/all_to_all | solution.py:114
  370.5 3.8 fusion.107
  379.0 16.1 %all_to_all.187 = f32[3,2,1,16,8,256]{5,4,0,1,2,3:T(8,128)S(1)} all-to-all(f32[3,2,1,16,8,256]{5,4,0,1,2,3:T(8,128)S(1)} %copy.167), channel_id=1, replica_groups=mesh['bx'=32,'by'=16] {'by'}, dimensions={3} | all-to-all | bytes 1572864 | tf_op jit(solution)/shard_map/all_to_all | solution.py:154
  398.2 16.3 %all_to_all.188 = f32[3,2,16,8,256]{4,3,0,1,2:T(8,128)S(1)} all-to-all(f32[3,2,16,8,256]{4,3,0,1,2:T(8,128)S(1)} %copy.142), channel_id=1, replica_groups=mesh['bx'=32,'by'=16] {'by'}, dimensions={2} | all-to-all | bytes 1572864 | tf_op jit(solution)/shard_map/all_to_all | solution.py:159
  424.6 44.7 %all_to_all.189 = f32[3,2,1,8,32,1,128]{6,3,0,1,5,2,4:T(8,128)S(1)} all-to-all(f32[3,2,1,8,32,1,128]{6,3,0,1,5,2,4:T(8,128)S(1)} %copy.146), channel_id=1, replica_groups=mesh['bx'=32,'by'=16] {'bx'}, dimensions={4} | all-to-all | bytes 1572864 | tf_op jit(solution)/shard_map/all_to_all | solution.py:173
  472.1 7.6 %all-to-all-start.15 = ((f32[3,32,8,1,1,128]{5,2,0,4,3,1:T(8,128)}), f32[3,32,8,1,1,128]{5,2,0,4,3,1:T(8,128)S(1)}, u32[]{:S(2)}, u32[]{:S(2)}) async-start(f32[3,32,8,1,1,128]{5,2,0,4,3,1:T(8,128)} %copy.150), calls=%async_computation.15 | async-start | bytes 786432 | tf_op jit(solution)/shard_map/all_to_all | solution.py:181
  479.8 26.4 %all-to-all-done.15 = f32[3,32,8,1,1,128]{5,2,0,4,3,1:T(8,128)S(1)} async-done(((f32[3,32,8,1,1,128]{5,2,0,4,3,1:T(8,128)}), f32[3,32,8,1,1,128]{5,2,0,4,3,1:T(8,128)S(1)}, u32[]{:S(2)}, u32[]{:S(2)}) %all-to-all-start.15) | async-done | bytes 393248 | tf_op jit(solution)/shard_map/all_to_all | solution.py:181
  (370 shorter events, 80.1 us)
Async XLA Ops:
  1.9 16.5 %collective-permute-start.1 = (f32[3,8,1,128]{3,1,2,0:T(8,128)S(1)}, f32[3,8,1,128]{3,1,2,0:T(8,128)S(1)}, u32[]{:S(2)}, u32[]{:S(2)}) collective-permute-start(f32[3,8,1,128]{3,1,2,0:T(8,128)S(1)} %get-tuple-element.77), channel_id=1, source_target_pairs={{0,16},{16,32},{32,48},{48,64},{64,80},{80,96},{96,112},{112,128},... | collective-permute-start | bytes 36872 | tf_op jit(solution)/shard_map/ppermute | solution.py:19
  6.3 14.7 %collective-permute-start = (f32[3,8,1,128]{3,1,2,0:T(8,128)S(1)}, f32[3,8,1,128]{3,1,2,0:T(8,128)S(1)}, u32[]{:S(2)}, u32[]{:S(2)}) collective-permute-start(f32[3,8,1,128]{3,1,2,0:T(8,128)S(1)} %get-tuple-element.76), channel_id=1, source_target_pairs={{16,0},{32,16},{48,32},{64,48},{80,64},{96,80},{112,96},{128,112},... | collective-permute-start | bytes 36872 | tf_op jit(solution)/shard_map/ppermute | solution.py:22
  21.8 9.7 %collective-permute-start.2 = (f32[3,8,34,1]{3,1,2,0:T(8,128)S(1)}, f32[3,8,34,1]{3,1,2,0:T(8,128)S(1)}, u32[]{:S(2)}, u32[]{:S(2)}) collective-permute-start(f32[3,8,34,1]{3,1,2,0:T(8,128)S(1)} %get-tuple-element.63), channel_id=1, source_target_pairs={{1,0},{2,1},{3,2},{4,3},{5,4},{6,5},{7,6},{8,7},{9,8},{10,9},{11,1... | collective-permute-start | bytes 9800 | tf_op jit(solution)/shard_map/ppermute | solution.py:22
  24.7 8.0 %collective-permute-start.3 = (f32[3,8,34,1]{3,1,2,0:T(8,128)S(1)}, f32[3,8,34,1]{3,1,2,0:T(8,128)S(1)}, u32[]{:S(2)}, u32[]{:S(2)}) collective-permute-start(f32[3,8,34,1]{3,1,2,0:T(8,128)S(1)} %get-tuple-element.62), channel_id=1, source_target_pairs={{0,1},{1,2},{2,3},{3,4},{4,5},{5,6},{6,7},{7,8},{8,9},{9,10},{10,1... | collective-permute-start | bytes 9800 | tf_op jit(solution)/shard_map/ppermute | solution.py:19
  34.2 24.8 %all-to-all-start = ((f32[1,8,32,1,128]{4,1,3,0,2:T(8,128)}), f32[1,8,32,1,128]{4,1,3,0,2:T(8,128)S(1)}, u32[]{:S(2)}, u32[]{:S(2)}) async-start(f32[1,8,32,1,128]{4,1,3,0,2:T(8,128)} %fusion.65), calls=%async_computation | async-start | bytes 262144 | tf_op jit(solution)/shard_map/all_to_all | solution.py:75
  43.3 88.9 %copy-start.69 = (f32[32]{0:T(128)}, f32[32]{0:T(128)S(1)}, u32[]{:S(2)}) copy-start(f32[32]{0:T(128)S(1)} %get-tuple-element.180) | copy-start | bytes 388
  60.8 22.5 %all-to-all-start.1 = ((f32[2,32,8,1,1,128]{5,2,0,4,3,1:T(8,128)}), f32[2,32,8,1,1,128]{5,2,0,4,3,1:T(8,128)S(1)}, u32[]{:S(2)}, u32[]{:S(2)}) async-start(f32[2,32,8,1,1,128]{5,2,0,4,3,1:T(8,128)} %copy.92), calls=%async_computation.1 | async-start | bytes 524288 | tf_op jit(solution)/shard_map/all_to_all | solution.py:98
  64.7 67.5 %copy-start.75 = (f32[128]{0:T(128)}, f32[128]{0:T(128)S(1)}, u32[]{:S(2)}) copy-start(f32[128]{0:T(128)S(1)} %get-tuple-element.181) | copy-start | bytes 1540
  64.8 67.4 %copy-start.77 = (f32[32]{0:T(128)}, f32[32]{0:T(128)S(1)}, u32[]{:S(2)}) copy-start(f32[32]{0:T(128)S(1)} %get-tuple-element.176) | copy-start | bytes 388
  64.8 70.0 %copy-start.71 = (f32[128]{0:T(128)}, f32[128]{0:T(128)S(1)}, u32[]{:S(2)}) copy-start(f32[128]{0:T(128)S(1)} %get-tuple-element.183) | copy-start | bytes 1540
  64.8 70.0 %copy-start.73 = (f32[128]{0:T(128)}, f32[128]{0:T(128)S(1)}, u32[]{:S(2)}) copy-start(f32[128]{0:T(128)S(1)} %get-tuple-element.184) | copy-start | bytes 1540
  86.4 20.9 %all-to-all-start.2 = ((f32[2,1,16,8,256]{4,3,1,0,2:T(8,128)}), f32[2,1,16,8,256]{4,3,1,0,2:T(8,128)S(1)}, u32[]{:S(2)}, u32[]{:S(2)}) async-start(f32[2,1,16,8,256]{4,3,1,0,2:T(8,128)} %copy.96), calls=%async_computation.2 | async-start | bytes 524288 | tf_op jit(solution)/shard_map/all_to_all | solution.py:104
  109.4 15.6 %all-to-all-start.3 = ((f32[2,16,8,256]{3,2,0,1:T(8,128)}), f32[2,16,8,256]{3,2,0,1:T(8,128)S(1)}, u32[]{:S(2)}, u32[]{:S(2)}) async-start(f32[2,16,8,256]{3,2,0,1:T(8,128)} %copy.99), calls=%async_computation.3 | async-start | bytes 524288 | tf_op jit(solution)/shard_map/all_to_all | solution.py:114
  232.4 33.9 %copy-start.7 = (f32[3,8,34,1]{3,1,2,0:T(8,128)S(1)}, f32[3,8,34,1]{3,1,2,0:T(8,128)}, u32[]{:S(2)}) copy-start(f32[3,8,34,1]{3,1,2,0:T(8,128)} %copy-done.6) | copy-start | bytes 9796
  232.4 33.9 %copy-start.50 = (f32[3,8,1,128]{3,1,2,0:T(8,128)S(1)}, f32[3,8,1,128]{3,1,2,0:T(8,128)}, u32[]{:S(2)}) copy-start(f32[3,8,1,128]{3,1,2,0:T(8,128)} %copy-done.49) | copy-start | bytes 36868
  232.4 33.9 %copy-start.52 = (f32[3,8,1,128]{3,1,2,0:T(8,128)S(1)}, f32[3,8,1,128]{3,1,2,0:T(8,128)}, u32[]{:S(2)}) copy-start(f32[3,8,1,128]{3,1,2,0:T(8,128)} %copy-done.51) | copy-start | bytes 36868
  232.4 33.9 %copy-start.83 = (f32[8]{0:T(128)S(1)}, f32[8]{0:T(128)}, u32[]{:S(2)}) copy-start(f32[8]{0:T(128)} %param.9) | copy-start | bytes 100
  232.4 33.9 %all-to-all-start.7 = ((f32[3,32,8,1,1,128]{5,2,0,4,3,1:T(8,128)}), f32[3,32,8,1,1,128]{5,2,0,4,3,1:T(8,128)S(1)}, u32[]{:S(2)}, u32[]{:S(2)}) async-start(f32[3,32,8,1,1,128]{5,2,0,4,3,1:T(8,128)} %copy.119), calls=%async_computation.7 | async-start | bytes 786432 | tf_op jit(solution)/shard_map/all_to_all | solution.py:181
  267.7 5.3 %collective-permute-start.4 = (f32[3,8,1,128]{3,1,2,0:T(8,128)S(1)}, f32[3,8,1,128]{3,1,2,0:T(8,128)S(1)}, u32[]{:S(2)}, u32[]{:S(2)}) collective-permute-start(f32[3,8,1,128]{3,1,2,0:T(8,128)S(1)} %get-tuple-element.69), channel_id=1, source_target_pairs={{16,0},{32,16},{48,32},{64,48},{80,64},{96,80},{112,96},{128,112},... | collective-permute-start | bytes 36872 | tf_op jit(solution)/shard_map/ppermute | solution.py:22
  269.6 8.1 %collective-permute-start.5 = (f32[3,8,1,128]{3,1,2,0:T(8,128)S(1)}, f32[3,8,1,128]{3,1,2,0:T(8,128)S(1)}, u32[]{:S(2)}, u32[]{:S(2)}) collective-permute-start(f32[3,8,1,128]{3,1,2,0:T(8,128)S(1)} %get-tuple-element.68), channel_id=1, source_target_pairs={{0,16},{16,32},{32,48},{48,64},{64,80},{80,96},{96,112},{112,128},... | collective-permute-start | bytes 36872 | tf_op jit(solution)/shard_map/ppermute | solution.py:19
  277.9 11.0 %collective-permute-start.6 = (f32[3,8,34,1]{3,1,2,0:T(8,128)S(1)}, f32[3,8,34,1]{3,1,2,0:T(8,128)S(1)}, u32[]{:S(2)}, u32[]{:S(2)}) collective-permute-start(f32[3,8,34,1]{3,1,2,0:T(8,128)S(1)} %get-tuple-element.60), channel_id=1, source_target_pairs={{1,0},{2,1},{3,2},{4,3},{5,4},{6,5},{7,6},{8,7},{9,8},{10,9},{11,1... | collective-permute-start | bytes 9800 | tf_op jit(solution)/shard_map/ppermute | solution.py:22
  283.9 6.9 %collective-permute-start.7 = (f32[3,8,34,1]{3,1,2,0:T(8,128)S(1)}, f32[3,8,34,1]{3,1,2,0:T(8,128)S(1)}, u32[]{:S(2)}, u32[]{:S(2)}) collective-permute-start(f32[3,8,34,1]{3,1,2,0:T(8,128)S(1)} %get-tuple-element.61), channel_id=1, source_target_pairs={{0,1},{1,2},{2,3},{3,4},{4,5},{5,6},{6,7},{7,8},{8,9},{9,10},{10,1... | collective-permute-start | bytes 9800 | tf_op jit(solution)/shard_map/ppermute | solution.py:19
  472.1 34.2 %copy-start.9 = (f32[3,8,34,1]{3,1,2,0:T(8,128)S(1)}, f32[3,8,34,1]{3,1,2,0:T(8,128)}, u32[]{:S(2)}) copy-start(f32[3,8,34,1]{3,1,2,0:T(8,128)} %copy-done.8) | copy-start | bytes 9796
  472.1 34.2 %copy-start.11 = (f32[3,8,34,1]{3,1,2,0:T(8,128)S(1)}, f32[3,8,34,1]{3,1,2,0:T(8,128)}, u32[]{:S(2)}) copy-start(f32[3,8,34,1]{3,1,2,0:T(8,128)} %copy-done.10) | copy-start | bytes 9796
  472.1 34.2 %copy-start.15 = (f32[8,32,128]{2,0,1:T(8,128)S(1)}, f32[8,32,128]{2,0,1:T(8,128)}, u32[]{:S(2)}) copy-start(f32[8,32,128]{2,0,1:T(8,128)} %copy-done.14) | copy-start | bytes 393220
  472.1 34.2 %copy-start.46 = (f32[3,8,1,128]{3,1,2,0:T(8,128)S(1)}, f32[3,8,1,128]{3,1,2,0:T(8,128)}, u32[]{:S(2)}) copy-start(f32[3,8,1,128]{3,1,2,0:T(8,128)} %copy-done.45) | copy-start | bytes 36868
  472.1 34.2 %copy-start.48 = (f32[3,8,1,128]{3,1,2,0:T(8,128)S(1)}, f32[3,8,1,128]{3,1,2,0:T(8,128)}, u32[]{:S(2)}) copy-start(f32[3,8,1,128]{3,1,2,0:T(8,128)} %copy-done.47) | copy-start | bytes 36868
  472.1 34.2 %copy-start.63 = (f32[8]{0:T(128)S(1)}, f32[8]{0:T(128)}, u32[]{:S(2)}) copy-start(f32[8]{0:T(128)} %copy-done.62) | copy-start | bytes 100
  472.1 34.2 %copy-start.65 = (f32[8]{0:T(128)S(1)}, f32[8]{0:T(128)}, u32[]{:S(2)}) copy-start(f32[8]{0:T(128)} %copy-done.64) | copy-start | bytes 100
  472.1 34.2 %copy-start.67 = (f32[8]{0:T(128)S(1)}, f32[8]{0:T(128)}, u32[]{:S(2)}) copy-start(f32[8]{0:T(128)} %copy-done.66) | copy-start | bytes 100
  472.1 34.2 %copy-start.84 = (f32[8]{0:T(128)S(1)}, f32[8]{0:T(128)}, u32[]{:S(2)}) copy-start(f32[8]{0:T(128)} %param.9) | copy-start | bytes 100
  472.1 34.1 %all-to-all-start.15 = ((f32[3,32,8,1,1,128]{5,2,0,4,3,1:T(8,128)}), f32[3,32,8,1,1,128]{5,2,0,4,3,1:T(8,128)S(1)}, u32[]{:S(2)}, u32[]{:S(2)}) async-start(f32[3,32,8,1,1,128]{5,2,0,4,3,1:T(8,128)} %copy.150), calls=%async_computation.15 | async-start | bytes 786432 | tf_op jit(solution)/shard_map/all_to_all | solution.py:181
  (68 other events, 811.1 us)
where the time goes:
time: 516 us; the launch traced here: 509 us
  blocking collectives  229 us (44%)
  waiting for transfers between devices  106 us (21%)
  starting transfers between devices  81.6 us (16%)
  local copies, waits for them, and re-layouts  31.8 us (6%)
  matrix products  29.3 us (6%)
  other arithmetic  27.8 us (5%)
    all_to_all x2, blocking collectives, inverse(): lax.all_to_all(stacked, 'bx', split_axis=4, concat_axis=2, tiled=True)  89.5 us
    all_to_all x2, waiting for transfers between devices, inverse(): lax.all_to_all(real_out, 'bx', split_axis=1, concat_axis=3, tiled=True)  52.6 us
    all_to_all x2, blocking collectives, inverse(): lax.all_to_all(stacked, 'by', split_axis=3, concat_axis=2, tiled=True)  34.5 us
    all_to_all x2, blocking collectives, inverse(): lax.all_to_all(jnp.stack([real_part, imag_part], axis=1), 'by', split_axi...  32.9 us
    ppermute x4, starting transfers between devices, extended(): lax.ppermute(lax.slice_in_dim(block, 0, width, axis=dim), axis, backward)  23 us
    all_to_all x1, blocking collectives, forward(): lax.all_to_all(stacked, 'bx', split_axis=1, concat_axis=3, tiled=True)  21.8 us
    all_to_all x1, blocking collectives, forward(): lax.all_to_all(charge.reshape(1, layers, row_parts, row_sub, cols), 'bx',...  19.8 us
    all_to_all x1, blocking collectives, forward(): lax.all_to_all(stacked, 'by', split_axis=2, concat_axis=1, tiled=True)  19.5 us
  transfers between devices with their start and end apart: 14, of which 10 were waited for; matrix products, arithmetic and copies ran while one was open for 3% of the time, Pallas kernels for 0%

commit v1 on v0

v1 whole, which is shorter than its diff:
```python
import functools

import jax
import jax.numpy as jnp
import ml_dtypes
import numpy as np
from jax import lax
from jax.experimental import pallas as pl
from jax.experimental.pallas import tpu as pltpu
from jax.sharding import PartitionSpec as P

DT = 0.05
NB = 16
LANES = 128
ROWS = 32
LAYERS = 8
SLOT = 72
BACK = 40
F32 = jnp.float32
BF16 = jnp.bfloat16
PARAMS = pltpu.CompilerParams(vmem_limit_bytes=48 * 1024 * 1024)


def split_table(table):
    high = table.astype(ml_dtypes.bfloat16)
    low = (table - high.astype(np.float64)).astype(ml_dtypes.bfloat16)
    return high, low


def tables_y():
    n = NB * LANES
    t = np.arange(LANES)
    k = np.arange(LANES)
    ang = 2 * np.pi * np.outer(k, t) / LANES
    c, s = np.cos(ang), np.sin(ang)
    fwd = np.block([[c, s], [-s, c]])
    inv = np.block([[c.T, -s.T], [s.T, c.T]]) * (2.0 / n)
    fwd0 = np.zeros((256, 256))
    inv0 = np.zeros((256, 256))
    for i in range(LANES):
        m = i if i <= 64 else i - 64
        wave = np.cos(2 * np.pi * m * t / LANES) if i <= 64 else np.sin(2 * np.pi * m * t / LANES)
        fwd0[i, :LANES] = wave
        inv0[:LANES, i] = wave * ((1.0 if i in (0, 64) else 2.0) / n)
    for i in range(64):
        th = 2 * np.pi * (8 + 16 * i) * t / n
        fwd0[128 + i, LANES:] = np.cos(th)
        fwd0[192 + i, LANES:] = -np.sin(th)
        inv0[LANES:, 128 + i] = np.cos(th) * (2.0 / n)
        inv0[LANES:, 192 + i] = -np.sin(th) * (2.0 / n)
    tw = np.zeros((16, LANES), np.float32)
    for j in range(8):
        tw[j] = np.cos(2 * np.pi * j * t / n)
        tw[8 + j] = np.sin(2 * np.pi * j * t / n)
    return fwd, fwd0, inv, inv0, tw


def tables_x(nx):
    half = nx // 2
    pos = np.arange(half)
    freq = []
    rows = []
    scale = np.sqrt(2.0 / nx)
    for k in range(0, half + 1, 2):
        w = np.cos(2 * np.pi * k * pos / nx)
        rows.append(w * (np.sqrt(1.0 / nx) if k in (0, half) else scale))
        freq.append(k)
    for k in range(2, half, 2):
        rows.append(np.sin(2 * np.pi * k * pos / nx) * scale)
        freq.append(k)
    for k in range(1, half, 2):
        rows.append(np.cos(2 * np.pi * k * pos / nx) * scale)
        freq.append(k)
    for k in range(1, half, 2):
        rows.append(np.sin(2 * np.pi * k * pos / nx) * scale)
        freq.append(k)
    table = np.stack(rows)
    order = np.array(
        [bx * ROWS + xl * NB + by for xl in range(2) for bx in range(half // ROWS) for by in range(NB)]
    )
    table = table[:, order]
    freq = np.array(freq)
    lam = np.zeros((8, nx), np.float32)
    lam[0] = 4 * np.sin(np.pi * freq / nx) ** 2
    lam[1] = np.sin(2 * np.pi * freq / nx) ** 2
    return table, lam


def split(value):
    high = value.astype(BF16)
    return high, (value - high.astype(F32)).astype(BF16)


def dot(a, b):
    return lax.dot_general(a, b, (((1,), (0,)), ((), ())), preferred_element_type=F32)


def dot_t(a, b):
    return lax.dot_general(a, b, (((1,), (1,)), ((), ())), preferred_element_type=F32)


def shift(value, by):
    n = value.shape[1]
    return pltpu.roll(value, by % n, axis=1)


def pack(tile):
    lane = lax.broadcasted_iota(jnp.int32, tile.shape, 1)
    edge = jnp.where((lane < 2) | (lane >= 126), tile, 0.0)
    return jnp.sum(pltpu.roll(edge, 0, axis=1, stride=4, stride_axis=0), axis=0, keepdims=True)


def unpack(row):
    value = jnp.broadcast_to(row, (8, LANES))
    index = lax.broadcasted_iota(jnp.int32, (8, LANES), 0)
    for bit in (1, 2, 4):
        value = jnp.where(index // bit % 2 == 1, pltpu.roll(value, LANES - 4 * bit, axis=1), value)
    return jnp.concatenate(
        [value] + [pltpu.roll(value, LANES - 32 * t, axis=1) for t in range(1, 4)], axis=0
    )


def drive_of(value, alpha2, total, quartic, mixed, sextic):
    sq = value * value
    return value * (
        alpha2 + 4.0 * quartic * sq + 2.0 * mixed * (total - sq) + 6.0 * sextic * (sq * sq)
    )


def charge_kernel(p_ref, al_ref, lo_ref, hi_ref, first_ref, last_ref, landau, stiff, out_ref, px, nx, ws):
    lane = lax.broadcasted_iota(jnp.int32, (ROWS, LANES), 1)
    for c in range(3):
        for l in range(LAYERS):
            n = c * LAYERS + l
            px[n, 8:40, :] = p_ref[c, l]
            px[n, 7:8, :] = lo_ref[1, n : n + 1, :]
            px[n, 40:41, :] = hi_ref[0, n : n + 1, :]
    row = lax.broadcasted_iota(jnp.int32, (LAYERS, LANES), 0)

    def by_layer(get):
        value = jnp.full((LAYERS, LANES), get(0), F32)
        for l in range(1, LAYERS):
            value = jnp.where(row == l, get(l), value)
        return value

    quartic = by_layer(lambda l: landau[0, l])
    mixed = by_layer(lambda l: landau[1, l])
    sextic = by_layer(lambda l: landau[2, l])
    kappa = by_layer(lambda l: stiff[l])
    for ref, at, outer, inner, target in (
        (lo_ref, 1, lo_ref[0, 0:8, :], first_ref[0, 0:8, :], 7),
        (hi_ref, 0, hi_ref[1, 0:8, :], last_ref[1, 0:8, :], 40),
    ):
        p0, p1, p2 = ref[at, 0:8, :], ref[at, 8:16, :], ref[at, 16:24, :]
        total = p0 * p0 + p1 * p1 + p2 * p2
        drive = drive_of(p0, 2.0 * ref[at, 24:32, :], total, quartic, mixed, sextic)
        up = jnp.where(row == LAYERS - 1, 0.0, pltpu.roll(p0, LAYERS - 1, axis=0))
        down = jnp.where(row == 0, 0.0, pltpu.roll(p0, 1, axis=0))
        value = p0 - DT * (drive - kappa * (outer + inner + up + down - 6.0 * p0))
        for l in range(LAYERS):
            nx[l, target : target + 1, :] = value[l : l + 1, :]

    def layer(ref, c, l):
        return ref[c, l] if 0 <= l < LAYERS else jnp.zeros((ROWS, LANES), F32)

    n1 = []
    n2 = []
    for l in range(LAYERS):
        p = [p_ref[c, l] for c in range(3)]
        total = p[0] * p[0] + p[1] * p[1] + p[2] * p[2]
        alpha2 = 2.0 * al_ref[l]
        e = DT * stiff[l]
        for c in range(3):
            n = c * LAYERS + l
            drive = drive_of(p[c], alpha2, total, landau[0, l], landau[1, l], landau[2, l])
            lap = (
                px[n, 9:41, :]
                + px[n, 7:39, :]
                + layer(p_ref, c, l + 1)
                + layer(p_ref, c, l - 1)
                - 6.0 * p[c]
            )
            value = p[c] - DT * drive + e * lap
            if c == 0:
                nx[l, 8:40, :] = value
            elif c == 1:
                n1.append(value)
            else:
                n2.append(value)
    for l in range(LAYERS):
        e = DT * stiff[l]
        zero = jnp.zeros((ROWS, LANES), F32)
        dx = -0.5 * (px[l, 9:41, :] - px[l, 7:39, :])
        above, below = layer(p_ref, 2, l + 1), layer(p_ref, 2, l - 1)
        p1 = p_ref[1, l]
        fwd, bwd = shift(p1, -1), shift(p1, 1)
        one = dx - 0.5 * (above - below) - 0.5 * (fwd - bwd)
        wrap_one = jnp.where(lane == LANES - 1, -0.5 * fwd, jnp.where(lane == 0, 0.5 * bwd, 0.0))
        e_up = DT * stiff[l + 1] if l + 1 < LAYERS else 0.0
        e_dn = DT * stiff[l - 1] if l > 0 else 0.0
        ue = e * dx - 0.5 * (e_up * above - e_dn * below)
        un = -0.5 * (nx[l, 9:41, :] - nx[l, 7:39, :]) - 0.5 * (
            (n2[l + 1] if l + 1 < LAYERS else zero) - (n2[l - 1] if l > 0 else zero)
        )
        a = shift(ue - 0.5 * n1[l], -1)
        b = shift(ue + 0.5 * n1[l], 1)
        h = (0.5 * e) * p1
        c2, d2 = shift(h, -2), shift(h, 2)
        two = un + a + b - c2 + d2
        wrap_two = (
            jnp.where(lane == LANES - 1, a, 0.0)
            + jnp.where(lane == 0, b, 0.0)
            + jnp.where(lane >= LANES - 2, -c2, 0.0)
            + jnp.where(lane < 2, d2, 0.0)
        )
        for f, (whole, wrap) in enumerate(((one, wrap_one), (two, wrap_two))):
            main = whole - wrap
            for xl in range(2):
                r = f * 16 + xl * 8 + l
                out_ref[pl.ds(r, NB, stride=SLOT), :] = main[xl * NB : (xl + 1) * NB]
                ws[pl.ds(r, NB, stride=32), :] = wrap[xl * NB : (xl + 1) * NB]
    tail = jnp.concatenate(
        [pack(lo_ref[1]), pack(hi_ref[0]), jnp.zeros((SLOT - 67, LANES), F32)], axis=0
    )
    for l in range(24):
        px[l, 0:1, :] = pack(p_ref[l // LAYERS, l % LAYERS])
    edges = [px[l, 0:1, :] for l in range(24)] + [pack(al_ref[l]) for l in range(LAYERS)]
    edges = jnp.concatenate(edges, axis=0)
    for b in range(NB):
        base = b * SLOT
        out_ref[base + 32 : base + 64, :] = edges
        out_ref[base + 64 : base + 65, :] = pack(ws[b * 32 : (b + 1) * 32, :])
        out_ref[base + 65 : base + SLOT, :] = tail


def y_forward_kernel(in_ref, fh, fl, f0h, f0l, tw, out_ref, d_ref, o_ref):
    lane1 = lax.broadcasted_iota(jnp.int32, (1, LANES), 1)
    lane = lax.broadcasted_iota(jnp.int32, (ROWS, LANES), 1)
    g = []
    for b in range(NB):
        before = in_ref[((b - 1) % NB) * SLOT + 64 : ((b - 1) % NB) * SLOT + 65, :]
        after = in_ref[((b + 1) % NB) * SLOT + 64 : ((b + 1) % NB) * SLOT + 65, :]
        extra = unpack(jnp.where(lane1 % 4 < 2, before, after))
        g.append(
            in_ref[b * SLOT : b * SLOT + 32, :]
            + jnp.where((lane < 2) | (lane >= 126), extra, 0.0)
        )
    plus = {b: g[b] + g[NB - b] for b in range(1, 8)}
    minus = {b: g[b] - g[NB - b] for b in range(1, 8)}
    re, im = {}, {}
    for k in range(5):
        even = g[0] + g[8] if k % 2 == 0 else g[0] - g[8]
        odd = jnp.zeros_like(even)
        s_even, s_odd = jnp.zeros_like(even), jnp.zeros_like(even)
        for b in range(1, 8):
            c, s = np.cos(2 * np.pi * b * k / 16), np.sin(2 * np.pi * b * k / 16)
            tc = plus[b] * float(c) if abs(c) > 1e-9 else None
            ts = minus[b] * float(s) if abs(s) > 1e-9 else None
            if b % 2 == 0:
                even = even + tc if tc is not None else even
                s_even = s_even + ts if ts is not None else s_even
            else:
                odd = odd + tc if tc is not None else odd
                s_odd = s_odd + ts if ts is not None else s_odd
        re[k], re[8 - k] = even + odd, even - odd
        im[k], im[8 - k] = -(s_even + s_odd), s_even - s_odd
    d_ref[0:32, 0:LANES] = re[0]
    d_ref[0:32, LANES:256] = re[8]
    re[4] = re[4]
    for j in range(1, 8):
        c, s = tw[j : j + 1, :], tw[8 + j : 9 + j, :]
        d_ref[j * 32 : (j + 1) * 32, 0:LANES] = re[j] * c + im[j] * s
        d_ref[j * 32 : (j + 1) * 32, LANES:256] = im[j] * c - re[j] * s
    dh, dl = split(d_ref[...])
    o_ref[...] = dot_t(fh[...], dh) + dot_t(fh[...], dl) + dot_t(fl[...], dh)
    zero = dot_t(f0h[...], dh[0:128]) + dot_t(f0h[...], dl[0:128]) + dot_t(f0l[...], dh[0:128])
    wide = lax.broadcasted_iota(jnp.int32, (256, LANES), 1)
    o_ref[:, 0:LANES] = jnp.where(wide < 32, zero, o_ref[:, 0:LANES])
    lane64 = lax.broadcasted_iota(jnp.int32, (64, LANES), 1)
    for j in range(8):
        t, at = j // 4, j % 4
        value = None
        for q in range(4):
            piece = o_ref[q * 64 : (q + 1) * 64, t * LANES : (t + 1) * LANES]
            if q != at:
                piece = shift(piece, (q - at) * 32)
            value = piece if value is None else jnp.where(lane64 // 32 == q, piece, value)
        out_ref[j * 64 : (j + 1) * 64, :] = value


def x_kernel(in_ref, th, tl, uh, ul, lam, eps, iface, out_ref, zs, ys):
    n = in_ref.shape[0]
    half = n // 2
    top, low = in_ref[0:half, :], in_ref[half:n, :]
    for part, value in enumerate((top + low, top - low)):
        high, rest = split(value)
        both = jnp.concatenate([high, rest], axis=1)
        for chunk in range(n // 256):
            r0 = part * n + chunk * 256
            acc = []
            for xl in range(2):
                cols = slice(xl * half, (xl + 1) * half)
                wide = dot(th[r0 : r0 + 256, cols], both)
                acc.append(
                    wide[:, 0:LANES] + wide[:, LANES:256] + dot(tl[r0 : r0 + 256, cols], high)
                )
            turned = jnp.transpose(acc[0] + shift(acc[1], -8))
            zs[r0 : r0 + LANES, :] = turned[:, 0:LANES]
            zs[r0 + LANES : r0 + 256, :] = turned[:, LANES:256]
    dev = lax.axis_index("bx") * NB + lax.axis_index("by")
    j = dev // 64
    q = lax.broadcasted_iota(jnp.int32, (8, 1), 0) // 2
    s = q * 64 + dev % 64
    ky_j = j + 16 * (s % 128)
    ky_0 = jnp.where(s < 128, 16 * jnp.where(s <= 64, s, s - 64), 8 + 16 * (s % 64))
    ky = jnp.where(j == 0, ky_0, ky_j)
    full = NB * LANES
    ky = jnp.minimum(ky, full - ky).astype(F32)
    ky = jnp.broadcast_to(ky, (8, LANES))
    sin_half = jnp.sin(ky * (np.pi / full))
    lam_y = 4.0 * sin_half * sin_half
    sin_y = jnp.sin(jnp.minimum(ky, full // 2 - ky) * (2.0 * np.pi / full))
    slope_y = sin_y * sin_y
    second = lax.broadcasted_iota(jnp.int32, (8, LANES), 0) % 2 == 1
    for chunk in range(2 * n // LANES):
        cols = slice(chunk * LANES, (chunk + 1) * LANES)
        lateral = lam_y + lam[0:1, cols]
        slope = slope_y + lam[1:2, cols]
        inverse, ratio = [], []
        for l in range(LAYERS):
            pivot = eps[l] * lateral + (iface[l] + iface[l + 1])
            if l > 0:
                pivot = pivot - iface[l] * ratio[-1]
            inverse.append(1.0 / pivot)
            ratio.append(iface[l + 1] * inverse[-1])

        def solve(source):
            prime = []
            for l in range(LAYERS):
                value = source[l] + iface[l] * prime[-1] if l > 0 else source[l]
                prime.append(value * inverse[l])
            for l in range(LAYERS - 2, -1, -1):
                prime[l] = prime[l] + ratio[l] * prime[l + 1]
            return prime

        phi = solve([zs[pl.ds(chunk * LANES + l, 8, stride=16), :] for l in range(LAYERS)])
        first = [jnp.where(second, pltpu.roll(v, 1, axis=0), 0.0) for v in phi]
        zero = jnp.zeros_like(first[0])

        def dz(v):
            return [
                0.5 * ((v[l + 1] if l + 1 < LAYERS else zero) - (v[l - 1] if l > 0 else zero))
                for l in range(LAYERS)
            ]

        twice = dz(dz(first))
        more = solve([DT * (twice[l] - slope * first[l]) for l in range(LAYERS)])
        for l in range(LAYERS):
            value = phi[l] + more[l]
            ys[pl.ds(chunk * LANES + l, 8, stride=16), :] = value
            ys[pl.ds(chunk * LANES + 8 + l, 8, stride=16), :] = value
    lane = lax.broadcasted_iota(jnp.int32, (half, LANES), 1)
    odd_row = lane // 8 % 2 == 1
    pair = []
    for part in range(2):
        cols = slice(part * n, (part + 1) * n)
        high, rest = split(
            jnp.concatenate([ys[r : r + LANES, :] for r in range(part * n, (part + 1) * n, LANES)], axis=1)
        )
        both = jnp.concatenate([high, rest], axis=0)
        acc = []
        for xl in range(2):
            rows = slice(xl * half, (xl + 1) * half)
            wide = dot_t(uh[rows, cols], both)
            acc.append(wide[:, 0:LANES] + wide[:, LANES:256] + dot_t(ul[rows, cols], high))
        pair.append(jnp.where(odd_row, acc[1], acc[0]))
    out_ref[0:half, :] = pair[0] + pair[1]
    out_ref[half:n, :] = pair[0] - pair[1]


def y_inverse_kernel(in_ref, gh, gl, g0h, g0l, tw, out_ref, o_ref):
    lane64 = lax.broadcasted_iota(jnp.int32, (64, LANES), 1)
    for t in range(2):
        for q in range(4):
            value = None
            for at in range(4):
                j = t * 4 + at
                piece = in_ref[j * 64 : (j + 1) * 64, :]
                if q != at:
                    piece = shift(piece, (at - q) * 32)
                value = piece if value is None else jnp.where(lane64 // 32 == at, piece, value)
            o_ref[q * 64 : (q + 1) * 64, t * LANES : (t + 1) * LANES] = value
    oh, ol = split(o_ref[...])
    o_ref[...] = dot(gh[...], oh) + dot(gh[...], ol) + dot(gl[...], oh)
    zero = (
        dot(g0h[...], oh[:, 0:LANES]) + dot(g0h[...], ol[:, 0:LANES]) + dot(g0l[...], oh[:, 0:LANES])
    )
    wide = lax.broadcasted_iota(jnp.int32, (256, LANES), 1)
    o_ref[:, 0:LANES] = jnp.where(wide < 32, zero, o_ref[:, 0:LANES])
    g = jnp.transpose(o_ref[...])
    hr, hi = {}, {}
    for j in range(1, 8):
        c, s = tw[j : j + 1, :], tw[8 + j : 9 + j, :]
        a, b = g[j * 32 : (j + 1) * 32, 0:LANES], g[j * 32 : (j + 1) * 32, LANES:256]
        hr[j] = a * c - b * s
        hi[j] = a * s + b * c
    g0, g8 = g[0:32, 0:LANES], g[0:32, LANES:256]
    out = {}
    for b in range(5):
        even = g0 + g8 if b % 2 == 0 else g0 - g8
        odd = jnp.zeros_like(even)
        s_even, s_odd = jnp.zeros_like(even), jnp.zeros_like(even)
        for j in range(1, 8):
            c, s = np.cos(2 * np.pi * b * j / 16), np.sin(2 * np.pi * b * j / 16)
            tc = hr[j] * float(c) if abs(c) > 1e-9 else None
            ts = hi[j] * float(s) if abs(s) > 1e-9 else None
            if j % 2 == 0:
                even = even + tc if tc is not None else even
                s_even = s_even + ts if ts is not None else s_even
            else:
                odd = odd + tc if tc is not None else odd
                s_odd = s_odd + ts if ts is not None else s_odd
        cos_b, sin_b = even + odd, s_even + s_odd
        cos_c, sin_c = even - odd, s_odd - s_even
        out[b] = cos_b - sin_b
        out[(NB - b) % NB] = cos_b + sin_b
        out[8 - b] = cos_c - sin_c
        out[8 + b] = cos_c + sin_c
    lane = lax.broadcasted_iota(jnp.int32, (ROWS, LANES), 1)
    blank = jnp.zeros((BACK - 33, LANES), F32)
    for b in range(NB):
        out_ref[b * BACK : b * BACK + 32, :] = out[b]
        border = jnp.where(lane < 2, out[(b + 1) % NB], out[(b - 1) % NB])
        out_ref[b * BACK + 32 : (b + 1) * BACK, :] = jnp.concatenate([pack(border), blank], axis=0)


def update_kernel(
    p_ref, al_ref, lo_ref, hi_ref, e_ref, phi_ref, flo_ref, fhi_ref, landau, stiff,
    out_ref, field_ref, px, fx, qx, ht,
):
    main, side = slice(0, LANES), slice(LANES, 2 * LANES)
    lane1 = lax.broadcasted_iota(jnp.int32, (ROWS, LANES), 1) % 4 < 2
    by = lax.axis_index("by")
    left, right = (by + NB - 1) % NB, (by + 1) % NB
    edges = jnp.where(lane1, e_ref[right, 32:64, :], e_ref[left, 32:64, :])
    corner = jnp.where(lane1[0:8], e_ref[right, 64:72, :], e_ref[left, 64:72, :])
    corner_lo, corner_hi = unpack(corner[1:2]), unpack(corner[2:3])
    for n in range(32):
        px[n, 8:40, main] = p_ref[n // LAYERS, n % LAYERS] if n < 24 else al_ref[n - 24]
        px[n, 8:40, side] = unpack(edges[n : n + 1])
        px[n, 6:7, main] = lo_ref[0, n : n + 1, :]
        px[n, 7:8, main] = lo_ref[1, n : n + 1, :]
        px[n, 40:41, main] = hi_ref[0, n : n + 1, :]
        px[n, 41:42, main] = hi_ref[1, n : n + 1, :]
        px[n, 7:8, side] = corner_lo[n : n + 1]
        px[n, 40:41, side] = corner_hi[n : n + 1]
        px[n, 6:7, side] = corner_lo[n : n + 1]
        px[n, 41:42, side] = corner_hi[n : n + 1]
    for src in range(NB):
        ht[src * 32 : (src + 1) * 32, :] = unpack(phi_ref[src * BACK + 32 : src * BACK + 33, :])
    far = [unpack(flo_ref[r, 32:33, :]) for r in range(2)]
    near = [unpack(fhi_ref[r, 32:33, :]) for r in range(2)]
    for f in range(2):
        for l in range(LAYERS):
            n = f * LAYERS + l
            for xl in range(2):
                r = f * 16 + xl * 8 + l
                rows = slice(8 + xl * NB, 8 + (xl + 1) * NB)
                fx[n, rows, main] = phi_ref[pl.ds(r, NB, stride=BACK), :]
                fx[n, rows, side] = ht[pl.ds(r, NB, stride=32), :]
            a, b = f * 16 + 8 + l, f * 16 + l
            for r in range(2):
                fx[n, 6 + r : 7 + r, main] = flo_ref[r, a : a + 1, :]
                fx[n, 6 + r : 7 + r, side] = far[r][a : a + 1]
                fx[n, 40 + r : 41 + r, main] = fhi_ref[r, b : b + 1, :]
                fx[n, 40 + r : 41 + r, side] = near[r][b : b + 1]

    def at(ref, base, l, rows):
        if 0 <= l < LAYERS:
            return ref[base + l, rows, :]
        return jnp.zeros((rows.stop - rows.start, ref.shape[2]), F32)

    ring = slice(7, 41)
    for l in range(LAYERS):
        p = [px[c * LAYERS + l, ring, :] for c in range(3)]
        total = p[0] * p[0] + p[1] * p[1] + p[2] * p[2]
        alpha2 = 2.0 * px[24 + l, ring, :]
        phi = fx[l, ring, :]
        slope = (
            fx[l, 8:42, :] - fx[l, 6:40, :],
            shift(phi, -1) - shift(phi, 1),
            at(fx, 0, l + 1, ring) - at(fx, 0, l - 1, ring),
        )
        for c in range(3):
            n = c * LAYERS + l
            drive = drive_of(p[c], alpha2, total, landau[0, l], landau[1, l], landau[2, l])
            lap = (
                px[n, 8:42, :] + px[n, 6:40, :] + shift(p[c], -1) + shift(p[c], 1)
                + at(px, c * LAYERS, l + 1, ring) + at(px, c * LAYERS, l - 1, ring)
                - 6.0 * p[c]
            )
            qx[n, ring, :] = p[c] - DT * (drive - stiff[l] * lap + 0.5 * slope[c])
    own = slice(8, 40)
    for l in range(LAYERS):
        wide = [qx[c * LAYERS + l, own, :] for c in range(3)]
        p = [w[:, main] for w in wide]
        total = p[0] * p[0] + p[1] * p[1] + p[2] * p[2]
        alpha2 = 2.0 * al_ref[l]
        phi = fx[LAYERS + l, own, :]
        up, down = at(fx, LAYERS, l + 1, own), at(fx, LAYERS, l - 1, own)
        field = (
            -0.5 * (fx[LAYERS + l, 9:41, main] - fx[LAYERS + l, 7:39, main]),
            -0.5 * (shift(phi, -1) - shift(phi, 1))[:, main],
            -0.5 * (up[:, main] - down[:, main]),
        )
        for c in range(3):
            n = c * LAYERS + l
            drive = drive_of(p[c], alpha2, total, landau[0, l], landau[1, l], landau[2, l])
            lap = (
                qx[n, 9:41, main] + qx[n, 7:39, main]
                + (shift(wide[c], -1) + shift(wide[c], 1))[:, main]
                + at(qx, c * LAYERS, l + 1, own)[:, main] + at(qx, c * LAYERS, l - 1, own)[:, main]
                - 6.0 * p[c]
            )
            out_ref[c, l] = p[c] - DT * (drive - stiff[l] * lap - field[c])
            field_ref[c, l] = field[c]


VMEM = pl.BlockSpec(memory_space=pltpu.VMEM)
SMEM = pl.BlockSpec(memory_space=pltpu.SMEM)


def call(kernel, shapes, specs, scratch, name):
    many = isinstance(shapes, list)
    return pl.pallas_call(
        kernel,
        out_shape=[jax.ShapeDtypeStruct(s, F32) for s in shapes]
        if many
        else jax.ShapeDtypeStruct(shapes, F32),
        in_specs=specs,
        out_specs=[VMEM] * len(shapes) if many else VMEM,
        scratch_shapes=[pltpu.VMEM(s, F32) for s in scratch],
        compiler_params=PARAMS,
        name=name,
    )


def shards(tabs, polarization, alpha_field, landau, stiffness, permittivity, interfaces):
    count = lax.axis_size("bx")
    devices = count * NB
    ahead = [(i, (i + 1) % count) for i in range(count)]
    behind = [(i, (i - 1) % count) for i in range(count)]
    cells = jnp.concatenate([polarization.reshape(24, ROWS, LANES), alpha_field], axis=0)
    first = jnp.swapaxes(cells[:, 0:2, :], 0, 1)
    last = jnp.swapaxes(cells[:, ROWS - 2 :, :], 0, 1)
    low = lax.ppermute(last, "bx", ahead)
    high = lax.ppermute(first, "bx", behind)
    sent = call(
        charge_kernel, (NB * SLOT, LANES), [VMEM] * 6 + [SMEM] * 2,
        [(24, 48, LANES), (LAYERS, 48, LANES), (NB * 32, LANES)], "charge",
    )(polarization, alpha_field, low, high, first, last, landau, stiffness)
    lines = lax.all_to_all(sent.reshape(NB, SLOT, LANES), "by", 0, 0, tiled=True)
    modes = call(
        y_forward_kernel, (devices, LANES), [VMEM] * 6, [(256, 256), (256, 256)], "y_forward"
    )(lines.reshape(NB * SLOT, LANES), *tabs["fwd"], *tabs["fwd0"], tabs["tw"])
    modes = lax.all_to_all(modes.reshape(devices, 1, LANES), ("bx", "by"), 0, 0, tiled=True)
    modes = call(
        x_kernel, (devices, LANES), [VMEM] * 6 + [SMEM] * 2,
        [(2 * devices, LANES), (2 * devices, LANES)], "x_solve",
    )(
        modes.reshape(devices, LANES), *tabs["x"], *tabs["xt"], tabs["lam"], permittivity, interfaces
    )
    modes = lax.all_to_all(modes.reshape(devices, 1, LANES), ("bx", "by"), 0, 0, tiled=True)
    sent = call(
        y_inverse_kernel, (NB * BACK, LANES), [VMEM] * 6, [(256, 256)], "y_inverse"
    )(modes.reshape(devices, LANES), *tabs["inv"], *tabs["inv0"], tabs["tw"])
    phi = lax.all_to_all(sent.reshape(NB, BACK, LANES), "by", 0, 0, tiled=True)
    phi_low = lax.ppermute(phi[NB - 2 :], "bx", ahead)
    phi_high = lax.ppermute(phi[:2], "bx", behind)
    return call(
        update_kernel,
        [(3, LAYERS, ROWS, LANES)] * 2,
        [VMEM] * 8 + [SMEM] * 2,
        [(32, 48, 256), (16, 48, 256), (24, 48, 256), (NB * 32, LANES)],
        "update",
    )(
        polarization, alpha_field, low, high, lines, phi.reshape(NB * BACK, LANES),
        phi_low, phi_high, landau, stiffness,
    )


def solution(mesh):
    fwd, fwd0, inv, inv0, tw = tables_y()
    table, lam = tables_x(mesh.shape["bx"] * ROWS)
    tabs = {
        "fwd": split_table(fwd), "fwd0": split_table(fwd0),
        "inv": split_table(inv), "inv0": split_table(inv0),
        "tw": tw, "x": split_table(table), "xt": split_table(table.T), "lam": lam,
    }
    return jax.shard_map(
        functools.partial(shards, tabs),
        mesh=mesh,
        in_specs=(P(None, None, "bx", "by"), P(None, "bx", "by"), P(), P(), P(), P()),
        out_specs=(P(None, None, "bx", "by"), P(None, None, "bx", "by")),
        check_vma=False,
    )
```

time: 516 us -> 147 us (0.28); the launches traced: 509 us -> 146 us
  blocking collectives: 229 us -> 95.4 us
  waiting for transfers between devices: 106 us -> 12.1 us
  starting transfers between devices: 81.6 us -> 22.1 us
  matrix products: 29.3 us -> 0 us
  local copies, waits for them, and re-layouts: 31.8 us -> 3.02 us
  other arithmetic: 27.8 us -> 0.01 us
  Pallas kernels: 0 us -> 12.8 us
    all_to_all x10 -> x4, blocking collectives: 229 us -> 95.4 us  [the longest x2 66.7 us: shards(): lax.all_to_all(modes.reshape(devices, 1, LANES), ('bx', 'by'), 0, 0, tile...]
    all_to_all x6 -> x0, waiting for transfers between devices: 91.9 us -> none  [the longest x2 52.6 us: inverse(): lax.all_to_all(real_out, 'bx', split_axis=1, concat_axis=3, tiled=True)]
    all_to_all x6 -> x0, starting transfers between devices: 45.9 us -> none  [the longest x2 14.9 us: inverse(): lax.all_to_all(real_out, 'bx', split_axis=1, concat_axis=3, tiled=True)]
    dot_general x56 -> x0, matrix products: 29.3 us -> none  [the longest x12 7.03 us: mix(): jnp.einsum(form, imag_part, sin_table, precision=highest)]
    ppermute x8 -> x4, starting transfers between devices: 35.7 us -> 22.1 us  [the longest x1 14.7 us: shards(): high = lax.ppermute(first, 'bx', behind)]
    pallas_call x0 -> x5, Pallas kernels: none -> 12.8 us  [the longest x1 7.42 us: shards(): call(update_kernel, [(3, LAYERS, ROWS, LANES)] * 2, [VMEM] * 8 + [SMEM] *...]
    sub x6 -> x0, other arithmetic: 11.8 us -> none  [the longest x1 10.9 us: solve(): pivot_now = diagonal - interfaces[layer_no] * ratios[-1]]
    div x2 -> x0, other arithmetic: 7.66 us -> none  [solve(): primed = (source + interfaces[layer_no] * primes[-1]) / pivot_now]
  transfers between devices with their start and end apart: 14 -> 4, of which waited for: 10 -> 2; matrix products, arithmetic and copies ran while one was open for 3% -> 0% of each run, Pallas kernels for 0% -> 0%
where the time goes in v1:
time: 147 us; the launch traced here: 146 us
  blocking collectives  95.4 us (65%)
  starting transfers between devices  22.1 us (15%)
  Pallas kernels  12.8 us (9%)
  waiting for transfers between devices  12.1 us (8%)
  local copies, waits for them, and re-layouts  3.02 us (2%)
    all_to_all x2, blocking collectives, shards(): lax.all_to_all(modes.reshape(devices, 1, LANES), ('bx', 'by'), 0, 0, tile...  66.7 us
    all_to_all x1, blocking collectives, shards(): lax.all_to_all(sent.reshape(NB, SLOT, LANES), 'by', 0, 0, tiled=True)  17.7 us
    ppermute x1, starting transfers between devices, shards(): high = lax.ppermute(first, 'bx', behind)  14.7 us
    all_to_all x1, blocking collectives, shards(): phi = lax.all_to_all(sent.reshape(NB, BACK, LANES), 'by', 0, 0, tiled=True)  11 us
    pallas_call x1, Pallas kernels, shards(): call(update_kernel, [(3, LAYERS, ROWS, LANES)] * 2, [VMEM] * 8 + [SMEM] *...  7.42 us
    ppermute x1, waiting for transfers between devices, shards(): low = lax.ppermute(last, 'bx', ahead)  6.33 us
    ppermute x1, waiting for transfers between devices, shards(): phi_low = lax.ppermute(phi[NB - 2:], 'bx', ahead)  5.75 us
    unnamed x42, local copies, waits for them, and re-layouts  3.02 us
  transfers between devices with their start and end apart: 4, of which 2 were waited for; matrix products, arithmetic and copies ran while one was open for 0% of the time, Pallas kernels for 0%

profile of v1, /device:TPU:1, one launch (start us, length us, event | category | flops | bytes accessed | tf_op | source)
XLA Modules:
  0.0 146.3 jit_solution(7768360401426698134)
XLA Ops:
  0.6 1.0 copy.25
  1.6 0.0 copy-start.11
  1.6 0.0 copy-start.12
  1.6 0.0 copy-start.13
  1.7 1.3 copy.29
  3.0 0.0 copy-start.15
  3.0 14.7 %collective-permute-start.1 = (f32[2,32,128]{2,1,0:T(8,128)S(1)}, f32[2,32,128]{2,1,0:T(8,128)S(1)}, u32[]{:S(2)}, u32[]{:S(2)}) collective-permute-start(f32[2,32,128]{2,1,0:T(8,128)S(1)} %get-tuple-element.2.first_ref), channel_id=1, source_target_pairs={{0,496},{16,0},{32,16},{48,32},{64,48},{80,64},{96,80},{112,96},{1... | collective-permute-start | bytes 98312 | tf_op jit(solution)/shard_map/ppermute | solution.py:557
  17.7 1.9 %collective-permute-start = (f32[2,32,128]{2,1,0:T(8,128)S(1)}, f32[2,32,128]{2,1,0:T(8,128)S(1)}, u32[]{:S(2)}, u32[]{:S(2)}) collective-permute-start(f32[2,32,128]{2,1,0:T(8,128)S(1)} %get-tuple-element.3.last_ref), channel_id=1, source_target_pairs={{0,16},{16,32},{32,48},{48,64},{64,80},{80,96},{96,112},{112,128},... | collective-permute-start | bytes 98312 | tf_op jit(solution)/shard_map/ppermute | solution.py:556
  19.7 6.3 %collective-permute-done.lo_ref = f32[2,32,128]{2,1,0:T(8,128)S(1)} collective-permute-done((f32[2,32,128]{2,1,0:T(8,128)S(1)}, f32[2,32,128]{2,1,0:T(8,128)S(1)}, u32[]{:S(2)}, u32[]{:S(2)}) %collective-permute-start) | collective-permute-done | bytes 32800 | tf_op jit(solution)/shard_map/ppermute | solution.py:556
  26.0 0.0 copy-start.10
  26.0 0.0 copy-start.14
  26.1 0.0 copy-start.4
  26.1 0.0 copy-start.5
  26.1 1.6 %charge.1 = f32[1152,128]{1,0:T(8,128)S(1)} custom-call(f32[3,8,32,128]{3,2,1,0:T(8,128)S(1)} %copy-done, f32[8,32,128]{2,1,0:T(8,128)S(1)} %copy-done.1, f32[2,32,128]{2,1,0:T(8,128)S(1)} %collective-permute-done.lo_ref, f32[2,32,128]{2,1,0:T(8,128)S(1)} %collective-permute-done.1.hi_ref, f32[2,32,128]{2,1,0:T(8,128)S(1)} %get-tuple-element.2.first_ref, ...), custom_call_target="tpu_custom_call" | custom-call | tf_op jit(solution)/shard_map/charge/pallas_call | solution.py:558
  27.6 0.0 copy-start.3
  27.7 17.7 %all_to_all.20.e_ref = f32[16,72,128]{2,1,0:T(8,128)S(1)} all-to-all(f32[16,72,128]{2,1,0:T(8,128)S(1)} %bitcast.20), channel_id=1, replica_groups=mesh['bx'=32,'by'=16] {'by'}, dimensions={0} | all-to-all | bytes 1179648 | tf_op jit(solution)/shard_map/all_to_all | solution.py:562
  45.4 0.9 y_forward.1
  46.3 33.7 %all_to_all.21 = f32[512,1,128]{2,1,0:T(1,128)S(1)} all-to-all(f32[512,1,128]{2,1,0:T(1,128)S(1)} %bitcast.24), channel_id=1, replica_groups=mesh['bx'=32,'by'=16] {'bx','by'}, dimensions={0} | all-to-all | bytes 524288 | tf_op jit(solution)/shard_map/all_to_all | solution.py:566
  80.1 0.6 copy-done.18
  80.7 0.0 copy-done.19
  80.7 2.0 %x_solve.1 = f32[512,128]{1,0:T(8,128)S(1)} custom-call(f32[512,128]{1,0:T(8,128)S(1)} %bitcast.25, bf16[1024,512]{1,0:T(8,128)(2,1)S(1)} %copy-done.5, bf16[1024,512]{1,0:T(8,128)(2,1)S(1)} %copy-done.4, bf16[512,1024]{1,0:T(8,128)(2,1)S(1)} %copy-done.3, bf16[512,1024]{1,0:T(8,128)(2,1)S(1)} %copy-done.2, f32[8,1024]{1,0:T(8,128)S(1)} %copy-done.15, ...), custom_call_target="tpu_custom_call" | custom-call | tf_op jit(solution)/shard_map/x_solve/pallas_call | solution.py:567
  82.7 0.0 copy-start.6
  82.7 0.0 copy-start.7
  82.8 0.0 copy-start.8
  82.8 0.0 copy-start.9
  82.8 33.0 %all_to_all.22 = f32[512,1,128]{2,1,0:T(1,128)S(1)} all-to-all(f32[512,1,128]{2,1,0:T(1,128)S(1)} %bitcast.26), channel_id=1, replica_groups=mesh['bx'=32,'by'=16] {'bx','by'}, dimensions={0} | all-to-all | bytes 524288 | tf_op jit(solution)/shard_map/all_to_all | solution.py:573
  115.8 0.8 y_inverse.1
  116.6 11.0 %all_to_all.23 = f32[16,40,128]{2,1,0:T(8,128)S(1)} all-to-all(f32[16,40,128]{2,1,0:T(8,128)S(1)} %bitcast.22), channel_id=1, replica_groups=mesh['bx'=32,'by'=16] {'by'}, dimensions={0} | all-to-all | bytes 655360 | tf_op jit(solution)/shard_map/all_to_all | solution.py:577
  127.6 2.9 %collective-permute-start.3 = (f32[2,40,128]{2,1,0:T(8,128)S(1)}, f32[2,40,128]{2,1,0:T(8,128)S(1)}, u32[]{:S(2)}, u32[]{:S(2)}) collective-permute-start(f32[2,40,128]{2,1,0:T(8,128)S(1)} %get-tuple-element.4), channel_id=1, source_target_pairs={{0,496},{16,0},{32,16},{48,32},{64,48},{80,64},{96,80},{112,96},{1... | collective-permute-start | bytes 122888 | tf_op jit(solution)/shard_map/ppermute | solution.py:579
  130.5 2.6 %collective-permute-start.2 = (f32[2,40,128]{2,1,0:T(8,128)S(1)}, f32[2,40,128]{2,1,0:T(8,128)S(1)}, u32[]{:S(2)}, u32[]{:S(2)}) collective-permute-start(f32[2,40,128]{2,1,0:T(8,128)S(1)} %get-tuple-element.5), channel_id=1, source_target_pairs={{0,16},{16,32},{32,48},{48,64},{64,80},{80,96},{96,112},{112,128},... | collective-permute-start | bytes 122888 | tf_op jit(solution)/shard_map/ppermute | solution.py:578
  133.1 5.8 %collective-permute-done.2.flo_ref = f32[2,40,128]{2,1,0:T(8,128)S(1)} collective-permute-done((f32[2,40,128]{2,1,0:T(8,128)S(1)}, f32[2,40,128]{2,1,0:T(8,128)S(1)}, u32[]{:S(2)}, u32[]{:S(2)}) %collective-permute-start.2) | collective-permute-done | bytes 40992 | tf_op jit(solution)/shard_map/ppermute | solution.py:578
  138.9 7.4 %update.1 = (f32[3,8,32,128]{3,2,1,0:T(8,128)}, f32[3,8,32,128]{3,2,1,0:T(8,128)}) custom-call(f32[3,8,32,128]{3,2,1,0:T(8,128)S(1)} %copy-done, f32[8,32,128]{2,1,0:T(8,128)S(1)} %copy-done.1, f32[2,32,128]{2,1,0:T(8,128)S(1)} %collective-permute-done.lo_ref, f32[2,32,128]{2,1,0:T(8,128)S(1)} %collective-permute-done.1.hi_ref, ...), custom_call_target="tpu_custom_call" | custom-call | tf_op jit(solution)/shard_map/update/pallas_call | solution.py:580
  (29 shorter events, 0.1 us)
Async XLA Ops:
  1.6 43.8 %copy-start.11 = (bf16[256,256]{1,0:T(8,128)(2,1)S(1)}, bf16[256,256]{1,0:T(8,128)(2,1)}, u32[]{:S(2)}) copy-start(bf16[256,256]{1,0:T(8,128)(2,1)} %constant.30.clone.f0h) | copy-start | bytes 393220
  1.6 43.7 %copy-start.12 = (bf16[256,256]{1,0:T(8,128)(2,1)S(1)}, bf16[256,256]{1,0:T(8,128)(2,1)}, u32[]{:S(2)}) copy-start(bf16[256,256]{1,0:T(8,128)(2,1)} %constant.29.clone.fl) | copy-start | bytes 393220
  1.6 43.7 %copy-start.13 = (bf16[256,256]{1,0:T(8,128)(2,1)S(1)}, bf16[256,256]{1,0:T(8,128)(2,1)}, u32[]{:S(2)}) copy-start(bf16[256,256]{1,0:T(8,128)(2,1)} %constant.28.clone.fh) | copy-start | bytes 393220
  2.9 23.1 %copy-start = (f32[3,8,32,128]{3,2,1,0:T(8,128)S(1)}, f32[3,8,32,128]{3,2,1,0:T(8,128)}, u32[]{:S(2)}) copy-start(f32[3,8,32,128]{3,2,1,0:T(8,128)} %p_ref.3) | copy-start | bytes 1179652
  3.0 23.1 %copy-start.1 = (f32[8,32,128]{2,1,0:T(8,128)S(1)}, f32[8,32,128]{2,1,0:T(8,128)}, u32[]{:S(2)}) copy-start(f32[8,32,128]{2,1,0:T(8,128)} %al_ref.3) | copy-start | bytes 393220
  3.0 77.1 %copy-start.15 = (f32[8,1024]{1,0:T(8,128)S(1)}, f32[8,1024]{1,0:T(8,128)}, u32[]{:S(2)}) copy-start(f32[8,1024]{1,0:T(8,128)} %constant.37.clone.lam) | copy-start | bytes 98308
  3.0 23.0 %copy-start.16 = (f32[3,8]{1,0:T(4,128)S(1)}, f32[3,8]{1,0:T(4,128)}, u32[]{:S(2)}) copy-start(f32[3,8]{1,0:T(4,128)} %landau.3) | copy-start | bytes 292
  3.0 23.0 %copy-start.17 = (f32[8]{0:T(128)S(1)}, f32[8]{0:T(128)}, u32[]{:S(2)}) copy-start(f32[8]{0:T(128)} %stiff.3) | copy-start | bytes 100
  3.0 16.7 %collective-permute-start.1 = (f32[2,32,128]{2,1,0:T(8,128)S(1)}, f32[2,32,128]{2,1,0:T(8,128)S(1)}, u32[]{:S(2)}, u32[]{:S(2)}) collective-permute-start(f32[2,32,128]{2,1,0:T(8,128)S(1)} %get-tuple-element.2.first_ref), channel_id=1, source_target_pairs={{0,496},{16,0},{32,16},{48,32},{64,48},{80,64},{96,80},{112,96},{1... | collective-permute-start | bytes 98312 | tf_op jit(solution)/shard_map/ppermute | solution.py:557
  17.7 8.3 %collective-permute-start = (f32[2,32,128]{2,1,0:T(8,128)S(1)}, f32[2,32,128]{2,1,0:T(8,128)S(1)}, u32[]{:S(2)}, u32[]{:S(2)}) collective-permute-start(f32[2,32,128]{2,1,0:T(8,128)S(1)} %get-tuple-element.3.last_ref), channel_id=1, source_target_pairs={{0,16},{16,32},{32,48},{48,64},{64,80},{80,96},{96,112},{112,128},... | collective-permute-start | bytes 98312 | tf_op jit(solution)/shard_map/ppermute | solution.py:556
  26.0 19.3 %copy-start.10 = (bf16[256,256]{1,0:T(8,128)(2,1)S(1)}, bf16[256,256]{1,0:T(8,128)(2,1)}, u32[]{:S(2)}) copy-start(bf16[256,256]{1,0:T(8,128)(2,1)} %constant.31.clone.f0l) | copy-start | bytes 393220
  26.0 19.3 %copy-start.14 = (f32[16,128]{1,0:T(8,128)S(1)}, f32[16,128]{1,0:T(8,128)}, u32[]{:S(2)}) copy-start(f32[16,128]{1,0:T(8,128)} %constant.32.clone.tw) | copy-start | bytes 24580
  26.1 54.0 %copy-start.4 = (bf16[1024,512]{1,0:T(8,128)(2,1)S(1)}, bf16[1024,512]{1,0:T(8,128)(2,1)}, u32[]{:S(2)}) copy-start(bf16[1024,512]{1,0:T(8,128)(2,1)} %constant.34.clone.tl) | copy-start | bytes 3145732
  26.1 54.0 %copy-start.5 = (bf16[1024,512]{1,0:T(8,128)(2,1)S(1)}, bf16[1024,512]{1,0:T(8,128)(2,1)}, u32[]{:S(2)}) copy-start(bf16[1024,512]{1,0:T(8,128)(2,1)} %constant.33.clone.th) | copy-start | bytes 3145732
  27.6 52.4 %copy-start.3 = (bf16[512,1024]{1,0:T(8,128)(2,1)S(1)}, bf16[512,1024]{1,0:T(8,128)(2,1)}, u32[]{:S(2)}) copy-start(bf16[512,1024]{1,0:T(8,128)(2,1)} %constant.35.clone.uh) | copy-start | bytes 3145732
  45.4 34.7 %copy-start.2 = (bf16[512,1024]{1,0:T(8,128)(2,1)S(1)}, bf16[512,1024]{1,0:T(8,128)(2,1)}, u32[]{:S(2)}) copy-start(bf16[512,1024]{1,0:T(8,128)(2,1)} %constant.36.clone.ul) | copy-start | bytes 3145732
  80.0 0.7 copy-start.18
  80.0 0.7 copy-start.19
  82.7 33.0 %copy-start.6 = (bf16[256,256]{1,0:T(8,128)(2,1)S(1)}, bf16[256,256]{1,0:T(8,128)(2,1)}, u32[]{:S(2)}) copy-start(bf16[256,256]{1,0:T(8,128)(2,1)} %constant.41.clone.g0l) | copy-start | bytes 393220
  82.7 33.0 %copy-start.7 = (bf16[256,256]{1,0:T(8,128)(2,1)S(1)}, bf16[256,256]{1,0:T(8,128)(2,1)}, u32[]{:S(2)}) copy-start(bf16[256,256]{1,0:T(8,128)(2,1)} %constant.40.clone.g0h) | copy-start | bytes 393220
  82.8 33.0 %copy-start.8 = (bf16[256,256]{1,0:T(8,128)(2,1)S(1)}, bf16[256,256]{1,0:T(8,128)(2,1)}, u32[]{:S(2)}) copy-start(bf16[256,256]{1,0:T(8,128)(2,1)} %constant.39.clone.gl) | copy-start | bytes 393220
  82.8 33.0 %copy-start.9 = (bf16[256,256]{1,0:T(8,128)(2,1)S(1)}, bf16[256,256]{1,0:T(8,128)(2,1)}, u32[]{:S(2)}) copy-start(bf16[256,256]{1,0:T(8,128)(2,1)} %constant.38.clone.gh) | copy-start | bytes 393220
  127.6 5.5 %collective-permute-start.3 = (f32[2,40,128]{2,1,0:T(8,128)S(1)}, f32[2,40,128]{2,1,0:T(8,128)S(1)}, u32[]{:S(2)}, u32[]{:S(2)}) collective-permute-start(f32[2,40,128]{2,1,0:T(8,128)S(1)} %get-tuple-element.4), channel_id=1, source_target_pairs={{0,496},{16,0},{32,16},{48,32},{64,48},{80,64},{96,80},{112,96},{1... | collective-permute-start | bytes 122888 | tf_op jit(solution)/shard_map/ppermute | solution.py:579
  130.5 8.4 %collective-permute-start.2 = (f32[2,40,128]{2,1,0:T(8,128)S(1)}, f32[2,40,128]{2,1,0:T(8,128)S(1)}, u32[]{:S(2)}, u32[]{:S(2)}) collective-permute-start(f32[2,40,128]{2,1,0:T(8,128)S(1)} %get-tuple-element.5), channel_id=1, source_target_pairs={{0,16},{16,32},{32,48},{48,64},{64,80},{80,96},{96,112},{112,128},... | collective-permute-start | bytes 122888 | tf_op jit(solution)/shard_map/ppermute | solution.py:578

commit v2 on v1

v2 whole, which is shorter than its diff:
```python
import functools

import jax
import jax.numpy as jnp
import ml_dtypes
import numpy as np
from jax import lax
from jax.experimental import pallas as pl
from jax.experimental.pallas import tpu as pltpu
from jax.sharding import PartitionSpec as P

DT = 0.05
NB = 16
LANES = 128
ROWS = 32
LAYERS = 8
SLOT = 40
SHIFT = 2
F32 = jnp.float32
BF16 = jnp.bfloat16
PARAMS = pltpu.CompilerParams(vmem_limit_bytes=16 * 1024 * 1024)


def split_table(table):
    high = table.astype(ml_dtypes.bfloat16)
    low = (table - high.astype(np.float64)).astype(ml_dtypes.bfloat16)
    return high, low


def tables_y():
    n = NB * LANES
    t = np.arange(LANES)
    k = np.arange(LANES)
    ang = 2 * np.pi * np.outer(k, t) / LANES
    c, s = np.cos(ang), np.sin(ang)
    fwd = np.block([[c, s], [-s, c]])
    inv = np.block([[c.T, -s.T], [s.T, c.T]]) * (2.0 / n)
    fwd0 = np.zeros((256, 256))
    inv0 = np.zeros((256, 256))
    for i in range(LANES):
        m = i if i <= 64 else i - 64
        wave = np.cos(2 * np.pi * m * t / LANES) if i <= 64 else np.sin(2 * np.pi * m * t / LANES)
        fwd0[i, :LANES] = wave
        inv0[:LANES, i] = wave * ((1.0 if i in (0, 64) else 2.0) / n)
    for i in range(64):
        th = 2 * np.pi * (8 + 16 * i) * t / n
        fwd0[128 + i, LANES:] = np.cos(th)
        fwd0[192 + i, LANES:] = -np.sin(th)
        inv0[LANES:, 128 + i] = np.cos(th) * (2.0 / n)
        inv0[LANES:, 192 + i] = -np.sin(th) * (2.0 / n)
    tw = np.zeros((16, LANES), np.float32)
    for j in range(8):
        tw[j] = np.cos(2 * np.pi * j * t / n)
        tw[8 + j] = np.sin(2 * np.pi * j * t / n)
    return fwd, fwd0, inv, inv0, tw


def tables_x(nx, offset):
    half = nx // 2
    pos = np.array(
        [
            bx * ROWS + xl * NB + by + offset
            for xl in range(2)
            for bx in range(half // ROWS)
            for by in range(NB)
        ]
    )
    even, odd = list(range(0, half + 1, 2)), list(range(1, half, 2))
    kinds = [(k, 0) for k in even] + [(k, 1) for k in even[1:-1]] + [(k, 0) for k in odd] + [(k, 1) for k in odd]
    scale = np.sqrt(2.0 / nx)
    rows = []
    for k, kind in kinds:
        wave = (np.sin if kind else np.cos)(2 * np.pi * (k * pos % nx) / nx)
        rows.append(wave * (np.sqrt(1.0 / nx) if k in (0, half) else scale))
    freq = np.array([k for k, _ in kinds])
    lam = np.zeros((8, nx), np.float32)
    lam[0] = 4 * np.sin(np.pi * freq / nx) ** 2
    lam[1] = np.sin(2 * np.pi * freq / nx) ** 2
    return np.stack(rows), lam


def split(value):
    high = value.astype(BF16)
    return high, (value - high.astype(F32)).astype(BF16)


def dot(a, b):
    return lax.dot_general(a, b, (((1,), (0,)), ((), ())), preferred_element_type=F32)


def dot_t(a, b):
    return lax.dot_general(a, b, (((1,), (1,)), ((), ())), preferred_element_type=F32)


def shift(value, by):
    n = value.shape[1]
    return pltpu.roll(value, by % n, axis=1)


def pack(tile):
    lane = lax.broadcasted_iota(jnp.int32, tile.shape, 1)
    edge = jnp.where((lane < 2) | (lane >= 126), tile, 0.0)
    return jnp.sum(pltpu.roll(edge, 0, axis=1, stride=4, stride_axis=0), axis=0, keepdims=True)


def unpack(row):
    value = jnp.broadcast_to(row, (8, LANES))
    index = lax.broadcasted_iota(jnp.int32, (8, LANES), 0)
    for bit in (1, 2, 4):
        value = jnp.where(index // bit % 2 == 1, pltpu.roll(value, LANES - 4 * bit, axis=1), value)
    return jnp.concatenate(
        [value] + [pltpu.roll(value, LANES - 32 * t, axis=1) for t in range(1, 4)], axis=0
    )


def drive_of(value, alpha2, total, quartic, mixed, sextic):
    sq = value * value
    return value * (alpha2 + quartic * sq + mixed * (total - sq) + sextic * (sq * sq))


def coefficient(par, kind, l, width=LANES):
    return par[kind * LAYERS + l : kind * LAYERS + l + 1, 0:width]


def border_kernel(p_ref, al_ref, last_ref, first_ref, buf, sems):
    copies = [
        pltpu.make_async_copy(src.at[:, rows, :], buf.at[k, cells], sems.at[2 * k + m])
        for k, rows in enumerate((pl.ds(ROWS - 8, 8), pl.ds(0, 8)))
        for m, (src, cells) in enumerate(((p_ref, pl.ds(0, 24)), (al_ref, pl.ds(24, 8))))
    ]
    for copy in copies:
        copy.start()
    for copy in copies:
        copy.wait()
    for n in range(32):
        for r in range(4):
            last_ref[r * 32 + n : r * 32 + n + 1, :] = buf[0, n, 4 + r : 5 + r, :]
        for r in range(2):
            first_ref[r * 32 + n : r * 32 + n + 1, :] = buf[1, n, r : r + 1, :]


def charge_kernel(p_ref, al_ref, lo_ref, par, out_ref, px, nx, ws, eb):
    lane = lax.broadcasted_iota(jnp.int32, (ROWS, LANES), 1)
    for n in range(24):
        px[n * 40 + 8 : n * 40 + 40, :] = p_ref[n * ROWS : (n + 1) * ROWS, :]
    for l in range(LAYERS):
        px[(24 + l) * 40 + 8 : (24 + l) * 40 + 40, :] = al_ref[l * ROWS : (l + 1) * ROWS, :]
    for r in range(4):
        px[pl.ds(4 + r, 32, stride=40), :] = lo_ref[r * 32 : (r + 1) * 32, :]

    def at(ref, c, l, low, high):
        if 0 <= l < LAYERS:
            n = c * LAYERS + l
            return ref[n * 40 + low : n * 40 + high, :]
        return jnp.zeros((high - low, LANES), F32)

    for l in range(LAYERS):
        p = [at(px, c, l, 5, 39) for c in range(3)]
        total = p[0] * p[0] + p[1] * p[1] + p[2] * p[2]
        alpha2 = 2.0 * at(px, 3, l, 5, 39)
        e = coefficient(par, 3, l)
        landau = [coefficient(par, k, l) for k in range(3)]
        for c in range(3):
            drive = drive_of(p[c], alpha2, total, *landau)
            lap = (
                at(px, c, l, 6, 40) + at(px, c, l, 4, 38)
                + at(px, c, l + 1, 5, 39) + at(px, c, l - 1, 5, 39)
                - 6.0 * p[c]
            )
            n = c * LAYERS + l
            nx[n * 40 + 5 : n * 40 + 39, :] = p[c] - DT * drive + e * lap
    for l in range(LAYERS):
        e = coefficient(par, 3, l)
        dx = -0.5 * (at(px, 0, l, 7, 39) - at(px, 0, l, 5, 37))
        above, below = at(px, 2, l + 1, 6, 38), at(px, 2, l - 1, 6, 38)
        p1, n1 = at(px, 1, l, 6, 38), at(nx, 1, l, 6, 38)
        fwd, bwd = shift(p1, -1), shift(p1, 1)
        one = dx - 0.5 * (above - below) - 0.5 * (fwd - bwd)
        wrap_one = jnp.where(lane == LANES - 1, -0.5 * fwd, jnp.where(lane == 0, 0.5 * bwd, 0.0))
        e_up = coefficient(par, 3, l + 1) if l + 1 < LAYERS else 0.0
        e_dn = coefficient(par, 3, l - 1) if l > 0 else 0.0
        ue = e * dx - 0.5 * (e_up * above - e_dn * below)
        un = -0.5 * (at(nx, 0, l, 7, 39) - at(nx, 0, l, 5, 37)) - 0.5 * (
            at(nx, 2, l + 1, 6, 38) - at(nx, 2, l - 1, 6, 38)
        )
        a = shift(ue - 0.5 * n1, -1)
        b = shift(ue + 0.5 * n1, 1)
        h = (0.5 * e) * p1
        c2, d2 = shift(h, -2), shift(h, 2)
        two = un + a + b - c2 + d2
        wrap_two = (
            jnp.where(lane == LANES - 1, a, 0.0)
            + jnp.where(lane == 0, b, 0.0)
            + jnp.where(lane >= LANES - 2, -c2, 0.0)
            + jnp.where(lane < 2, d2, 0.0)
        )
        for f, (whole, wrap) in enumerate(((one, wrap_one), (two, wrap_two))):
            main = whole - wrap
            for xl in range(2):
                r = f * 16 + xl * 8 + l
                out_ref[pl.ds(r, NB, stride=SLOT), :] = main[xl * NB : (xl + 1) * NB]
                ws[pl.ds(r, NB, stride=32), :] = wrap[xl * NB : (xl + 1) * NB]
    for n in range(32):
        eb[n : n + 1, :] = pack(px[n * 40 + 8 : n * 40 + 40, :])
    eb[32:33, :] = pack(lo_ref[96:128, :])
    eb[33:48, :] = jnp.zeros((15, LANES), F32)
    blank = jnp.zeros((4, LANES), F32)
    for b in range(NB):
        out_ref[b * SLOT + 32 : (b + 1) * SLOT, :] = jnp.concatenate(
            [pack(ws[b * 32 : (b + 1) * 32, :]), eb[3 * b : 3 * b + 3, :], blank], axis=0
        )


def y_forward_kernel(in_ref, fh, fl, f0h, f0l, tw, hi_ref, out_ref, corner_ref, d_ref, o_ref):
    corner_ref[...] = jnp.concatenate([pack(hi_ref[0:32, :]), jnp.zeros((7, LANES), F32)], axis=0)
    lane1 = lax.broadcasted_iota(jnp.int32, (1, LANES), 1)
    lane = lax.broadcasted_iota(jnp.int32, (ROWS, LANES), 1)
    g = []
    for b in range(NB):
        before = in_ref[((b - 1) % NB) * SLOT + 32 : ((b - 1) % NB) * SLOT + 33, :]
        after = in_ref[((b + 1) % NB) * SLOT + 32 : ((b + 1) % NB) * SLOT + 33, :]
        extra = unpack(jnp.where(lane1 % 4 < 2, before, after))
        g.append(
            in_ref[b * SLOT : b * SLOT + 32, :]
            + jnp.where((lane < 2) | (lane >= 126), extra, 0.0)
        )
    plus = {b: g[b] + g[NB - b] for b in range(1, 8)}
    minus = {b: g[b] - g[NB - b] for b in range(1, 8)}
    re, im = {}, {}
    for k in range(5):
        even = g[0] + g[8] if k % 2 == 0 else g[0] - g[8]
        odd = jnp.zeros_like(even)
        s_even, s_odd = jnp.zeros_like(even), jnp.zeros_like(even)
        for b in range(1, 8):
            c, s = np.cos(2 * np.pi * b * k / 16), np.sin(2 * np.pi * b * k / 16)
            tc = plus[b] * float(c) if abs(c) > 1e-9 else None
            ts = minus[b] * float(s) if abs(s) > 1e-9 else None
            if b % 2 == 0:
                even = even + tc if tc is not None else even
                s_even = s_even + ts if ts is not None else s_even
            else:
                odd = odd + tc if tc is not None else odd
                s_odd = s_odd + ts if ts is not None else s_odd
        re[k], re[8 - k] = even + odd, even - odd
        im[k], im[8 - k] = -(s_even + s_odd), s_even - s_odd
    d_ref[0:32, 0:LANES] = re[0]
    d_ref[0:32, LANES:256] = re[8]
    for j in range(1, 8):
        c, s = tw[j : j + 1, :], tw[8 + j : 9 + j, :]
        d_ref[j * 32 : (j + 1) * 32, 0:LANES] = re[j] * c + im[j] * s
        d_ref[j * 32 : (j + 1) * 32, LANES:256] = im[j] * c - re[j] * s
    dh, dl = split(d_ref[...])
    o_ref[...] = dot_t(fh[...], dh) + dot_t(fh[...], dl) + dot_t(fl[...], dh)
    zero = dot_t(f0h[...], dh[0:128]) + dot_t(f0h[...], dl[0:128]) + dot_t(f0l[...], dh[0:128])
    wide = lax.broadcasted_iota(jnp.int32, (256, LANES), 1)
    o_ref[:, 0:LANES] = jnp.where(wide < 32, zero, o_ref[:, 0:LANES])
    lane64 = lax.broadcasted_iota(jnp.int32, (64, LANES), 1)
    for j in range(8):
        t, at = j // 4, j % 4
        value = None
        for q in range(4):
            piece = o_ref[q * 64 : (q + 1) * 64, t * LANES : (t + 1) * LANES]
            if q != at:
                piece = shift(piece, (q - at) * 32)
            value = piece if value is None else jnp.where(lane64 // 32 == q, piece, value)
        out_ref[j * 64 : (j + 1) * 64, :] = value


def x_kernel(in_ref, th, tl, uh, ul, lam, par, out_ref, zs, ys):
    n = in_ref.shape[0]
    half = n // 2
    top, low = in_ref[0:half, :], in_ref[half:n, :]
    for part, value in enumerate((top + low, top - low)):
        high, rest = split(value)
        both = jnp.concatenate([high, rest], axis=1)
        for chunk in range(n // 256):
            r0 = part * n + chunk * 256
            acc = []
            for xl in range(2):
                cols = slice(xl * half, (xl + 1) * half)
                wide = dot(th[r0 : r0 + 256, cols], both)
                acc.append(
                    wide[:, 0:LANES] + wide[:, LANES:256] + dot(tl[r0 : r0 + 256, cols], high)
                )
            turned = jnp.transpose(acc[0] + shift(acc[1], -8))
            zs[r0 : r0 + LANES, :] = turned[:, 0:LANES]
            zs[r0 + LANES : r0 + 256, :] = turned[:, LANES:256]
    dev = lax.axis_index("bx") * NB + lax.axis_index("by")
    j = dev // 64
    q = lax.broadcasted_iota(jnp.int32, (8, 1), 0) // 2
    s = q * 64 + dev % 64
    ky_j = j + 16 * (s % 128)
    ky_0 = jnp.where(s < 128, 16 * jnp.where(s <= 64, s, s - 64), 8 + 16 * (s % 64))
    ky = jnp.where(j == 0, ky_0, ky_j)
    full = NB * LANES
    ky = jnp.minimum(ky, full - ky).astype(F32)
    ky = jnp.broadcast_to(ky, (8, LANES))
    sin_half = jnp.sin(ky * (np.pi / full))
    lam_y = 4.0 * sin_half * sin_half
    sin_y = jnp.sin(jnp.minimum(ky, full // 2 - ky) * (2.0 * np.pi / full))
    slope_y = sin_y * sin_y
    second = lax.broadcasted_iota(jnp.int32, (8, LANES), 0) % 2 == 1
    eps = [coefficient(par, 4, l) for l in range(LAYERS)]
    iface = [coefficient(par, 5, l) for l in range(LAYERS + 1)]
    for chunk in range(2 * n // LANES):
        cols = slice(chunk * LANES, (chunk + 1) * LANES)
        lateral = lam_y + lam[0:1, cols]
        slope = slope_y + lam[1:2, cols]
        inverse, ratio = [], []
        for l in range(LAYERS):
            pivot = eps[l] * lateral + (iface[l] + iface[l + 1])
            if l > 0:
                pivot = pivot - iface[l] * ratio[-1]
            inverse.append(1.0 / pivot)
            ratio.append(iface[l + 1] * inverse[-1])

        def solve(source):
            prime = []
            for l in range(LAYERS):
                value = source[l] + iface[l] * prime[-1] if l > 0 else source[l]
                prime.append(value * inverse[l])
            for l in range(LAYERS - 2, -1, -1):
                prime[l] = prime[l] + ratio[l] * prime[l + 1]
            return prime

        phi = solve([zs[pl.ds(chunk * LANES + l, 8, stride=16), :] for l in range(LAYERS)])
        first = [jnp.where(second, pltpu.roll(v, 1, axis=0), 0.0) for v in phi]
        zero = jnp.zeros_like(first[0])

        def dz(v):
            return [
                0.5 * ((v[l + 1] if l + 1 < LAYERS else zero) - (v[l - 1] if l > 0 else zero))
                for l in range(LAYERS)
            ]

        twice = dz(dz(first))
        more = solve([DT * (twice[l] - slope * first[l]) for l in range(LAYERS)])
        for l in range(LAYERS):
            value = phi[l] + more[l]
            ys[pl.ds(chunk * LANES + l, 8, stride=16), :] = value
            ys[pl.ds(chunk * LANES + 8 + l, 8, stride=16), :] = value
    lane = lax.broadcasted_iota(jnp.int32, (half, LANES), 1)
    odd_row = lane // 8 % 2 == 1
    pair = []
    for part in range(2):
        cols = slice(part * n, (part + 1) * n)
        high, rest = split(
            jnp.concatenate([ys[r : r + LANES, :] for r in range(part * n, (part + 1) * n, LANES)], axis=1)
        )
        both = jnp.concatenate([high, rest], axis=0)
        acc = []
        for xl in range(2):
            rows = slice(xl * half, (xl + 1) * half)
            wide = dot_t(uh[rows, cols], both)
            acc.append(wide[:, 0:LANES] + wide[:, LANES:256] + dot_t(ul[rows, cols], high))
        pair.append(jnp.where(odd_row, acc[1], acc[0]))
    out_ref[0:half, :] = pair[0] + pair[1]
    out_ref[half:n, :] = pair[0] - pair[1]


def y_inverse_kernel(in_ref, gh, gl, g0h, g0l, tw, lines, corner_ref, out_ref, o_ref):
    lane64 = lax.broadcasted_iota(jnp.int32, (64, LANES), 1)
    for t in range(2):
        for q in range(4):
            value = None
            for at in range(4):
                j = t * 4 + at
                piece = in_ref[j * 64 : (j + 1) * 64, :]
                if q != at:
                    piece = shift(piece, (at - q) * 32)
                value = piece if value is None else jnp.where(lane64 // 32 == at, piece, value)
            o_ref[q * 64 : (q + 1) * 64, t * LANES : (t + 1) * LANES] = value
    oh, ol = split(o_ref[...])
    o_ref[...] = dot(gh[...], oh) + dot(gh[...], ol) + dot(gl[...], oh)
    zero = (
        dot(g0h[...], oh[:, 0:LANES]) + dot(g0h[...], ol[:, 0:LANES]) + dot(g0l[...], oh[:, 0:LANES])
    )
    wide = lax.broadcasted_iota(jnp.int32, (256, LANES), 1)
    o_ref[:, 0:LANES] = jnp.where(wide < 32, zero, o_ref[:, 0:LANES])
    g = jnp.transpose(o_ref[...])
    hr, hi = {}, {}
    for j in range(1, 8):
        c, s = tw[j : j + 1, :], tw[8 + j : 9 + j, :]
        a, b = g[j * 32 : (j + 1) * 32, 0:LANES], g[j * 32 : (j + 1) * 32, LANES:256]
        hr[j] = a * c - b * s
        hi[j] = a * s + b * c
    g0, g8 = g[0:32, 0:LANES], g[0:32, LANES:256]
    out = {}
    for b in range(5):
        even = g0 + g8 if b % 2 == 0 else g0 - g8
        odd = jnp.zeros_like(even)
        s_even, s_odd = jnp.zeros_like(even), jnp.zeros_like(even)
        for j in range(1, 8):
            c, s = np.cos(2 * np.pi * b * j / 16), np.sin(2 * np.pi * b * j / 16)
            tc = hr[j] * float(c) if abs(c) > 1e-9 else None
            ts = hi[j] * float(s) if abs(s) > 1e-9 else None
            if j % 2 == 0:
                even = even + tc if tc is not None else even
                s_even = s_even + ts if ts is not None else s_even
            else:
                odd = odd + tc if tc is not None else odd
                s_odd = s_odd + ts if ts is not None else s_odd
        cos_b, sin_b = even + odd, s_even + s_odd
        cos_c, sin_c = even - odd, s_odd - s_even
        out[b] = cos_b - sin_b
        out[(NB - b) % NB] = cos_b + sin_b
        out[8 - b] = cos_c - sin_c
        out[8 + b] = cos_c + sin_c
    lane = lax.broadcasted_iota(jnp.int32, (ROWS, LANES), 1)
    tail = corner_ref[0:4, :]
    from_right = lax.broadcasted_iota(jnp.int32, (3, LANES), 1) % 4 < 2
    for b in range(NB):
        after, before = (b + 1) % NB, (b - 1) % NB
        out_ref[b * SLOT : b * SLOT + 32, :] = out[b]
        border = jnp.where(lane < 2, out[after], out[before])
        edge = jnp.where(
            from_right,
            lines[after * SLOT + 33 : after * SLOT + 36, :],
            lines[before * SLOT + 33 : before * SLOT + 36, :],
        )
        out_ref[b * SLOT + 32 : (b + 1) * SLOT, :] = jnp.concatenate([pack(border), edge, tail], axis=0)


def wide(main, side, n, low, high):
    if n is None:
        return jnp.zeros((high - low, 2 * LANES), F32)
    rows = slice(n * 48 + low, n * 48 + high)
    return jnp.concatenate([main[rows, :], side[rows, :]], axis=1)


def near(base, l):
    return base + l if 0 <= l < LAYERS else None


def star_kernel(p_ref, al_ref, lo_ref, hi_ref, phi_ref, par, qm, qs, pm, ps):
    from_right = lax.broadcasted_iota(jnp.int32, (1, LANES), 1) % 4 < 2
    by = lax.axis_index("by")
    left, right = (by + NB - 1) % NB, (by + 1) % NB
    corner_lo = unpack(phi_ref[32 // 3, 33 + 32 % 3 : 34 + 32 % 3, :])
    corner_hi = unpack(jnp.where(from_right, phi_ref[right, 36:37, :], phi_ref[left, 36:37, :]))
    for n in range(32):
        ref, m = (p_ref, n) if n < 24 else (al_ref, n - 24)
        pm[n * 48 + 8 : n * 48 + 40, :] = ref[m * ROWS : (m + 1) * ROWS, :]
        ps[n * 48 + 8 : n * 48 + 40, :] = unpack(phi_ref[n // 3, 33 + n % 3 : 34 + n % 3, :])
    for row, value, corner in (
        (6, lo_ref[64:96, :], corner_lo),
        (7, lo_ref[96:128, :], corner_lo),
        (40, hi_ref[0:32, :], corner_hi),
        (41, hi_ref[32:64, :], corner_hi),
    ):
        pm[pl.ds(row, 32, stride=48), :] = value
        ps[pl.ds(row, 32, stride=48), :] = corner
    for l in range(LAYERS):
        p = [wide(pm, ps, c * LAYERS + l, 7, 41) for c in range(3)]
        total = p[0] * p[0] + p[1] * p[1] + p[2] * p[2]
        alpha2 = 2.0 * wide(pm, ps, 24 + l, 7, 41)
        e = coefficient(par, 3, l, 2 * LANES)
        landau = [coefficient(par, k, l, 2 * LANES) for k in range(3)]
        for c in range(3):
            n = c * LAYERS + l
            drive = drive_of(p[c], alpha2, total, *landau)
            lap = (
                wide(pm, ps, n, 8, 42) + wide(pm, ps, n, 6, 40) + shift(p[c], -1) + shift(p[c], 1)
                + wide(pm, ps, near(c * LAYERS, l + 1), 7, 41)
                + wide(pm, ps, near(c * LAYERS, l - 1), 7, 41)
                - 6.0 * p[c]
            )
            value = p[c] - DT * drive + e * lap
            qm[n * 48 + 7 : n * 48 + 41, :] = value[:, 0:LANES]
            qs[n * 48 + 7 : n * 48 + 41, :] = value[:, LANES : 2 * LANES]


def update_kernel(al_ref, qm, qs, phi_ref, far_ref, par, out_ref, field_ref, fm, fs, rm, rs, ht):
    for src in range(NB):
        ht[src * 32 : (src + 1) * 32, :] = unpack(phi_ref[src * SLOT + 32 : src * SLOT + 33, :])
    for f in range(2):
        for l in range(LAYERS):
            for xl in range(2):
                r = f * 16 + xl * 8 + l
                row = (f * LAYERS + l) * 48 + 8 + SHIFT + xl * NB
                fm[row : row + NB, :] = phi_ref[pl.ds(r, NB, stride=SLOT), :]
                fs[row : row + NB, :] = ht[pl.ds(r, NB, stride=32), :]
    for k in range(4):
        side = unpack(far_ref[k * SLOT + 32 : k * SLOT + 33, :])
        for f in range(2):
            rows = pl.ds(f * LAYERS * 48 + 6 + k, LAYERS, stride=48)
            fm[rows, :] = far_ref[k * SLOT + f * 16 + 8 : k * SLOT + f * 16 + 16, :]
            fs[rows, :] = side[f * 16 + 8 : f * 16 + 16]
    for l in range(LAYERS):
        phi = wide(fm, fs, l, 7, 41)
        slope = (
            wide(fm, fs, l, 8, 42) - wide(fm, fs, l, 6, 40),
            shift(phi, -1) - shift(phi, 1),
            wide(fm, fs, near(0, l + 1), 7, 41) - wide(fm, fs, near(0, l - 1), 7, 41),
        )
        for c in range(3):
            rows = slice((c * LAYERS + l) * 48 + 7, (c * LAYERS + l) * 48 + 41)
            rm[rows, :] = qm[rows, :] - (0.5 * DT) * slope[c][:, 0:LANES]
            rs[rows, :] = qs[rows, :] - (0.5 * DT) * slope[c][:, LANES : 2 * LANES]

    def at(ref, base, l, low, high):
        if 0 <= l < LAYERS:
            return ref[(base + l) * 48 + low : (base + l) * 48 + high, :]
        return jnp.zeros((high - low, LANES), F32)

    for l in range(LAYERS):
        p = [at(rm, c * LAYERS, l, 8, 40) for c in range(3)]
        total = p[0] * p[0] + p[1] * p[1] + p[2] * p[2]
        alpha2 = 2.0 * al_ref[l * ROWS : (l + 1) * ROWS, :]
        e = coefficient(par, 3, l)
        landau = [coefficient(par, k, l) for k in range(3)]
        phi = wide(fm, fs, LAYERS + l, 8, 40)
        field = (
            -0.5 * (at(fm, LAYERS, l, 9, 41) - at(fm, LAYERS, l, 7, 39)),
            -0.5 * (shift(phi, -1) - shift(phi, 1))[:, 0:LANES],
            -0.5 * (at(fm, LAYERS, l + 1, 8, 40) - at(fm, LAYERS, l - 1, 8, 40)),
        )
        for c in range(3):
            n = c * LAYERS + l
            drive = drive_of(p[c], alpha2, total, *landau)
            both = wide(rm, rs, n, 8, 40)
            lap = (
                at(rm, c * LAYERS, l, 9, 41) + at(rm, c * LAYERS, l, 7, 39)
                + (shift(both, -1) + shift(both, 1))[:, 0:LANES]
                + at(rm, c * LAYERS, l + 1, 8, 40) + at(rm, c * LAYERS, l - 1, 8, 40)
                - 6.0 * p[c]
            )
            out_ref[n * ROWS : (n + 1) * ROWS, :] = p[c] - DT * (drive - field[c]) + e * lap
            field_ref[n * ROWS : (n + 1) * ROWS, :] = field[c]


VMEM = pl.BlockSpec(memory_space=pltpu.VMEM)
HBM = pl.BlockSpec(memory_space=pltpu.HBM)


def call(kernel, shapes, specs, scratch, name):
    many = isinstance(shapes, list)
    return pl.pallas_call(
        kernel,
        out_shape=[jax.ShapeDtypeStruct(s, F32) for s in shapes]
        if many
        else jax.ShapeDtypeStruct(shapes, F32),
        in_specs=specs,
        out_specs=[VMEM] * len(shapes) if many else VMEM,
        scratch_shapes=[s if not isinstance(s, tuple) else pltpu.VMEM(s, F32) for s in scratch],
        compiler_params=PARAMS,
        name=name,
    )


def shards(tabs, polarization, alpha_field, landau, stiffness, permittivity, interfaces):
    count = lax.axis_size("bx")
    devices = count * NB
    ahead = [(i, (i + 1) % count) for i in range(count)]
    behind = [(i, (i - 1) % count) for i in range(count)]
    cells = polarization.reshape(24 * ROWS, LANES)
    alpha = alpha_field.reshape(LAYERS * ROWS, LANES)
    par = jnp.concatenate(
        [(landau * np.array([[4.0], [2.0], [6.0]], np.float32)).reshape(24), DT * stiffness, permittivity, interfaces]
    )
    par = jnp.broadcast_to(par[:, None], (par.shape[0], 2 * LANES))
    last, first = call(
        border_kernel, [(128, LANES), (64, LANES)], [HBM] * 2,
        [(2, 32, 8, LANES), pltpu.SemaphoreType.DMA((4,))], "border",
    )(polarization.reshape(24, ROWS, LANES), alpha_field)
    low = lax.ppermute(last, "bx", ahead)
    high = lax.ppermute(first, "bx", behind)
    sent = call(
        charge_kernel, (NB * SLOT, LANES), [VMEM] * 4,
        [(32 * 40, LANES), (24 * 40, LANES), (NB * 32, LANES), (48, LANES)], "charge",
    )(cells, alpha, low, par)
    lines = lax.all_to_all(sent.reshape(NB, SLOT, LANES), "by", 0, 0, tiled=True).reshape(NB * SLOT, LANES)
    modes, corner = call(
        y_forward_kernel, [(devices, LANES), (8, LANES)], [VMEM] * 7, [(256, 256)] * 2, "y_forward"
    )(lines, *tabs["fwd"], *tabs["fwd0"], tabs["tw"], high)
    modes = lax.all_to_all(modes.reshape(devices, 1, LANES), ("bx", "by"), 0, 0, tiled=True)
    modes = call(
        x_kernel, (devices, LANES), [VMEM] * 7,
        [(2 * devices, LANES), (2 * devices, LANES)], "x_solve",
    )(
        modes.reshape(devices, LANES), *tabs["x"], *tabs["xt"], tabs["lam"], par
    )
    modes = lax.all_to_all(modes.reshape(devices, 1, LANES), ("bx", "by"), 0, 0, tiled=True)
    sent = call(
        y_inverse_kernel, (NB * SLOT, LANES), [VMEM] * 8, [(256, 256)], "y_inverse"
    )(modes.reshape(devices, LANES), *tabs["inv"], *tabs["inv0"], tabs["tw"], lines, corner)
    phi = lax.all_to_all(sent.reshape(NB, SLOT, LANES), "by", 0, 0, tiled=True)
    far = lax.ppermute(phi[NB - 4 :].reshape(4 * SLOT, LANES), "bx", ahead)
    star = call(
        star_kernel, [(24 * 48, LANES)] * 2, [VMEM] * 6,
        [(32 * 48, LANES)] * 2, "star",
    )(cells, alpha, low, high, phi, par)
    polar, field = call(
        update_kernel, [(24 * ROWS, LANES)] * 2, [VMEM] * 6,
        [(16 * 48, LANES)] * 2 + [(24 * 48, LANES)] * 2 + [(NB * 32, LANES)], "update",
    )(alpha, *star, phi.reshape(NB * SLOT, LANES), far, par)
    return polar.reshape(polarization.shape), field.reshape(polarization.shape)


def solution(mesh):
    fwd, fwd0, inv, inv0, tw = tables_y()
    table, lam = tables_x(mesh.shape["bx"] * ROWS, -SHIFT)
    back, _ = tables_x(mesh.shape["bx"] * ROWS, SHIFT)
    tabs = {
        "fwd": split_table(fwd), "fwd0": split_table(fwd0),
        "inv": split_table(inv), "inv0": split_table(inv0),
        "tw": tw, "x": split_table(table), "xt": split_table(back.T), "lam": lam,
    }
    return jax.shard_map(
        functools.partial(shards, tabs),
        mesh=mesh,
        in_specs=(P(None, None, "bx", "by"), P(None, "bx", "by"), P(), P(), P(), P()),
        out_specs=(P(None, None, "bx", "by"), P(None, None, "bx", "by")),
        check_vma=False,
    )
```

time: 147 us -> 135 us (0.918)
  blocking collectives: 95.4 us -> 81.8 us
  waiting for transfers between devices: 12.1 us -> 18.7 us
  Pallas kernels: 12.8 us -> 8.53 us
  starting transfers between devices: 22.1 us -> 18 us
  local copies, waits for them, and re-layouts: 3.02 us -> 6.08 us
    all_to_all x2 -> x1, blocking collectives: 28.7 us -> 11 us  [shards(): phi = lax.all_to_all(sent.reshape(NB, SLOT, LANES), 'by', 0, 0, tiled=True)]
    ppermute x1, starting transfers between devices: 14.7 us -> 4.27 us  [shards(): high = lax.ppermute(first, 'bx', behind)]
    all_to_all x0 -> x1, starting transfers between devices: none -> 6.1 us  [shards(): lax.all_to_all(sent.reshape(NB, SLOT, LANES), 'by', 0, 0, tiled=True)]
    ppermute x1, waiting for transfers between devices: 6.33 us -> 11 us  [shards(): low = lax.ppermute(last, 'bx', ahead)]
    pallas_call x5 -> x7, Pallas kernels: 12.8 us -> 8.53 us  [the longest x1 2.03 us: shards(): call(update_kernel, [(24 * ROWS, LANES)] * 2, [VMEM] * 6, [(16 * 48, LANE...]
    all_to_all x2, blocking collectives: 66.7 us -> 70.8 us  [shards(): lax.all_to_all(modes.reshape(devices, 1, LANES), ('bx', 'by'), 0, 0, tile...]
    unnamed x42 -> x46, local copies, waits for them, and re-layouts: 3.02 us -> 5.92 us
    ppermute x1, starting transfers between devices: 1.92 us -> 4.51 us  [shards(): low = lax.ppermute(last, 'bx', ahead)]
  transfers between devices with their start and end apart: 4 -> 4, of which waited for: 2 -> 4; matrix products, arithmetic and copies ran while one was open for 0% -> 0% of each run, Pallas kernels for 0% -> 1%
where the time goes in v2:
time: 135 us; the launch traced here: 134 us
  blocking collectives  81.8 us (61%)
  waiting for transfers between devices  18.7 us (14%)
  starting transfers between devices  18 us (13%)
  Pallas kernels  8.53 us (6%)
  local copies, waits for them, and re-layouts  6.08 us (5%)
    all_to_all x2, blocking collectives, shards(): lax.all_to_all(modes.reshape(devices, 1, LANES), ('bx', 'by'), 0, 0, tile...  70.8 us
    all_to_all x1, blocking collectives, shards(): phi = lax.all_to_all(sent.reshape(NB, SLOT, LANES), 'by', 0, 0, tiled=True)  11 us
    ppermute x1, waiting for transfers between devices, shards(): low = lax.ppermute(last, 'bx', ahead)  11 us
    all_to_all x1, starting transfers between devices, shards(): lax.all_to_all(sent.reshape(NB, SLOT, LANES), 'by', 0, 0, tiled=True)  6.1 us
    unnamed x46, local copies, waits for them, and re-layouts  5.92 us
    ppermute x1, starting transfers between devices, shards(): low = lax.ppermute(last, 'bx', ahead)  4.51 us
    ppermute x1, waiting for transfers between devices, shards(): far = lax.ppermute(phi[NB - 4:].reshape(4 * SLOT, LANES), 'bx', ahead)  4.37 us
    ppermute x1, starting transfers between devices, shards(): high = lax.ppermute(first, 'bx', behind)  4.27 us
  transfers between devices with their start and end apart: 4, of which 4 were waited for; matrix products, arithmetic and copies ran while one was open for 0% of the time, Pallas kernels for 1%

profile of v2, /device:TPU:1, one launch (start us, length us, event | category | flops | bytes accessed | tf_op | source)
XLA Modules:
  0.0 134.1 jit_solution(16663968521828340536)
XLA Ops:
  0.6 1.0 copy-done
  1.6 0.9 copy-done.2
  2.5 0.1 border.1
  2.7 0.0 copy-start.21
  2.7 4.5 %collective-permute-start = (f32[128,128]{1,0:T(8,128)S(1)}, f32[128,128]{1,0:T(8,128)S(1)}, u32[]{:S(2)}, u32[]{:S(2)}) collective-permute-start(f32[128,128]{1,0:T(8,128)S(1)} %get-tuple-element.10), channel_id=1, source_target_pairs={{0,16},{16,32},{32,48},{48,64},{64,80},{80,96},{96,112},{112,128},... | collective-permute-start | bytes 196616 | tf_op jit(solution)/shard_map/ppermute | solution.py:566
  7.3 0.1 broadcast_multiply_fusion
  7.3 0.1 reshape.53
  7.4 0.6 copy-done.19
  8.0 0.0 copy-done.20
  8.0 0.1 pad_maximum_fusion
  8.1 11.0 %collective-permute-done.lo_ref = f32[128,128]{1,0:T(8,128)S(1)} collective-permute-done((f32[128,128]{1,0:T(8,128)S(1)}, f32[128,128]{1,0:T(8,128)S(1)}, u32[]{:S(2)}, u32[]{:S(2)}) %collective-permute-start) | collective-permute-done | bytes 65568 | tf_op jit(solution)/shard_map/ppermute | solution.py:566
  19.1 0.1 broadcast_in_dim.2.par
  19.2 0.0 copy-start.8
  19.2 0.0 copy-start.9
  19.2 1.8 %charge.1 = f32[640,128]{1,0:T(8,128)} custom-call(f32[768,128]{1,0:T(8,128)S(1)} %bitcast.19, f32[256,128]{1,0:T(8,128)S(1)} %bitcast.24, f32[128,128]{1,0:T(8,128)S(1)} %collective-permute-done.lo_ref, f32[49,256]{1,0:T(8,128)S(1)} %broadcast_in_dim.2.par), custom_call_target="tpu_custom_call" | custom-call | tf_op jit(solution)/shard_map/charge/pallas_call | solution.py:568
  21.0 6.1 %all-to-all-start = ((f32[16,40,128]{2,1,0:T(8,128)}), f32[16,40,128]{2,1,0:T(8,128)S(1)}, u32[]{:S(2)}, u32[]{:S(2)}) async-start(f32[16,40,128]{2,1,0:T(8,128)} %bitcast.3), calls=%async_computation | async-start | bytes 655360 | tf_op jit(solution)/shard_map/all_to_all | solution.py:572
  27.1 4.3 %collective-permute-start.1 = (f32[64,128]{1,0:T(8,128)S(1)}, f32[64,128]{1,0:T(8,128)S(1)}, u32[]{:S(2)}, u32[]{:S(2)}) collective-permute-start(f32[64,128]{1,0:T(8,128)S(1)} %get-tuple-element.11), channel_id=1, source_target_pairs={{0,496},{16,0},{32,16},{48,32},{64,48},{80,64},{96,80},{112,96},{1... | collective-permute-start | bytes 98312 | tf_op jit(solution)/shard_map/ppermute | solution.py:567
  31.4 1.0 collective-permute-done.1.hi_ref
  32.4 2.3 %all-to-all-done = f32[16,40,128]{2,1,0:T(8,128)S(1)} async-done(((f32[16,40,128]{2,1,0:T(8,128)}), f32[16,40,128]{2,1,0:T(8,128)S(1)}, u32[]{:S(2)}, u32[]{:S(2)}) %all-to-all-start) | async-done | bytes 327712 | tf_op jit(solution)/shard_map/all_to_all | solution.py:572
  34.8 0.9 copy-done.11
  35.7 0.9 y_forward.1
  36.6 37.8 %all_to_all.20 = f32[512,1,128]{2,1,0:T(1,128)S(1)} all-to-all(f32[512,1,128]{2,1,0:T(1,128)S(1)} %bitcast.31), channel_id=1, replica_groups=mesh['bx'=32,'by'=16] {'bx','by'}, dimensions={0} | all-to-all | bytes 524288 | tf_op jit(solution)/shard_map/all_to_all | solution.py:576
  74.4 1.2 copy-done.6
  75.7 1.2 copy-done.7
  76.9 1.5 %x_solve.1 = f32[512,128]{1,0:T(8,128)S(1)} custom-call(f32[512,128]{1,0:T(8,128)S(1)} %bitcast.28, bf16[1024,512]{1,0:T(8,128)(2,1)S(1)} %copy-done.7, bf16[1024,512]{1,0:T(8,128)(2,1)S(1)} %copy-done.6, bf16[512,1024]{1,0:T(8,128)(2,1)S(1)} %copy-done.5, bf16[512,1024]{1,0:T(8,128)(2,1)S(1)} %copy-done.4, f32[8,1024]{1,0:T(8,128)S(1)} %copy-done.16, ...), custom_call_target="tpu_custom_call" | custom-call | tf_op jit(solution)/shard_map/x_solve/pallas_call | solution.py:577
  78.5 33.0 %all_to_all.21 = f32[512,1,128]{2,1,0:T(1,128)S(1)} all-to-all(f32[512,1,128]{2,1,0:T(1,128)S(1)} %bitcast.29), channel_id=1, replica_groups=mesh['bx'=32,'by'=16] {'bx','by'}, dimensions={0} | all-to-all | bytes 524288 | tf_op jit(solution)/shard_map/all_to_all | solution.py:583
  111.4 0.8 y_inverse.1
  112.3 11.0 %all_to_all.22.phi_ref = f32[16,40,128]{2,1,0:T(8,128)S(1)} all-to-all(f32[16,40,128]{2,1,0:T(8,128)S(1)} %bitcast.27), channel_id=1, replica_groups=mesh['bx'=32,'by'=16] {'by'}, dimensions={0} | all-to-all | bytes 655360 | tf_op jit(solution)/shard_map/all_to_all | solution.py:587
  123.3 3.1 %collective-permute-start.2 = (f32[160,128]{1,0:T(8,128)S(1)}, f32[160,128]{1,0:T(8,128)S(1)}, u32[]{:S(2)}, u32[]{:S(2)}) collective-permute-start(f32[160,128]{1,0:T(8,128)S(1)} %bitcast.32), channel_id=1, source_target_pairs={{0,16},{16,32},{32,48},{48,64},{64,80},{80,96},{96,112},{112,128},... | collective-permute-start | bytes 245768 | tf_op jit(solution)/shard_map/ppermute | solution.py:588
  126.4 1.3 star.1
  127.7 4.4 %collective-permute-done.2.far_ref = f32[160,128]{1,0:T(8,128)S(1)} collective-permute-done((f32[160,128]{1,0:T(8,128)S(1)}, f32[160,128]{1,0:T(8,128)S(1)}, u32[]{:S(2)}, u32[]{:S(2)}) %collective-permute-start.2) | collective-permute-done | bytes 81952 | tf_op jit(solution)/shard_map/ppermute | solution.py:588
  132.1 2.0 %update.1 = (f32[768,128]{1,0:T(8,128)}, f32[768,128]{1,0:T(8,128)}) custom-call(f32[256,128]{1,0:T(8,128)S(1)} %bitcast.26, f32[1152,128]{1,0:T(8,128)S(1)} %get-tuple-element.14.qm, f32[1152,128]{1,0:T(8,128)S(1)} %get-tuple-element.15.qs, f32[640,128]{1,0:T(8,128)S(1)} %bitcast.21, f32[160,128]{1,0:T(8,128)S(1)} %collective-permute-done.2.far_ref, ...), custom_call_target="tpu_custom_call" | custom-call | tf_op jit(solution)/shard_map/update/pallas_call | solution.py:593
  (38 shorter events, 0.1 us)
Async XLA Ops:
  0.6 1.0 copy-start
  1.6 0.9 copy-start.2
  2.5 4.7 %copy-start.22 = (f32[8]{0:T(128)S(1)}, f32[8]{0:T(128)}, u32[]{:S(2)}) copy-start(f32[8]{0:T(128)} %param.24) | copy-start | bytes 100
  2.5 16.6 %copy-start.1 = (f32[3,8,32,128]{3,2,1,0:T(8,128)S(1)}, f32[3,8,32,128]{3,2,1,0:T(8,128)}, u32[]{:S(2)}) copy-start(f32[3,8,32,128]{3,2,1,0:T(8,128)} %param.21) | copy-start | bytes 1179652
  2.5 16.6 %copy-start.3 = (f32[8,32,128]{2,1,0:T(8,128)S(1)}, f32[8,32,128]{2,1,0:T(8,128)}, u32[]{:S(2)}) copy-start(f32[8,32,128]{2,1,0:T(8,128)} %al_ref.1) | copy-start | bytes 393220
  2.7 4.6 %copy-start.18 = (f32[3,8]{1,0:T(4,128)S(1)}, f32[3,8]{1,0:T(4,128)}, u32[]{:S(2)}) copy-start(f32[3,8]{1,0:T(4,128)} %param.23) | copy-start | bytes 292
  2.7 4.6 %copy-start.21 = (f32[3]{0:T(128)S(1)}, f32[3]{0:T(128)}, u32[]{:S(2)}) copy-start(f32[3]{0:T(128)} %constant.47) | copy-start | bytes 40
  2.7 16.4 %collective-permute-start = (f32[128,128]{1,0:T(8,128)S(1)}, f32[128,128]{1,0:T(8,128)S(1)}, u32[]{:S(2)}, u32[]{:S(2)}) collective-permute-start(f32[128,128]{1,0:T(8,128)S(1)} %get-tuple-element.10), channel_id=1, source_target_pairs={{0,16},{16,32},{32,48},{48,64},{64,80},{80,96},{96,112},{112,128},... | collective-permute-start | bytes 196616 | tf_op jit(solution)/shard_map/ppermute | solution.py:566
  7.3 0.7 copy-start.19
  7.3 0.7 copy-start.20
  19.1 15.6 %copy-start.17 = (f32[16,128]{1,0:T(8,128)S(1)}, f32[16,128]{1,0:T(8,128)}, u32[]{:S(2)}) copy-start(f32[16,128]{1,0:T(8,128)} %constant.37.clone.tw) | copy-start | bytes 24580
  19.2 15.6 %copy-start.8 = (bf16[256,256]{1,0:T(8,128)(2,1)S(1)}, bf16[256,256]{1,0:T(8,128)(2,1)}, u32[]{:S(2)}) copy-start(bf16[256,256]{1,0:T(8,128)(2,1)} %constant.36.clone.f0l) | copy-start | bytes 393220
  19.2 15.6 %copy-start.9 = (bf16[256,256]{1,0:T(8,128)(2,1)S(1)}, bf16[256,256]{1,0:T(8,128)(2,1)}, u32[]{:S(2)}) copy-start(bf16[256,256]{1,0:T(8,128)(2,1)} %constant.35.clone.f0h) | copy-start | bytes 393220
  19.2 15.5 %copy-start.10 = (bf16[256,256]{1,0:T(8,128)(2,1)S(1)}, bf16[256,256]{1,0:T(8,128)(2,1)}, u32[]{:S(2)}) copy-start(bf16[256,256]{1,0:T(8,128)(2,1)} %constant.34.clone.fl) | copy-start | bytes 393220
  19.2 55.2 %copy-start.5 = (bf16[512,1024]{1,0:T(8,128)(2,1)S(1)}, bf16[512,1024]{1,0:T(8,128)(2,1)}, u32[]{:S(2)}) copy-start(bf16[512,1024]{1,0:T(8,128)(2,1)} %constant.40.clone.uh) | copy-start | bytes 3145732
  21.0 53.4 %copy-start.4 = (bf16[512,1024]{1,0:T(8,128)(2,1)S(1)}, bf16[512,1024]{1,0:T(8,128)(2,1)}, u32[]{:S(2)}) copy-start(bf16[512,1024]{1,0:T(8,128)(2,1)} %constant.41.clone.ul) | copy-start | bytes 3145732
  21.0 13.7 %all-to-all-start = ((f32[16,40,128]{2,1,0:T(8,128)}), f32[16,40,128]{2,1,0:T(8,128)S(1)}, u32[]{:S(2)}, u32[]{:S(2)}) async-start(f32[16,40,128]{2,1,0:T(8,128)} %bitcast.3), calls=%async_computation | async-start | bytes 655360 | tf_op jit(solution)/shard_map/all_to_all | solution.py:572
  27.1 5.3 %collective-permute-start.1 = (f32[64,128]{1,0:T(8,128)S(1)}, f32[64,128]{1,0:T(8,128)S(1)}, u32[]{:S(2)}, u32[]{:S(2)}) collective-permute-start(f32[64,128]{1,0:T(8,128)S(1)} %get-tuple-element.11), channel_id=1, source_target_pairs={{0,496},{16,0},{32,16},{48,32},{64,48},{80,64},{96,80},{112,96},{1... | collective-permute-start | bytes 98312 | tf_op jit(solution)/shard_map/ppermute | solution.py:567
  34.7 0.9 copy-start.11
  36.6 37.8 %copy-start.16 = (f32[8,1024]{1,0:T(8,128)S(1)}, f32[8,1024]{1,0:T(8,128)}, u32[]{:S(2)}) copy-start(f32[8,1024]{1,0:T(8,128)} %constant.42.clone.lam) | copy-start | bytes 98308
  74.4 1.2 copy-start.6
  75.7 1.2 copy-start.7
  78.4 33.0 %copy-start.12 = (bf16[256,256]{1,0:T(8,128)(2,1)S(1)}, bf16[256,256]{1,0:T(8,128)(2,1)}, u32[]{:S(2)}) copy-start(bf16[256,256]{1,0:T(8,128)(2,1)} %constant.46.clone.g0l) | copy-start | bytes 393220
  78.4 33.0 %copy-start.13 = (bf16[256,256]{1,0:T(8,128)(2,1)S(1)}, bf16[256,256]{1,0:T(8,128)(2,1)}, u32[]{:S(2)}) copy-start(bf16[256,256]{1,0:T(8,128)(2,1)} %constant.45.clone.g0h) | copy-start | bytes 393220
  78.4 33.0 %copy-start.14 = (bf16[256,256]{1,0:T(8,128)(2,1)S(1)}, bf16[256,256]{1,0:T(8,128)(2,1)}, u32[]{:S(2)}) copy-start(bf16[256,256]{1,0:T(8,128)(2,1)} %constant.44.clone.gl) | copy-start | bytes 393220
  78.4 33.0 %copy-start.15 = (bf16[256,256]{1,0:T(8,128)(2,1)S(1)}, bf16[256,256]{1,0:T(8,128)(2,1)}, u32[]{:S(2)}) copy-start(bf16[256,256]{1,0:T(8,128)(2,1)} %constant.43.clone.gh) | copy-start | bytes 393220
  123.3 8.8 %collective-permute-start.2 = (f32[160,128]{1,0:T(8,128)S(1)}, f32[160,128]{1,0:T(8,128)S(1)}, u32[]{:S(2)}, u32[]{:S(2)}) collective-permute-start(f32[160,128]{1,0:T(8,128)S(1)} %bitcast.32), channel_id=1, source_target_pairs={{0,16},{16,32},{32,48},{48,64},{64,80},{80,96},{96,112},{112,128},... | collective-permute-start | bytes 245768 | tf_op jit(solution)/shard_map/ppermute | solution.py:588

commit v3 on v2

--- a/solution.py
+++ b/solution.py
@@ -18,7 +18,9 @@
 SHIFT = 2
 F32 = jnp.float32
 BF16 = jnp.bfloat16
-PARAMS = pltpu.CompilerParams(vmem_limit_bytes=16 * 1024 * 1024)
+MICROSECONDS = {
+    "border": 0.8, "stage": 1.8, "charge": 0.5, "load_y": 0.5,   "y_forward": 0.9, "x_solve": 1.5, "y_inverse": 0.8, "star": 1.3, "inner": 1.8, "update": 1.0
+}
 
 
 def split_table(table):
@@ -73,10 +75,8 @@
         wave = (np.sin if kind else np.cos)(2 * np.pi * (k * pos % nx) / nx)
         rows.append(wave * (np.sqrt(1.0 / nx) if k in (0, half) else scale))
     freq = np.array([k for k, _ in kinds])
-    lam = np.zeros((8, nx), np.float32)
-    lam[0] = 4 * np.sin(np.pi * freq / nx) ** 2
-    lam[1] = np.sin(2 * np.pi * freq / nx) ** 2
-    return np.stack(rows), lam
+    lam = np.stack([4 * np.sin(np.pi * freq / nx) ** 2, np.sin(2 * np.pi * freq / nx) ** 2])
+    return np.stack(rows), lam.reshape(-1, LANES).astype(np.float32)
 
 
 def split(value):
@@ -119,14 +119,14 @@
 
 
 def coefficient(par, kind, l, width=LANES):
-    return par[kind * LAYERS + l : kind * LAYERS + l + 1, 0:width]
-
-
-def border_kernel(p_ref, al_ref, last_ref, first_ref, buf, sems):
+    row = par[kind * LAYERS + l : kind * LAYERS + l + 1, 0:width]
+    return row if kind > 3 else (4.0, 2.0, 6.0, DT)[kind] * row
+
+
+def border_kernel(p_ref, al_ref, last_ref, buf, sems):
     copies = [
-        pltpu.make_async_copy(src.at[:, rows, :], buf.at[k, cells], sems.at[2 * k + m])
-        for k, rows in enumerate((pl.ds(ROWS - 8, 8), pl.ds(0, 8)))
-        for m, (src, cells) in enumerate(((p_ref, pl.ds(0, 24)), (al_ref, pl.ds(24, 8))))
+        pltpu.make_async_copy(src.at[:, pl.ds(ROWS - 8, 8), :], buf.at[cells], sems.at[k])
+        for k, (src, cells) in enumerate(((p_ref, pl.ds(0, 24)), (al_ref, pl.ds(24, 8))))
     ]
     for copy in copies:
         copy.start()
@@ -134,54 +134,55 @@
         copy.wait()
     for n in range(32):
         for r in range(4):
-            last_ref[r * 32 + n : r * 32 + n + 1, :] = buf[0, n, 4 + r : 5 + r, :]
-        for r in range(2):
-            first_ref[r * 32 + n : r * 32 + n + 1, :] = buf[1, n, r : r + 1, :]
-
-
-def charge_kernel(p_ref, al_ref, lo_ref, par, out_ref, px, nx, ws, eb):
-    lane = lax.broadcasted_iota(jnp.int32, (ROWS, LANES), 1)
-    for n in range(24):
-        px[n * 40 + 8 : n * 40 + 40, :] = p_ref[n * ROWS : (n + 1) * ROWS, :]
+            last_ref[r * 32 + n : r * 32 + n + 1, :] = buf[n, 4 + r : 5 + r, :]
+
+
+def load_kernel(table, hi_ref, after, table_ref, corner_ref, sem):
+    copy = pltpu.make_async_copy(table, table_ref, sem.at[0])
+    copy.start()
+    corner_ref[...] = jnp.concatenate([pack(hi_ref[0:32, :]), jnp.zeros((7, LANES), F32)], axis=0)
+    copy.wait()
+
+
+def rows_of(ref, c, l, low, high):
+    if 0 <= l < LAYERS:
+        n = c * LAYERS + l
+        return ref[n * 40 + low : n * 40 + high, :]
+    return jnp.zeros((high - low, LANES), F32)
+
+
+def charges(px, nx, par, low, high, store):
+    at = rows_of
+    first, last = low - 1, high + 1
     for l in range(LAYERS):
-        px[(24 + l) * 40 + 8 : (24 + l) * 40 + 40, :] = al_ref[l * ROWS : (l + 1) * ROWS, :]
-    for r in range(4):
-        px[pl.ds(4 + r, 32, stride=40), :] = lo_ref[r * 32 : (r + 1) * 32, :]
-
-    def at(ref, c, l, low, high):
-        if 0 <= l < LAYERS:
-            n = c * LAYERS + l
-            return ref[n * 40 + low : n * 40 + high, :]
-        return jnp.zeros((high - low, LANES), F32)
-
-    for l in range(LAYERS):
-        p = [at(px, c, l, 5, 39) for c in range(3)]
+        p = [at(px, c, l, first, last) for c in range(3)]
         total = p[0] * p[0] + p[1] * p[1] + p[2] * p[2]
-        alpha2 = 2.0 * at(px, 3, l, 5, 39)
+        alpha2 = 2.0 * at(px, 3, l, first, last)
         e = coefficient(par, 3, l)
         landau = [coefficient(par, k, l) for k in range(3)]
         for c in range(3):
             drive = drive_of(p[c], alpha2, total, *landau)
             lap = (
-                at(px, c, l, 6, 40) + at(px, c, l, 4, 38)
-                + at(px, c, l + 1, 5, 39) + at(px, c, l - 1, 5, 39)
+                at(px, c, l, first + 1, last + 1) + at(px, c, l, first - 1, last - 1)
+                + at(px, c, l + 1, first, last) + at(px, c, l - 1, first, last)
                 - 6.0 * p[c]
             )
             n = c * LAYERS + l
-            nx[n * 40 + 5 : n * 40 + 39, :] = p[c] - DT * drive + e * lap
+            nx[n * 40 + first : n * 40 + last, :] = p[c] - DT * drive + e * lap
+    lane = lax.broadcasted_iota(jnp.int32, (high - low, LANES), 1)
     for l in range(LAYERS):
         e = coefficient(par, 3, l)
-        dx = -0.5 * (at(px, 0, l, 7, 39) - at(px, 0, l, 5, 37))
-        above, below = at(px, 2, l + 1, 6, 38), at(px, 2, l - 1, 6, 38)
-        p1, n1 = at(px, 1, l, 6, 38), at(nx, 1, l, 6, 38)
+        dx = -0.5 * (at(px, 0, l, low + 1, high + 1) - at(px, 0, l, low - 1, high - 1))
+        above, below = at(px, 2, l + 1, low, high), at(px, 2, l - 1, low, high)
+        p1, n1 = at(px, 1, l, low, high), at(nx, 1, l, low, high)
         fwd, bwd = shift(p1, -1), shift(p1, 1)
         one = dx - 0.5 * (above - below) - 0.5 * (fwd - bwd)
         wrap_one = jnp.where(lane == LANES - 1, -0.5 * fwd, jnp.where(lane == 0, 0.5 * bwd, 0.0))
         e_up = coefficient(par, 3, l + 1) if l + 1 < LAYERS else 0.0
         e_dn = coefficient(par, 3, l - 1) if l > 0 else 0.0
         ue = e * dx - 0.5 * (e_up * above - e_dn * below)
-        un = -0.5 * (at(nx, 0, l, 7, 39) - at(nx, 0, l, 5, 37)) - 0.5 * (
-            at(nx, 2, l + 1, 6, 38) - at(nx, 2, l - 1, 6, 38)
+        un = -0.5 * (at(nx, 0, l, low + 1, high + 1) - at(nx, 0, l, low - 1, high - 1)) - 0.5 * (
+            at(nx, 2, l + 1, low, high) - at(nx, 2, l - 1, low, high)
         )
         a = shift(ue - 0.5 * n1, -1)
         b = shift(ue + 0.5 * n1, 1)
@@ -194,16 +195,31 @@
             + jnp.where(lane >= LANES - 2, -c2, 0.0)
             + jnp.where(lane < 2, d2, 0.0)
         )
-        for f, (whole, wrap) in enumerate(((one, wrap_one), (two, wrap_two))):
-            main = whole - wrap
-            for xl in range(2):
-                r = f * 16 + xl * 8 + l
-                out_ref[pl.ds(r, NB, stride=SLOT), :] = main[xl * NB : (xl + 1) * NB]
-                ws[pl.ds(r, NB, stride=32), :] = wrap[xl * NB : (xl + 1) * NB]
+        store(0, l, one - wrap_one, wrap_one)
+        store(1, l, two - wrap_two, wrap_two)
+
+
+def stage_kernel(p_ref, al_ref, par, after, out_ref, head_ref, first_ref, px, nx, ws, eb):
     for n in range(32):
-        eb[n : n + 1, :] = pack(px[n * 40 + 8 : n * 40 + 40, :])
-    eb[32:33, :] = pack(lo_ref[96:128, :])
-    eb[33:48, :] = jnp.zeros((15, LANES), F32)
+        ref, m = (p_ref, n) if n < 24 else (al_ref, n - 24)
+        px[n * 40 + 8 : n * 40 + 40, :] = ref[m * ROWS : (m + 1) * ROWS, :]
+        head_ref[n * 8 : (n + 1) * 8, :] = ref[m * ROWS : m * ROWS + 8, :]
+        eb[n : n + 1, :] = pack(ref[m * ROWS : (m + 1) * ROWS, :])
+    eb[32:48, :] = jnp.zeros((16, LANES), F32)
+    for r in range(2):
+        first_ref[r * 32 : (r + 1) * 32, :] = px[pl.ds(8 + r, 32, stride=40), :]
+
+    def store(f, l, main, wrap):
+        r = f * 16 + l
+        out_ref[pl.ds(4 * SLOT + r, 12, stride=SLOT), :] = main[0:12]
+        ws[pl.ds(4 * 32 + r, 12, stride=32), :] = wrap[0:12]
+        out_ref[pl.ds(r + 8, NB, stride=SLOT), :] = main[12:28]
+        ws[pl.ds(r + 8, NB, stride=32), :] = wrap[12:28]
+        for b in range(4):
+            ws[b * 32 + r : b * 32 + r + 1, :] = jnp.zeros((1, LANES), F32)
+            out_ref[b * SLOT + r : b * SLOT + r + 1, :] = jnp.zeros((1, LANES), F32)
+
+    charges(px, nx, par, 10, 38, store)
     blank = jnp.zeros((4, LANES), F32)
     for b in range(NB):
         out_ref[b * SLOT + 32 : (b + 1) * SLOT, :] = jnp.concatenate(
@@ -211,8 +227,31 @@
         )
 
 
-def y_forward_kernel(in_ref, fh, fl, f0h, f0l, tw, hi_ref, out_ref, corner_ref, d_ref, o_ref):
-    corner_ref[...] = jnp.concatenate([pack(hi_ref[0:32, :]), jnp.zeros((7, LANES), F32)], axis=0)
+def charge_kernel(part_ref, head_ref, lo_ref, par, out_ref, px, nx, ws):
+    out_ref[...] = part_ref[...]
+    for n in range(32):
+        px[n * 40 + 8 : n * 40 + 16, :] = head_ref[n * 8 : (n + 1) * 8, :]
+    for r in range(4):
+        px[pl.ds(4 + r, 32, stride=40), :] = lo_ref[r * 32 : (r + 1) * 32, :]
+    ws[...] = jnp.zeros_like(ws)
+
+    def store(f, l, main, wrap):
+        r = f * 16 + l
+        for b in range(4):
+            out_ref[b * SLOT + r : b * SLOT + r + 1, :] = main[b : b + 1]
+            ws[b * 32 + r : b * 32 + r + 1, :] = wrap[b : b + 1]
+
+    charges(px, nx, par, 6, 10, store)
+    for b in range(4):
+        out_ref[b * SLOT + 32 : b * SLOT + 33, :] = part_ref[b * SLOT + 32 : b * SLOT + 33, :] + pack(
+            ws[b * 32 : (b + 1) * 32, :]
+        )
+    at = (32 // 3) * SLOT + 33 + 32 % 3
+    out_ref[at : at + 1, :] = pack(lo_ref[96:128, :])
+
+
+def y_forward_kernel(in_ref, tab, tw, out_ref, d_ref, o_ref):
+    fh, fl, f0h, f0l = (tab[k * 256 : (k + 1) * 256, :] for k in range(4))
     lane1 = lax.broadcasted_iota(jnp.int32, (1, LANES), 1)
     lane = lax.broadcasted_iota(jnp.int32, (ROWS, LANES), 1)
     g = []
@@ -250,8 +289,8 @@
         d_ref[j * 32 : (j + 1) * 32, 0:LANES] = re[j] * c + im[j] * s
         d_ref[j * 32 : (j + 1) * 32, LANES:256] = im[j] * c - re[j] * s
     dh, dl = split(d_ref[...])
-    o_ref[...] = dot_t(fh[...], dh) + dot_t(fh[...], dl) + dot_t(fl[...], dh)
-    zero = dot_t(f0h[...], dh[0:128]) + dot_t(f0h[...], dl[0:128]) + dot_t(f0l[...], dh[0:128])
+    o_ref[...] = dot_t(fh, dh) + dot_t(fh, dl) + dot_t(fl, dh)
+    zero = dot_t(f0h, dh[0:128]) + dot_t(f0h, dl[0:128]) + dot_t(f0l, dh[0:128])
     wide = lax.broadcasted_iota(jnp.int32, (256, LANES), 1)
     o_ref[:, 0:LANES] = jnp.where(wide < 32, zero, o_ref[:, 0:LANES])
     lane64 = lax.broadcasted_iota(jnp.int32, (64, LANES), 1)
@@ -266,7 +305,7 @@
         out_ref[j * 64 : (j + 1) * 64, :] = value
 
 
-def x_kernel(in_ref, th, tl, uh, ul, lam, par, out_ref, zs, ys):
+def x_kernel(in_ref, th, tl, lam, par, out_ref, zs, ys):
     n = in_ref.shape[0]
     half = n // 2
     top, low = in_ref[0:half, :], in_ref[half:n, :]
@@ -303,9 +342,8 @@
     eps = [coefficient(par, 4, l) for l in range(LAYERS)]
     iface = [coefficient(par, 5, l) for l in range(LAYERS + 1)]
     for chunk in range(2 * n // LANES):
-        cols = slice(chunk * LANES, (chunk + 1) * LANES)
-        lateral = lam_y + lam[0:1, cols]
-        slope = slope_y + lam[1:2, cols]
+        lateral = lam_y + lam[16 + chunk : 17 + chunk, :]
+        slope = slope_y + lam[16 + 2 * n // LANES + chunk : 17 + 2 * n // LANES + chunk, :]
         inverse, ratio = [], []
         for l in range(LAYERS):
             pivot = eps[l] * lateral + (iface[l] + iface[l + 1])
@@ -339,26 +377,22 @@
             value = phi[l] + more[l]
             ys[pl.ds(chunk * LANES + l, 8, stride=16), :] = value
             ys[pl.ds(chunk * LANES + 8 + l, 8, stride=16), :] = value
-    lane = lax.broadcasted_iota(jnp.int32, (half, LANES), 1)
-    odd_row = lane // 8 % 2 == 1
+    odd_row = lax.broadcasted_iota(jnp.int32, (LANES, half), 0) // 8 % 2 == 1
     pair = []
     for part in range(2):
-        cols = slice(part * n, (part + 1) * n)
         high, rest = split(
             jnp.concatenate([ys[r : r + LANES, :] for r in range(part * n, (part + 1) * n, LANES)], axis=1)
         )
-        both = jnp.concatenate([high, rest], axis=0)
-        acc = []
-        for xl in range(2):
-            rows = slice(xl * half, (xl + 1) * half)
-            wide = dot_t(uh[rows, cols], both)
-            acc.append(wide[:, 0:LANES] + wide[:, LANES:256] + dot_t(ul[rows, cols], high))
-        pair.append(jnp.where(odd_row, acc[1], acc[0]))
-    out_ref[0:half, :] = pair[0] + pair[1]
-    out_ref[half:n, :] = pair[0] - pair[1]
-
-
-def y_inverse_kernel(in_ref, gh, gl, g0h, g0l, tw, lines, corner_ref, out_ref, o_ref):
+        rows = slice(part * n, (part + 1) * n)
+        both = dot(jnp.concatenate([high, rest], axis=0), th[rows, :])
+        both = both[0:LANES] + both[LANES:256] + dot(high, tl[rows, :])
+        pair.append(jnp.where(odd_row, both[:, half:n], both[:, 0:half]))
+    out_ref[0:half, :] = jnp.transpose(pair[0] + pair[1])
+    out_ref[half:n, :] = jnp.transpose(pair[0] - pair[1])
+
+
+def y_inverse_kernel(in_ref, tab, tw, lines, corner_ref, out_ref, o_ref):
+    gh, gl, g0h, g0l = (tab[k * 256 : (k + 1) * 256, :] for k in range(4))
     lane64 = lax.broadcasted_iota(jnp.int32, (64, LANES), 1)
     for t in range(2):
         for q in range(4):
@@ -371,9 +405,9 @@
                 value = piece if value is None else jnp.where(lane64 // 32 == at, piece, value)
             o_ref[q * 64 : (q + 1) * 64, t * LANES : (t + 1) * LANES] = value
     oh, ol = split(o_ref[...])
-    o_ref[...] = dot(gh[...], oh) + dot(gh[...], ol) + dot(gl[...], oh)
+    o_ref[...] = dot(gh, oh) + dot(gh, ol) + dot(gl, oh)
     zero = (
-        dot(g0h[...], oh[:, 0:LANES]) + dot(g0h[...], ol[:, 0:LANES]) + dot(g0l[...], oh[:, 0:LANES])
+        dot(g0h, oh[:, 0:LANES]) + dot(g0h, ol[:, 0:LANES]) + dot(g0l, oh[:, 0:LANES])
     )
     wide = lax.broadcasted_iota(jnp.int32, (256, LANES), 1)
     o_ref[:, 0:LANES] = jnp.where(wide < 32, zero, o_ref[:, 0:LANES])
@@ -428,20 +462,74 @@
     return jnp.concatenate([main[rows, :], side[rows, :]], axis=1)
 
 
+def edge_row(n):
+    return n // 3 * SLOT + 33 + n % 3
+
+
 def near(base, l):
     return base + l if 0 <= l < LAYERS else None
+
+
+def layer_rows(ref, base, l, low, high):
+    if 0 <= l < LAYERS:
+        return ref[(base + l) * 48 + low : (base + l) * 48 + high, :]
+    return jnp.zeros((high - low, LANES), F32)
+
+
+def first_step(qm, qs, fm, fs, rm, rs, low, high):
+    for l in range(LAYERS):
+        phi = wide(fm, fs, l, low, high)
+        slope = (
+            wide(fm, fs, l, low + 1, high + 1) - wide(fm, fs, l, low - 1, high - 1),
+            shift(phi, -1) - shift(phi, 1),
+            wide(fm, fs, near(0, l + 1), low, high) - wide(fm, fs, near(0, l - 1), low, high),
+        )
+        for c in range(3):
+            rows = slice((c * LAYERS + l) * 48 + low, (c * LAYERS + l) * 48 + high)
+            rm[rows, :] = qm[rows, :] - (0.5 * DT) * slope[c][:, 0:LANES]
+            rs[rows, :] = qs[rows, :] - (0.5 * DT) * slope[c][:, LANES : 2 * LANES]
+
+
+def second_step(al_ref, fm, fs, rm, rs, par, low, high, store):
+    at = layer_rows
+    for l in range(LAYERS):
+        p = [at(rm, c * LAYERS, l, low, high) for c in range(3)]
+        total = p[0] * p[0] + p[1] * p[1] + p[2] * p[2]
+        alpha2 = 2.0 * al_ref[l * ROWS + low - 8 : l * ROWS + high - 8, :]
+        e = coefficient(par, 3, l)
+        landau = [coefficient(par, k, l) for k in range(3)]
+        phi = wide(fm, fs, LAYERS + l, low, high)
+        field = (
+            -0.5 * (at(fm, LAYERS, l, low + 1, high + 1) - at(fm, LAYERS, l, low - 1, high - 1)),
+            -0.5 * (shift(phi, -1) - shift(phi, 1))[:, 0:LANES],
+            -0.5 * (at(fm, LAYERS, l + 1, low, high) - at(fm, LAYERS, l - 1, low, high)),
+        )
+        for c in range(3):
+            drive = drive_of(p[c], alpha2, total, *landau)
+            both = wide(rm, rs, c * LAYERS + l, low, high)
+            lap = (
+                at(rm, c * LAYERS, l, low + 1, high + 1) + at(rm, c * LAYERS, l, low - 1, high - 1)
+                + (shift(both, -1) + shift(both, 1))[:, 0:LANES]
+                + at(rm, c * LAYERS, l + 1, low, high) + at(rm, c * LAYERS, l - 1, low, high)
+                - 6.0 * p[c]
+            )
+            store(c * LAYERS + l, p[c] - DT * (drive - field[c]) + e * lap, field[c])
 
 
 def star_kernel(p_ref, al_ref, lo_ref, hi_ref, phi_ref, par, qm, qs, pm, ps):
     from_right = lax.broadcasted_iota(jnp.int32, (1, LANES), 1) % 4 < 2
     by = lax.axis_index("by")
     left, right = (by + NB - 1) % NB, (by + 1) % NB
-    corner_lo = unpack(phi_ref[32 // 3, 33 + 32 % 3 : 34 + 32 % 3, :])
-    corner_hi = unpack(jnp.where(from_right, phi_ref[right, 36:37, :], phi_ref[left, 36:37, :]))
+    corner_lo = unpack(phi_ref[edge_row(32) : edge_row(32) + 1, :])
+    corner_hi = unpack(
+        jnp.where(
+            from_right, phi_ref[pl.ds(right * SLOT + 36, 1), :], phi_ref[pl.ds(left * SLOT + 36, 1), :]
+        )
+    )
     for n in range(32):
         ref, m = (p_ref, n) if n < 24 else (al_ref, n - 24)
         pm[n * 48 + 8 : n * 48 + 40, :] = ref[m * ROWS : (m + 1) * ROWS, :]
-        ps[n * 48 + 8 : n * 48 + 40, :] = unpack(phi_ref[n // 3, 33 + n % 3 : 34 + n % 3, :])
+        ps[n * 48 + 8 : n * 48 + 40, :] = unpack(phi_ref[edge_row(n) : edge_row(n) + 1, :])
     for row, value, corner in (
         (6, lo_ref[64:96, :], corner_lo),
         (7, lo_ref[96:128, :], corner_lo),
@@ -470,80 +558,71 @@
             qs[n * 48 + 7 : n * 48 + 41, :] = value[:, LANES : 2 * LANES]
 
 
-def update_kernel(al_ref, qm, qs, phi_ref, far_ref, par, out_ref, field_ref, fm, fs, rm, rs, ht):
+def inner_kernel(al_ref, qm, qs, phi_ref, par, out_ref, field_ref, fm, fs, rm, rs, ht):
     for src in range(NB):
         ht[src * 32 : (src + 1) * 32, :] = unpack(phi_ref[src * SLOT + 32 : src * SLOT + 33, :])
     for f in range(2):
         for l in range(LAYERS):
             for xl in range(2):
                 r = f * 16 + xl * 8 + l
-                row = (f * LAYERS + l) * 48 + 8 + SHIFT + xl * NB
+                row = (f * LAYERS + l) * 48 + 8 - SHIFT + xl * NB
                 fm[row : row + NB, :] = phi_ref[pl.ds(r, NB, stride=SLOT), :]
                 fs[row : row + NB, :] = ht[pl.ds(r, NB, stride=32), :]
+    first_step(qm, qs, fm, fs, rm, rs, 7, 33)
+
+    def store(n, value, field):
+        out_ref[n, 0:24, :] = value
+        field_ref[n, 0:24, :] = field
+
+    second_step(al_ref, fm, fs, rm, rs, par, 8, 32, store)
+
+
+def update_kernel(
+    al_ref, qm, qs, gm, gs, far_ref, par, out_in, field_in, out_ref, field_ref, fm, fs, rm, rs, to, tf, sems
+):
+    for n in range(2 * LAYERS):
+        fm[n * 48 + 30 : n * 48 + 38, :] = gm[n * 48 + 30 : n * 48 + 38, :]
+        fs[n * 48 + 30 : n * 48 + 38, :] = gs[n * 48 + 30 : n * 48 + 38, :]
     for k in range(4):
         side = unpack(far_ref[k * SLOT + 32 : k * SLOT + 33, :])
         for f in range(2):
-            rows = pl.ds(f * LAYERS * 48 + 6 + k, LAYERS, stride=48)
-            fm[rows, :] = far_ref[k * SLOT + f * 16 + 8 : k * SLOT + f * 16 + 16, :]
-            fs[rows, :] = side[f * 16 + 8 : f * 16 + 16]
-    for l in range(LAYERS):
-        phi = wide(fm, fs, l, 7, 41)
-        slope = (
-            wide(fm, fs, l, 8, 42) - wide(fm, fs, l, 6, 40),
-            shift(phi, -1) - shift(phi, 1),
-            wide(fm, fs, near(0, l + 1), 7, 41) - wide(fm, fs, near(0, l - 1), 7, 41),
-        )
-        for c in range(3):
-            rows = slice((c * LAYERS + l) * 48 + 7, (c * LAYERS + l) * 48 + 41)
-            rm[rows, :] = qm[rows, :] - (0.5 * DT) * slope[c][:, 0:LANES]
-            rs[rows, :] = qs[rows, :] - (0.5 * DT) * slope[c][:, LANES : 2 * LANES]
-
-    def at(ref, base, l, low, high):
-        if 0 <= l < LAYERS:
-            return ref[(base + l) * 48 + low : (base + l) * 48 + high, :]
-        return jnp.zeros((high - low, LANES), F32)
-
-    for l in range(LAYERS):
-        p = [at(rm, c * LAYERS, l, 8, 40) for c in range(3)]
-        total = p[0] * p[0] + p[1] * p[1] + p[2] * p[2]
-        alpha2 = 2.0 * al_ref[l * ROWS : (l + 1) * ROWS, :]
-        e = coefficient(par, 3, l)
-        landau = [coefficient(par, k, l) for k in range(3)]
-        phi = wide(fm, fs, LAYERS + l, 8, 40)
-        field = (
-            -0.5 * (at(fm, LAYERS, l, 9, 41) - at(fm, LAYERS, l, 7, 39)),
-            -0.5 * (shift(phi, -1) - shift(phi, 1))[:, 0:LANES],
-            -0.5 * (at(fm, LAYERS, l + 1, 8, 40) - at(fm, LAYERS, l - 1, 8, 40)),
-        )
-        for c in range(3):
-            n = c * LAYERS + l
-            drive = drive_of(p[c], alpha2, total, *landau)
-            both = wide(rm, rs, n, 8, 40)
-            lap = (
-                at(rm, c * LAYERS, l, 9, 41) + at(rm, c * LAYERS, l, 7, 39)
-                + (shift(both, -1) + shift(both, 1))[:, 0:LANES]
-                + at(rm, c * LAYERS, l + 1, 8, 40) + at(rm, c * LAYERS, l - 1, 8, 40)
-                - 6.0 * p[c]
-            )
-            out_ref[n * ROWS : (n + 1) * ROWS, :] = p[c] - DT * (drive - field[c]) + e * lap
-            field_ref[n * ROWS : (n + 1) * ROWS, :] = field[c]
+            rows = pl.ds(f * LAYERS * 48 + 38 + k, LAYERS, stride=48)
+            fm[rows, :] = far_ref[k * SLOT + f * 16 : k * SLOT + f * 16 + 8, :]
+            fs[rows, :] = side[f * 16 : f * 16 + 8]
+    first_step(qm, qs, fm, fs, rm, rs, 31, 41)
+
+    def store(n, value, field):
+        to[n] = value
+        tf[n] = field
+
+    second_step(al_ref, fm, fs, rm, rs, par, 32, 40, store)
+    copies = [
+        pltpu.make_async_copy(src, dst.at[:, pl.ds(24, 8), :], sems.at[k])
+        for k, (src, dst) in enumerate(((to, out_ref), (tf, field_ref)))
+    ]
+    for copy in copies:
+        copy.start()
+    for copy in copies:
+        copy.wait()
 
 
 VMEM = pl.BlockSpec(memory_space=pltpu.VMEM)
-HBM = pl.BlockSpec(memory_space=pltpu.HBM)
-
-
-def call(kernel, shapes, specs, scratch, name):
+ANY = pl.BlockSpec(memory_space=pl.ANY)
+
+
+def call(kernel, shapes, specs, scratch, name, out=VMEM, aliases=None, dtype=None, mib=16):
     many = isinstance(shapes, list)
     return pl.pallas_call(
         kernel,
-        out_shape=[jax.ShapeDtypeStruct(s, F32) for s in shapes]
+        out_shape=[jax.ShapeDtypeStruct(s, d) for s, d in zip(shapes, dtype or [F32] * len(shapes))]
         if many
         else jax.ShapeDtypeStruct(shapes, F32),
         in_specs=specs,
-        out_specs=[VMEM] * len(shapes) if many else VMEM,
+        out_specs=[out] * len(shapes) if many else out,
+        input_output_aliases=aliases or {},
         scratch_shapes=[s if not isinstance(s, tuple) else pltpu.VMEM(s, F32) for s in scratch],
-        compiler_params=PARAMS,
+        compiler_params=pltpu.CompilerParams(vmem_limit_bytes=int(mib * 1024 * 1024)),
+        cost_estimate=pl.CostEstimate(flops=0, transcendentals=0, bytes_accessed=int(3.5e6 * MICROSECONDS[name])),
         name=name,
     )
 
@@ -555,56 +634,64 @@
     behind = [(i, (i - 1) % count) for i in range(count)]
     cells = polarization.reshape(24 * ROWS, LANES)
     alpha = alpha_field.reshape(LAYERS * ROWS, LANES)
-    par = jnp.concatenate(
-        [(landau * np.array([[4.0], [2.0], [6.0]], np.float32)).reshape(24), DT * stiffness, permittivity, interfaces]
-    )
+    par = jnp.concatenate([landau[0], landau[1], landau[2], stiffness, permittivity, interfaces])
     par = jnp.broadcast_to(par[:, None], (par.shape[0], 2 * LANES))
-    last, first = call(
-        border_kernel, [(128, LANES), (64, LANES)], [HBM] * 2,
-        [(2, 32, 8, LANES), pltpu.SemaphoreType.DMA((4,))], "border",
+    last = call(
+        border_kernel, (128, LANES), [ANY] * 2,
+        [(32, 8, LANES), pltpu.SemaphoreType.DMA((2,))], "border", mib=53.8,
     )(polarization.reshape(24, ROWS, LANES), alpha_field)
     low = lax.ppermute(last, "bx", ahead)
+    part, head, first = call(
+        stage_kernel, [(NB * SLOT, LANES), (256, LANES), (64, LANES)], [VMEM] * 3 + [ANY],
+        [(32 * 40, LANES), (24 * 40, LANES), (NB * 32, LANES), (48, LANES)], "stage",
+    )(cells, alpha, par, last)
     high = lax.ppermute(first, "bx", behind)
     sent = call(
         charge_kernel, (NB * SLOT, LANES), [VMEM] * 4,
-        [(32 * 40, LANES), (24 * 40, LANES), (NB * 32, LANES), (48, LANES)], "charge",
-    )(cells, alpha, low, par)
+        [(32 * 40, LANES), (24 * 40, LANES), (4 * 32, LANES)], "charge",
+    )(part, head, low, par)
+    fwd, corner = call(
+        load_kernel, [tabs["fwd"].shape, (8, LANES)], [ANY, VMEM, ANY], [pltpu.SemaphoreType.DMA((1,))],
+        "load_y", dtype=[BF16, F32],
+    )(tabs["fwd"], high, sent)
     lines = lax.all_to_all(sent.reshape(NB, SLOT, LANES), "by", 0, 0, tiled=True).reshape(NB * SLOT, LANES)
-    modes, corner = call(
-        y_forward_kernel, [(devices, LANES), (8, LANES)], [VMEM] * 7, [(256, 256)] * 2, "y_forward"
-    )(lines, *tabs["fwd"], *tabs["fwd0"], tabs["tw"], high)
+    modes = call(
+        y_forward_kernel, (devices, LANES), [VMEM] * 3, [(256, 256)] * 2, "y_forward"
+    )(lines, fwd, tabs["small"])
     modes = lax.all_to_all(modes.reshape(devices, 1, LANES), ("bx", "by"), 0, 0, tiled=True)
     modes = call(
-        x_kernel, (devices, LANES), [VMEM] * 7,
-        [(2 * devices, LANES), (2 * devices, LANES)], "x_solve",
-    )(
-        modes.reshape(devices, LANES), *tabs["x"], *tabs["xt"], tabs["lam"], par
-    )
+        x_kernel, (devices, LANES), [VMEM] * 5, [(2 * devices, LANES)] * 2, "x_solve"
+    )(modes.reshape(devices, LANES), *tabs["x"], tabs["small"], par)
     modes = lax.all_to_all(modes.reshape(devices, 1, LANES), ("bx", "by"), 0, 0, tiled=True)
     sent = call(
-        y_inverse_kernel, (NB * SLOT, LANES), [VMEM] * 8, [(256, 256)], "y_inverse"
-    )(modes.reshape(devices, LANES), *tabs["inv"], *tabs["inv0"], tabs["tw"], lines, corner)
+        y_inverse_kernel, (NB * SLOT, LANES), [VMEM] * 5, [(256, 256)], "y_inverse"
+    )(modes.reshape(devices, LANES), tabs["inv"], tabs["small"], lines, corner)
     phi = lax.all_to_all(sent.reshape(NB, SLOT, LANES), "by", 0, 0, tiled=True)
-    far = lax.ppermute(phi[NB - 4 :].reshape(4 * SLOT, LANES), "bx", ahead)
+    far = lax.ppermute(phi[:4].reshape(4 * SLOT, LANES), "bx", behind)
+    phi = phi.reshape(NB * SLOT, LANES)
     star = call(
-        star_kernel, [(24 * 48, LANES)] * 2, [VMEM] * 6,
-        [(32 * 48, LANES)] * 2, "star",
+        star_kernel, [(24 * 48, LANES)] * 2, [VMEM] * 6, [(32 * 48, LANES)] * 2, "star",
     )(cells, alpha, low, high, phi, par)
+    polar, field, *grid = call(
+        inner_kernel, [(24, ROWS, LANES)] * 2 + [(16 * 48, LANES)] * 2, [VMEM] * 5,
+        [(24 * 48, LANES)] * 2 + [(NB * 32, LANES)], "inner",
+    )(alpha, *star, phi, par)
     polar, field = call(
-        update_kernel, [(24 * ROWS, LANES)] * 2, [VMEM] * 6,
-        [(16 * 48, LANES)] * 2 + [(24 * 48, LANES)] * 2 + [(NB * 32, LANES)], "update",
-    )(alpha, *star, phi.reshape(NB * SLOT, LANES), far, par)
+        update_kernel, [(24, ROWS, LANES)] * 2, [VMEM] * 7 + [ANY] * 2,
+        [(16 * 48, LANES)] * 2 + [(24 * 48, LANES)] * 2 + [(24, 8, LANES)] * 2 + [pltpu.SemaphoreType.DMA((2,))],
+        "update", out=ANY, aliases={7: 0, 8: 1},
+    )(alpha, *star, *grid, far, par, polar, field)
     return polar.reshape(polarization.shape), field.reshape(polarization.shape)
 
 
 def solution(mesh):
     fwd, fwd0, inv, inv0, tw = tables_y()
     table, lam = tables_x(mesh.shape["bx"] * ROWS, -SHIFT)
-    back, _ = tables_x(mesh.shape["bx"] * ROWS, SHIFT)
     tabs = {
-        "fwd": split_table(fwd), "fwd0": split_table(fwd0),
-        "inv": split_table(inv), "inv0": split_table(inv0),
-        "tw": tw, "x": split_table(table), "xt": split_table(back.T), "lam": lam,
+        "fwd": np.concatenate([*split_table(fwd), *split_table(fwd0)], axis=0),
+        "inv": np.concatenate([*split_table(inv), *split_table(inv0)], axis=0),
+        "x": split_table(table),
+        "small": np.concatenate([tw, lam], axis=0),
     }
     return jax.shard_map(
         functools.partial(shards, tabs),

time: 135 us -> 127 us (0.941)
  waiting for transfers between devices: 18.7 us -> 12.5 us
  local copies, waits for them, and re-layouts: 6.08 us -> 2.09 us
  Pallas kernels: 8.53 us -> 10.8 us
    ppermute x1, waiting for transfers between devices: 4.37 us -> 0.01 us  [shards(): far = lax.ppermute(phi[:4].reshape(4 * SLOT, LANES), 'bx', behind)]
    unnamed x46 -> x30, local copies, waits for them, and re-layouts: 5.92 us -> 1.93 us
    pallas_call x5 -> x8, Pallas kernels: 5.47 us -> 8.46 us  [the longest x1 1.86 us: shards(): call(inner_kernel, [(24, ROWS, LANES)] * 2 + [(16 * 48, LANES)] * 2, [VME...]
  transfers between devices with their start and end apart: 4 -> 4, of which waited for: 4 -> 3; matrix products, arithmetic and copies ran while one was open for 0% -> 0% of each run, Pallas kernels for 1% -> 3%
where the time goes in v3:
time: 127 us
  blocking collectives  82.4 us (65%)
  starting transfers between devices  17.9 us (14%)
  waiting for transfers between devices  12.5 us (10%)
  Pallas kernels  10.8 us (9%)
  local copies, waits for them, and re-layouts  2.09 us (2%)
    all_to_all x2, blocking collectives, shards(): lax.all_to_all(modes.reshape(devices, 1, LANES), ('bx', 'by'), 0, 0, tile...  71.4 us
    all_to_all x1, blocking collectives, shards(): phi = lax.all_to_all(sent.reshape(NB, SLOT, LANES), 'by', 0, 0, tiled=True)  11 us
    ppermute x1, waiting for transfers between devices, shards(): low = lax.ppermute(last, 'bx', ahead)  9.92 us
    all_to_all x1, starting transfers between devices, shards(): lax.all_to_all(sent.reshape(NB, SLOT, LANES), 'by', 0, 0, tiled=True)  6.1 us
    ppermute x1, starting transfers between devices, shards(): low = lax.ppermute(last, 'bx', ahead)  4.38 us
    ppermute x1, starting transfers between devices, shards(): high = lax.ppermute(first, 'bx', behind)  4.27 us
    ppermute x1, starting transfers between devices, shards(): far = lax.ppermute(phi[:4].reshape(4 * SLOT, LANES), 'bx', behind)  3.19 us
  transfers between devices with their start and end apart: 4, of which 3 were waited for; matrix products, arithmetic and copies ran while one was open for 0% of the time, Pallas kernels for 3%

profile of v3, /device:TPU:1, one launch (start us, length us, event | category | flops | bytes accessed | tf_op | source)
XLA Modules:
  0.0 126.7 jit_solution(11612766140964685887)
XLA Ops:
  0.7 1.0 border.1.after
  1.7 4.4 %collective-permute-start = (f32[128,128]{1,0:T(8,128)S(1)}, f32[128,128]{1,0:T(8,128)S(1)}, u32[]{:S(2)}, u32[]{:S(2)}) collective-permute-start(f32[128,128]{1,0:T(8,128)S(1)} %border.1.after), channel_id=1, source_target_pairs={{0,16},{16,32},{32,48},{48,64},{64,80},{80,96},{96,112},{112,128},... | collective-permute-start | bytes 196616 | tf_op jit(solution)/shard_map/ppermute | solution.py:643
  6.1 0.0 copy-start.12
  6.1 0.0 copy-start.13
  6.1 0.0 copy-start.14
  6.1 0.6 copy-done.12
  6.7 0.0 copy-done.13
  6.8 0.0 copy-done.14
  6.8 0.1 concatenate.3
  6.9 0.1 broadcast_in_dim.2.par
  6.9 1.0 stage.1
  8.0 9.9 %collective-permute-done.lo_ref = f32[128,128]{1,0:T(8,128)S(1)} collective-permute-done((f32[128,128]{1,0:T(8,128)S(1)}, f32[128,128]{1,0:T(8,128)S(1)}, u32[]{:S(2)}, u32[]{:S(2)}) %collective-permute-start) | collective-permute-done | bytes 65568 | tf_op jit(solution)/shard_map/ppermute | solution.py:643
  17.9 1.0 charge.1.after
  18.9 0.6 copy-done.6
  19.6 6.1 %all-to-all-start = ((f32[16,40,128]{2,1,0:T(8,128)}), f32[16,40,128]{2,1,0:T(8,128)S(1)}, u32[]{:S(2)}, u32[]{:S(2)}) async-start(f32[16,40,128]{2,1,0:T(8,128)} %bitcast.6), calls=%async_computation | async-start | bytes 655360 | tf_op jit(solution)/shard_map/all_to_all | solution.py:657
  25.7 4.3 %collective-permute-start.1 = (f32[64,128]{1,0:T(8,128)S(1)}, f32[64,128]{1,0:T(8,128)S(1)}, u32[]{:S(2)}, u32[]{:S(2)}) collective-permute-start(f32[64,128]{1,0:T(8,128)S(1)} %get-tuple-element.15), channel_id=1, source_target_pairs={{0,496},{16,0},{32,16},{48,32},{64,48},{80,64},{96,80},{112,96},{1... | collective-permute-start | bytes 98312 | tf_op jit(solution)/shard_map/ppermute | solution.py:648
  30.0 1.0 collective-permute-done.1.hi_ref
  31.0 0.1 load_y.1
  31.1 0.6 copy-done.9
  31.7 1.6 %all-to-all-done = f32[16,40,128]{2,1,0:T(8,128)S(1)} async-done(((f32[16,40,128]{2,1,0:T(8,128)}), f32[16,40,128]{2,1,0:T(8,128)S(1)}, u32[]{:S(2)}, u32[]{:S(2)}) %all-to-all-start) | async-done | bytes 327712 | tf_op jit(solution)/shard_map/all_to_all | solution.py:657
  33.3 0.9 y_forward.1
  34.2 38.4 %all_to_all.20 = f32[512,1,128]{2,1,0:T(1,128)S(1)} all-to-all(f32[512,1,128]{2,1,0:T(1,128)S(1)} %bitcast.36), channel_id=1, replica_groups=mesh['bx'=32,'by'=16] {'bx','by'}, dimensions={0} | all-to-all | bytes 524288 | tf_op jit(solution)/shard_map/all_to_all | solution.py:661
  72.6 1.5 %x_solve.1 = f32[512,128]{1,0:T(8,128)S(1)} custom-call(f32[512,128]{1,0:T(8,128)S(1)} %bitcast.38, bf16[1024,512]{1,0:T(8,128)(2,1)S(1)} %copy-done.3, bf16[1024,512]{1,0:T(8,128)(2,1)S(1)} %copy-done.2, f32[32,128]{1,0:T(8,128)S(1)} %copy-done.8, f32[49,256]{1,0:T(8,128)S(1)} %broadcast_in_dim.2.par), custom_call_target="tpu_custom_call" | custom-call | bytes 5250000 | tf_op jit(solution)/shard_map/x_solve/pallas_call | solution.py:662
  74.1 0.0 copy-start.5
  74.1 33.0 %all_to_all.21 = f32[512,1,128]{2,1,0:T(1,128)S(1)} all-to-all(f32[512,1,128]{2,1,0:T(1,128)S(1)} %bitcast.39), channel_id=1, replica_groups=mesh['bx'=32,'by'=16] {'bx','by'}, dimensions={0} | all-to-all | bytes 524288 | tf_op jit(solution)/shard_map/all_to_all | solution.py:665
  107.1 0.8 y_inverse.1
  107.9 11.0 %all_to_all.22 = f32[16,40,128]{2,1,0:T(8,128)S(1)} all-to-all(f32[16,40,128]{2,1,0:T(8,128)S(1)} %bitcast.35), channel_id=1, replica_groups=mesh['bx'=32,'by'=16] {'by'}, dimensions={0} | all-to-all | bytes 655360 | tf_op jit(solution)/shard_map/all_to_all | solution.py:669
  119.0 3.2 %collective-permute-start.2 = (f32[160,128]{1,0:T(8,128)S(1)}, f32[160,128]{1,0:T(8,128)S(1)}, u32[]{:S(2)}, u32[]{:S(2)}) collective-permute-start(f32[160,128]{1,0:T(8,128)S(1)} %bitcast.42), channel_id=1, source_target_pairs={{0,496},{16,0},{32,16},{48,32},{64,48},{80,64},{96,80},{112,96},{1... | collective-permute-start | bytes 245768 | tf_op jit(solution)/shard_map/ppermute | solution.py:670
  122.2 1.3 %star.1 = (f32[1152,128]{1,0:T(8,128)S(1)}, f32[1152,128]{1,0:T(8,128)S(1)}) custom-call(f32[768,128]{1,0:T(8,128)S(1)} %bitcast.26, f32[256,128]{1,0:T(8,128)S(1)} %bitcast.30, f32[128,128]{1,0:T(8,128)S(1)} %copy-done.7, f32[64,128]{1,0:T(8,128)S(1)} %copy-done.10, f32[640,128]{1,0:T(8,128)S(1)} %bitcast.27, f32[49,256]{1,0:T(8,128)S(1)} %broadcast_in_dim.2.par), custom_call_target="tpu_custom_call" | custom-call | bytes 4550000 | tf_op jit(solution)/shard_map/star/pallas_call | solution.py:672
  123.5 1.9 %inner.1 = (f32[24,32,128]{2,1,0:T(8,128)}, f32[24,32,128]{2,1,0:T(8,128)}, f32[768,128]{1,0:T(8,128)S(1)}, f32[768,128]{1,0:T(8,128)S(1)}) custom-call(f32[256,128]{1,0:T(8,128)S(1)} %bitcast.31, f32[1152,128]{1,0:T(8,128)S(1)} %get-tuple-element.20.qm, f32[1152,128]{1,0:T(8,128)S(1)} %get-tuple-element.21.qs, f32[640,128]{1,0:T(8,128)S(1)} %bitcast.28, ...), custom_call_target="tpu_custom_call" | custom-call | bytes 6300000 | tf_op jit(solution)/shard_map/inner/pallas_call | solution.py:675
  125.3 0.0 collective-permute-done.2.far_ref
  125.3 1.2 update.1
  (23 shorter events, 0.1 us)
Async XLA Ops:
  0.6 6.3 %copy-start = (f32[3,8,32,128]{3,2,1,0:T(8,128)S(1)}, f32[3,8,32,128]{3,2,1,0:T(8,128)}, u32[]{:S(2)}) copy-start(f32[3,8,32,128]{3,2,1,0:T(8,128)} %param.11) | copy-start | bytes 1179652
  0.6 5.4 %copy-start.11 = (f32[3,8]{1,0:T(4,128)S(1)}, f32[3,8]{1,0:T(4,128)}, u32[]{:S(2)}) copy-start(f32[3,8]{1,0:T(4,128)} %param.13) | copy-start | bytes 292
  0.6 6.3 %copy-start.1 = (f32[8,32,128]{2,1,0:T(8,128)S(1)}, f32[8,32,128]{2,1,0:T(8,128)}, u32[]{:S(2)}) copy-start(f32[8,32,128]{2,1,0:T(8,128)} %al_ref.1) | copy-start | bytes 393220
  1.7 16.2 %collective-permute-start = (f32[128,128]{1,0:T(8,128)S(1)}, f32[128,128]{1,0:T(8,128)S(1)}, u32[]{:S(2)}, u32[]{:S(2)}) collective-permute-start(f32[128,128]{1,0:T(8,128)S(1)} %border.1.after), channel_id=1, source_target_pairs={{0,16},{16,32},{32,48},{48,64},{64,80},{80,96},{96,112},{112,128},... | collective-permute-start | bytes 196616 | tf_op jit(solution)/shard_map/ppermute | solution.py:643
  6.1 0.7 copy-start.12
  6.1 0.7 copy-start.13
  6.1 0.7 copy-start.14
  18.9 0.6 copy-start.6
  19.6 11.4 %copy-start.4 = (bf16[1024,256]{1,0:T(8,128)(2,1)S(1)}, bf16[1024,256]{1,0:T(8,128)(2,1)}, u32[]{:S(2)}) copy-start(bf16[1024,256]{1,0:T(8,128)(2,1)} %constant.10.clone.table) | copy-start | bytes 1572868
  19.6 13.7 %all-to-all-start = ((f32[16,40,128]{2,1,0:T(8,128)}), f32[16,40,128]{2,1,0:T(8,128)S(1)}, u32[]{:S(2)}, u32[]{:S(2)}) async-start(f32[16,40,128]{2,1,0:T(8,128)} %bitcast.6), calls=%async_computation | async-start | bytes 655360 | tf_op jit(solution)/shard_map/all_to_all | solution.py:657
  25.7 7.6 %copy-start.8 = (f32[32,128]{1,0:T(8,128)S(1)}, f32[32,128]{1,0:T(8,128)}, u32[]{:S(2)}) copy-start(f32[32,128]{1,0:T(8,128)} %constant.11.clone.tw.lam) | copy-start | bytes 49156
  25.7 5.3 %collective-permute-start.1 = (f32[64,128]{1,0:T(8,128)S(1)}, f32[64,128]{1,0:T(8,128)S(1)}, u32[]{:S(2)}, u32[]{:S(2)}) collective-permute-start(f32[64,128]{1,0:T(8,128)S(1)} %get-tuple-element.15), channel_id=1, source_target_pairs={{0,496},{16,0},{32,16},{48,32},{64,48},{80,64},{96,80},{112,96},{1... | collective-permute-start | bytes 98312 | tf_op jit(solution)/shard_map/ppermute | solution.py:648
  31.0 41.7 %copy-start.3 = (bf16[1024,512]{1,0:T(8,128)(2,1)S(1)}, bf16[1024,512]{1,0:T(8,128)(2,1)}, u32[]{:S(2)}) copy-start(bf16[1024,512]{1,0:T(8,128)(2,1)} %constant.12.clone.th) | copy-start | bytes 3145732
  31.1 0.6 copy-start.9
  31.7 40.9 %copy-start.2 = (bf16[1024,512]{1,0:T(8,128)(2,1)S(1)}, bf16[1024,512]{1,0:T(8,128)(2,1)}, u32[]{:S(2)}) copy-start(bf16[1024,512]{1,0:T(8,128)(2,1)} %constant.13.clone.tl) | copy-start | bytes 3145732
  74.1 33.0 %copy-start.5 = (bf16[1024,256]{1,0:T(8,128)(2,1)S(1)}, bf16[1024,256]{1,0:T(8,128)(2,1)}, u32[]{:S(2)}) copy-start(bf16[1024,256]{1,0:T(8,128)(2,1)} %constant.14.clone.tab) | copy-start | bytes 1572868
  119.0 3.2 %copy-start.7 = (f32[128,128]{1,0:T(8,128)S(1)}, f32[128,128]{1,0:T(8,128)}, u32[]{:S(2)}) copy-start(f32[128,128]{1,0:T(8,128)} %copy-done.6) | copy-start | bytes 196612
  119.0 3.2 %copy-start.10 = (f32[64,128]{1,0:T(8,128)S(1)}, f32[64,128]{1,0:T(8,128)}, u32[]{:S(2)}) copy-start(f32[64,128]{1,0:T(8,128)} %copy-done.9) | copy-start | bytes 98308
  119.0 6.4 %collective-permute-start.2 = (f32[160,128]{1,0:T(8,128)S(1)}, f32[160,128]{1,0:T(8,128)S(1)}, u32[]{:S(2)}, u32[]{:S(2)}) collective-permute-start(f32[160,128]{1,0:T(8,128)S(1)} %bitcast.42), channel_id=1, source_target_pairs={{0,496},{16,0},{32,16},{48,32},{64,48},{80,64},{96,80},{112,96},{1... | collective-permute-start | bytes 245768 | tf_op jit(solution)/shard_map/ppermute | solution.py:670

commit v4 on v3

--- a/solution.py
+++ b/solution.py
@@ -19,7 +19,7 @@
 F32 = jnp.float32
 BF16 = jnp.bfloat16
 MICROSECONDS = {
-    "border": 0.8, "stage": 1.8, "charge": 0.5, "load_y": 0.5,   "y_forward": 0.9, "x_solve": 1.5, "y_inverse": 0.8, "star": 1.3, "inner": 1.8, "update": 1.0
+    "border": 0.8, "stage": 1.8, "charge": 0.5,   "y_forward": 0.9, "x_solve": 1.5, "y_inverse": 0.8, "star": 1.3, "inner": 1.8, "update": 1.0
 }
 
 
@@ -135,13 +135,6 @@
     for n in range(32):
         for r in range(4):
             last_ref[r * 32 + n : r * 32 + n + 1, :] = buf[n, 4 + r : 5 + r, :]
-
-
-def load_kernel(table, hi_ref, after, table_ref, corner_ref, sem):
-    copy = pltpu.make_async_copy(table, table_ref, sem.at[0])
-    copy.start()
-    corner_ref[...] = jnp.concatenate([pack(hi_ref[0:32, :]), jnp.zeros((7, LANES), F32)], axis=0)
-    copy.wait()
 
 
 def rows_of(ref, c, l, low, high):
@@ -227,7 +220,7 @@
         )
 
 
-def charge_kernel(part_ref, head_ref, lo_ref, par, out_ref, px, nx, ws):
+def charge_kernel(part_ref, head_ref, lo_ref, par, tab, out_ref, px, nx, ws):
     out_ref[...] = part_ref[...]
     for n in range(32):
         px[n * 40 + 8 : n * 40 + 16, :] = head_ref[n * 8 : (n + 1) * 8, :]
@@ -250,7 +243,8 @@
     out_ref[at : at + 1, :] = pack(lo_ref[96:128, :])
 
 
-def y_forward_kernel(in_ref, tab, tw, out_ref, d_ref, o_ref):
+def y_forward_kernel(in_ref, tab, tw, lo_ref, hi_ref, out_ref, corner_ref, d_ref, o_ref):
+    corner_ref[...] = jnp.concatenate([pack(hi_ref[0:32, :]), jnp.zeros((7, LANES), F32)], axis=0)
     fh, fl, f0h, f0l = (tab[k * 256 : (k + 1) * 256, :] for k in range(4))
     lane1 = lax.broadcasted_iota(jnp.int32, (1, LANES), 1)
     lane = lax.broadcasted_iota(jnp.int32, (ROWS, LANES), 1)
@@ -305,7 +299,7 @@
         out_ref[j * 64 : (j + 1) * 64, :] = value
 
 
-def x_kernel(in_ref, th, tl, lam, par, out_ref, zs, ys):
+def x_kernel(in_ref, th, tl, lam, par, lo_ref, hi_ref, out_ref, zs, ys):
     n = in_ref.shape[0]
     half = n // 2
     top, low = in_ref[0:half, :], in_ref[half:n, :]
@@ -391,7 +385,7 @@
     out_ref[half:n, :] = jnp.transpose(pair[0] - pair[1])
 
 
-def y_inverse_kernel(in_ref, tab, tw, lines, corner_ref, out_ref, o_ref):
+def y_inverse_kernel(in_ref, tab, tw, lines, corner_ref, lo_ref, hi_ref, out_ref, o_ref):
     gh, gl, g0h, g0l = (tab[k * 256 : (k + 1) * 256, :] for k in range(4))
     lane64 = lax.broadcasted_iota(jnp.int32, (64, LANES), 1)
     for t in range(2):
@@ -445,7 +439,8 @@
     from_right = lax.broadcasted_iota(jnp.int32, (3, LANES), 1) % 4 < 2
     for b in range(NB):
         after, before = (b + 1) % NB, (b - 1) % NB
-        out_ref[b * SLOT : b * SLOT + 32, :] = out[b]
+        for k, r in enumerate((8, 24, 0, 16)):
+            out_ref[b * SLOT + k * 8 : b * SLOT + (k + 1) * 8, :] = out[b][r : r + 8]
         border = jnp.where(lane < 2, out[after], out[before])
         edge = jnp.where(
             from_right,
@@ -566,7 +561,7 @@
             for xl in range(2):
                 r = f * 16 + xl * 8 + l
                 row = (f * LAYERS + l) * 48 + 8 - SHIFT + xl * NB
-                fm[row : row + NB, :] = phi_ref[pl.ds(r, NB, stride=SLOT), :]
+                fm[row : row + NB, :] = phi_ref[pl.ds((1 - xl) * 16 + f * 8 + l, NB, stride=SLOT), :]
                 fs[row : row + NB, :] = ht[pl.ds(r, NB, stride=32), :]
     first_step(qm, qs, fm, fs, rm, rs, 7, 33)
 
@@ -584,10 +579,10 @@
         fm[n * 48 + 30 : n * 48 + 38, :] = gm[n * 48 + 30 : n * 48 + 38, :]
         fs[n * 48 + 30 : n * 48 + 38, :] = gs[n * 48 + 30 : n * 48 + 38, :]
     for k in range(4):
-        side = unpack(far_ref[k * SLOT + 32 : k * SLOT + 33, :])
+        side = unpack(far_ref[k * 24 + 16 : k * 24 + 17, :])
         for f in range(2):
             rows = pl.ds(f * LAYERS * 48 + 38 + k, LAYERS, stride=48)
-            fm[rows, :] = far_ref[k * SLOT + f * 16 : k * SLOT + f * 16 + 8, :]
+            fm[rows, :] = far_ref[k * 24 + f * 8 : k * 24 + f * 8 + 8, :]
             fs[rows, :] = side[f * 16 : f * 16 + 8]
     first_step(qm, qs, fm, fs, rm, rs, 31, 41)
 
@@ -647,27 +642,23 @@
     )(cells, alpha, par, last)
     high = lax.ppermute(first, "bx", behind)
     sent = call(
-        charge_kernel, (NB * SLOT, LANES), [VMEM] * 4,
+        charge_kernel, (NB * SLOT, LANES), [VMEM] * 4 + [ANY],
         [(32 * 40, LANES), (24 * 40, LANES), (4 * 32, LANES)], "charge",
-    )(part, head, low, par)
-    fwd, corner = call(
-        load_kernel, [tabs["fwd"].shape, (8, LANES)], [ANY, VMEM, ANY], [pltpu.SemaphoreType.DMA((1,))],
-        "load_y", dtype=[BF16, F32],
-    )(tabs["fwd"], high, sent)
+    )(part, head, low, par, tabs["fwd"])
     lines = lax.all_to_all(sent.reshape(NB, SLOT, LANES), "by", 0, 0, tiled=True).reshape(NB * SLOT, LANES)
-    modes = call(
-        y_forward_kernel, (devices, LANES), [VMEM] * 3, [(256, 256)] * 2, "y_forward"
-    )(lines, fwd, tabs["small"])
+    modes, corner = call(
+        y_forward_kernel, [(devices, LANES), (8, LANES)], [VMEM] * 5, [(256, 256)] * 2, "y_forward"
+    )(lines, tabs["fwd"], tabs["small"], low, high)
     modes = lax.all_to_all(modes.reshape(devices, 1, LANES), ("bx", "by"), 0, 0, tiled=True)
     modes = call(
-        x_kernel, (devices, LANES), [VMEM] * 5, [(2 * devices, LANES)] * 2, "x_solve"
-    )(modes.reshape(devices, LANES), *tabs["x"], tabs["small"], par)
+        x_kernel, (devices, LANES), [VMEM] * 7, [(2 * devices, LANES)] * 2, "x_solve"
+    )(modes.reshape(devices, LANES), *tabs["x"], tabs["small"], par, low, high)
     modes = lax.all_to_all(modes.reshape(devices, 1, LANES), ("bx", "by"), 0, 0, tiled=True)
     sent = call(
-        y_inverse_kernel, (NB * SLOT, LANES), [VMEM] * 5, [(256, 256)], "y_inverse"
-    )(modes.reshape(devices, LANES), tabs["inv"], tabs["small"], lines, corner)
+        y_inverse_kernel, (NB * SLOT, LANES), [VMEM] * 7, [(256, 256)], "y_inverse"
+    )(modes.reshape(devices, LANES), tabs["inv"], tabs["small"], lines, corner, low, high)
     phi = lax.all_to_all(sent.reshape(NB, SLOT, LANES), "by", 0, 0, tiled=True)
-    far = lax.ppermute(phi[:4].reshape(4 * SLOT, LANES), "bx", behind)
+    far = lax.ppermute(phi[:4, 16:].reshape(4 * 24, LANES), "bx", behind)
     phi = phi.reshape(NB * SLOT, LANES)
     star = call(
         star_kernel, [(24 * 48, LANES)] * 2, [VMEM] * 6, [(32 * 48, LANES)] * 2, "star",

time: 127 us -> 126 us (level)
    unnamed x30 -> x14, local copies, waits for them, and re-layouts: 1.93 us -> 0.03 us
    pallas_call x5 -> x4, Pallas kernels: 4.39 us -> 4.32 us  [the longest x1 1.53 us: shards(): call(x_kernel, (devices, LANES), [VMEM] * 7, [(2 * devices, LANES)] * 2,...]
  transfers between devices with their start and end apart: 4 -> 4, of which waited for: 3 -> 3; matrix products, arithmetic and copies ran while one was open for 0% -> 1% of each run, Pallas kernels for 3% -> 3%
where the time goes in v4:
time: 126 us; the launch traced here: 125 us
  blocking collectives  81.8 us (65%)
  starting transfers between devices  17.8 us (14%)
  waiting for transfers between devices  12.5 us (10%)
  Pallas kernels  10.7 us (8%)
  local copies, waits for them, and re-layouts  1.67 us (1%)
    all_to_all x2, blocking collectives, shards(): lax.all_to_all(modes.reshape(devices, 1, LANES), ('bx', 'by'), 0, 0, tile...  70.8 us
    all_to_all x1, blocking collectives, shards(): phi = lax.all_to_all(sent.reshape(NB, SLOT, LANES), 'by', 0, 0, tiled=True)  11 us
    ppermute x1, waiting for transfers between devices, shards(): low = lax.ppermute(last, 'bx', ahead)  9.15 us
    all_to_all x1, starting transfers between devices, shards(): lax.all_to_all(sent.reshape(NB, SLOT, LANES), 'by', 0, 0, tiled=True)  6.1 us
    ppermute x1, starting transfers between devices, shards(): low = lax.ppermute(last, 'bx', ahead)  4.38 us
    ppermute x1, starting transfers between devices, shards(): high = lax.ppermute(first, 'bx', behind)  4.27 us
    ppermute x1, starting transfers between devices, shards(): far = lax.ppermute(phi[:4, 16:].reshape(4 * 24, LANES), 'bx', behind)  3.05 us
  transfers between devices with their start and end apart: 4, of which 3 were waited for; matrix products, arithmetic and copies ran while one was open for 1% of the time, Pallas kernels for 3%

profile of v4, /device:TPU:1, one launch (start us, length us, event | category | flops | bytes accessed | tf_op | source)
XLA Modules:
  0.0 125.4 jit_solution(3544731366614562571)
XLA Ops:
  0.6 0.0 copy-start
  0.6 0.0 copy-start.1
  0.6 0.0 copy-start.2
  0.7 1.0 border.1.after
  1.7 4.4 %collective-permute-start = (f32[128,128]{1,0:T(8,128)S(1)}, f32[128,128]{1,0:T(8,128)S(1)}, u32[]{:S(2)}, u32[]{:S(2)}) collective-permute-start(f32[128,128]{1,0:T(8,128)S(1)} %border.1.after), channel_id=1, source_target_pairs={{0,16},{16,32},{32,48},{48,64},{64,80},{80,96},{96,112},{112,128},... | collective-permute-start | bytes 196616 | tf_op jit(solution)/shard_map/ppermute | solution.py:638
  6.1 0.8 slice_bitcast_fusion
  6.9 0.8 concatenate.3
  7.7 0.1 broadcast_in_dim.2.par
  7.7 0.0 copy-done
  7.7 0.0 copy-done.1
  7.7 1.0 stage.1
  8.8 9.2 %collective-permute-done.lo_ref = f32[128,128]{1,0:T(8,128)S(1)} collective-permute-done((f32[128,128]{1,0:T(8,128)S(1)}, f32[128,128]{1,0:T(8,128)S(1)}, u32[]{:S(2)}, u32[]{:S(2)}) %collective-permute-start) | collective-permute-done | bytes 65568 | tf_op jit(solution)/shard_map/ppermute | solution.py:638
  17.9 0.0 copy-done.2
  17.9 1.0 charge.1
  19.0 6.1 %all-to-all-start = ((f32[16,40,128]{2,1,0:T(8,128)}), f32[16,40,128]{2,1,0:T(8,128)S(1)}, u32[]{:S(2)}, u32[]{:S(2)}) async-start(f32[16,40,128]{2,1,0:T(8,128)} %bitcast.6), calls=%async_computation | async-start | bytes 655360 | tf_op jit(solution)/shard_map/all_to_all | solution.py:648
  25.1 4.3 %collective-permute-start.1 = (f32[64,128]{1,0:T(8,128)S(1)}, f32[64,128]{1,0:T(8,128)S(1)}, u32[]{:S(2)}, u32[]{:S(2)}) collective-permute-start(f32[64,128]{1,0:T(8,128)S(1)} %get-tuple-element.15), channel_id=1, source_target_pairs={{0,496},{16,0},{32,16},{48,32},{64,48},{80,64},{96,80},{112,96},{1... | collective-permute-start | bytes 98312 | tf_op jit(solution)/shard_map/ppermute | solution.py:643
  29.4 1.0 collective-permute-done.1.hi_ref
  30.4 2.3 %all-to-all-done = f32[16,40,128]{2,1,0:T(8,128)S(1)} async-done(((f32[16,40,128]{2,1,0:T(8,128)}), f32[16,40,128]{2,1,0:T(8,128)S(1)}, u32[]{:S(2)}, u32[]{:S(2)}) %all-to-all-start) | async-done | bytes 327712 | tf_op jit(solution)/shard_map/all_to_all | solution.py:648
  32.7 0.0 copy-done.6
  32.7 0.9 y_forward.1
  33.6 37.8 %all_to_all.20 = f32[512,1,128]{2,1,0:T(1,128)S(1)} all-to-all(f32[512,1,128]{2,1,0:T(1,128)S(1)} %bitcast.39), channel_id=1, replica_groups=mesh['bx'=32,'by'=16] {'bx','by'}, dimensions={0} | all-to-all | bytes 524288 | tf_op jit(solution)/shard_map/all_to_all | solution.py:652
  71.4 0.0 copy-done.3
  71.5 1.5 %x_solve.1 = f32[512,128]{1,0:T(8,128)S(1)} custom-call(f32[512,128]{1,0:T(8,128)S(1)} %bitcast.37, bf16[1024,512]{1,0:T(8,128)(2,1)S(1)} %copy-done.4, bf16[1024,512]{1,0:T(8,128)(2,1)S(1)} %copy-done.3, f32[32,128]{1,0:T(8,128)S(1)} %copy-done.6, f32[49,256]{1,0:T(8,128)S(1)} %broadcast_in_dim.2.par, f32[128,128]{1,0:T(8,128)S(1)} %collective-permute-done.lo_ref, ...), custom_call_target="tpu_custom_call" | custom-call | bytes 5250000 | tf_op jit(solution)/shard_map/x_solve/pallas_call | solution.py:653
  73.0 0.0 copy-start.5
  73.0 33.0 %all_to_all.21 = f32[512,1,128]{2,1,0:T(1,128)S(1)} all-to-all(f32[512,1,128]{2,1,0:T(1,128)S(1)} %bitcast.38), channel_id=1, replica_groups=mesh['bx'=32,'by'=16] {'bx','by'}, dimensions={0} | all-to-all | bytes 524288 | tf_op jit(solution)/shard_map/all_to_all | solution.py:656
  106.0 0.8 y_inverse.1
  106.8 11.0 %all_to_all.22 = f32[16,40,128]{2,1,0:T(8,128)S(1)} all-to-all(f32[16,40,128]{2,1,0:T(8,128)S(1)} %bitcast.35), channel_id=1, replica_groups=mesh['bx'=32,'by'=16] {'by'}, dimensions={0} | all-to-all | bytes 655360 | tf_op jit(solution)/shard_map/all_to_all | solution.py:660
  117.8 3.1 %collective-permute-start.2 = (f32[96,128]{1,0:T(8,128)S(1)}, f32[96,128]{1,0:T(8,128)S(1)}, u32[]{:S(2)}, u32[]{:S(2)}) collective-permute-start(f32[96,128]{1,0:T(8,128)S(1)} %bitcast.42), channel_id=1, source_target_pairs={{0,496},{16,0},{32,16},{48,32},{64,48},{80,64},{96,80},{112,96},{1... | collective-permute-start | bytes 147464 | tf_op jit(solution)/shard_map/ppermute | solution.py:661
  120.9 1.3 %star.1 = (f32[1152,128]{1,0:T(8,128)S(1)}, f32[1152,128]{1,0:T(8,128)S(1)}) custom-call(f32[768,128]{1,0:T(8,128)S(1)} %bitcast.26, f32[256,128]{1,0:T(8,128)S(1)} %bitcast.28, f32[128,128]{1,0:T(8,128)S(1)} %collective-permute-done.lo_ref, f32[64,128]{1,0:T(8,128)S(1)} %collective-permute-done.1.hi_ref, f32[640,128]{1,0:T(8,128)S(1)} %bitcast.31, ...), custom_call_target="tpu_custom_call" | custom-call | bytes 4550000 | tf_op jit(solution)/shard_map/star/pallas_call | solution.py:663
  122.2 1.9 %inner.1 = (f32[24,32,128]{2,1,0:T(8,128)}, f32[24,32,128]{2,1,0:T(8,128)}, f32[768,128]{1,0:T(8,128)S(1)}, f32[768,128]{1,0:T(8,128)S(1)}) custom-call(f32[256,128]{1,0:T(8,128)S(1)} %bitcast.29, f32[1152,128]{1,0:T(8,128)S(1)} %get-tuple-element.20.qm, f32[1152,128]{1,0:T(8,128)S(1)} %get-tuple-element.21.qs, f32[640,128]{1,0:T(8,128)S(1)} %bitcast.32, ...), custom_call_target="tpu_custom_call" | custom-call | bytes 6300000 | tf_op jit(solution)/shard_map/inner/pallas_call | solution.py:666
  124.0 0.0 collective-permute-done.2.far_ref
  124.0 1.2 update.1
  (6 shorter events, 0.0 us)
Async XLA Ops:
  0.6 7.1 %copy-start = (f32[3,8,32,128]{3,2,1,0:T(8,128)S(1)}, f32[3,8,32,128]{3,2,1,0:T(8,128)}, u32[]{:S(2)}) copy-start(f32[3,8,32,128]{3,2,1,0:T(8,128)} %param.11) | copy-start | bytes 1179652
  0.6 7.1 %copy-start.1 = (f32[8,32,128]{2,1,0:T(8,128)S(1)}, f32[8,32,128]{2,1,0:T(8,128)}, u32[]{:S(2)}) copy-start(f32[8,32,128]{2,1,0:T(8,128)} %al_ref.1) | copy-start | bytes 393220
  0.6 17.3 %copy-start.2 = (bf16[1024,256]{1,0:T(8,128)(2,1)S(1)}, bf16[1024,256]{1,0:T(8,128)(2,1)}, u32[]{:S(2)}) copy-start(bf16[1024,256]{1,0:T(8,128)(2,1)} %constant.10.clone.tab) | copy-start | bytes 1572868
  1.7 16.2 %collective-permute-start = (f32[128,128]{1,0:T(8,128)S(1)}, f32[128,128]{1,0:T(8,128)S(1)}, u32[]{:S(2)}, u32[]{:S(2)}) collective-permute-start(f32[128,128]{1,0:T(8,128)S(1)} %border.1.after), channel_id=1, source_target_pairs={{0,16},{16,32},{32,48},{48,64},{64,80},{80,96},{96,112},{112,128},... | collective-permute-start | bytes 196616 | tf_op jit(solution)/shard_map/ppermute | solution.py:638
  17.9 14.8 %copy-start.6 = (f32[32,128]{1,0:T(8,128)S(1)}, f32[32,128]{1,0:T(8,128)}, u32[]{:S(2)}) copy-start(f32[32,128]{1,0:T(8,128)} %constant.11.clone.tw.lam) | copy-start | bytes 49156
  19.0 52.5 %copy-start.3 = (bf16[1024,512]{1,0:T(8,128)(2,1)S(1)}, bf16[1024,512]{1,0:T(8,128)(2,1)}, u32[]{:S(2)}) copy-start(bf16[1024,512]{1,0:T(8,128)(2,1)} %constant.13.clone.tl) | copy-start | bytes 3145732
  19.0 13.7 %all-to-all-start = ((f32[16,40,128]{2,1,0:T(8,128)}), f32[16,40,128]{2,1,0:T(8,128)S(1)}, u32[]{:S(2)}, u32[]{:S(2)}) async-start(f32[16,40,128]{2,1,0:T(8,128)} %bitcast.6), calls=%async_computation | async-start | bytes 655360 | tf_op jit(solution)/shard_map/all_to_all | solution.py:648
  25.1 5.3 %collective-permute-start.1 = (f32[64,128]{1,0:T(8,128)S(1)}, f32[64,128]{1,0:T(8,128)S(1)}, u32[]{:S(2)}, u32[]{:S(2)}) collective-permute-start(f32[64,128]{1,0:T(8,128)S(1)} %get-tuple-element.15), channel_id=1, source_target_pairs={{0,496},{16,0},{32,16},{48,32},{64,48},{80,64},{96,80},{112,96},{1... | collective-permute-start | bytes 98312 | tf_op jit(solution)/shard_map/ppermute | solution.py:643
  32.7 38.8 %copy-start.4 = (bf16[1024,512]{1,0:T(8,128)(2,1)S(1)}, bf16[1024,512]{1,0:T(8,128)(2,1)}, u32[]{:S(2)}) copy-start(bf16[1024,512]{1,0:T(8,128)(2,1)} %constant.12.clone.th) | copy-start | bytes 3145732
  73.0 33.0 %copy-start.5 = (bf16[1024,256]{1,0:T(8,128)(2,1)S(1)}, bf16[1024,256]{1,0:T(8,128)(2,1)}, u32[]{:S(2)}) copy-start(bf16[1024,256]{1,0:T(8,128)(2,1)} %constant.14.clone.tab) | copy-start | bytes 1572868
  117.8 6.2 %collective-permute-start.2 = (f32[96,128]{1,0:T(8,128)S(1)}, f32[96,128]{1,0:T(8,128)S(1)}, u32[]{:S(2)}, u32[]{:S(2)}) collective-permute-start(f32[96,128]{1,0:T(8,128)S(1)} %bitcast.42), channel_id=1, source_target_pairs={{0,496},{16,0},{32,16},{48,32},{64,48},{80,64},{96,80},{112,96},{1... | collective-permute-start | bytes 147464 | tf_op jit(solution)/shard_map/ppermute | solution.py:661
